TPU v7x, 32 devices: a whole 2x2x4 slice. The times are simulated.
32 devices in a mesh: node: 4 (over y, x), local: 2 (over core), edata: 4 (over z).
Axes of the slice: x: 2, y: 2, z: 4, core: 2. Of those that a mesh axis runs over, the one named last changes fastest.
Arguments:
- tokens: bfloat16 [2048, 4096], P(('node', 'local'), 'edata'), may hold values from -6 to 6
- grad_out: bfloat16 [2048, 4096], P(('node', 'local'), 'edata'), may hold values from -0.59765625 to 0.59765625
- routes: int32 [2048, 2], P(('node', 'local')), may hold values from 0 to 63, all different within a row
- gates: bfloat16 [2048, 2], P(('node', 'local')), may hold values from 0.099609375 to 1
- w_in: bfloat16 [4096, 2048], P('edata', ('node', 'local')), may hold values from -0.09375 to 0.09375
- w_out: bfloat16 [2048, 4096], P(('node', 'local'), 'edata'), may hold values from -0.09375 to 0.09375
Outputs:
- grad_tokens: bfloat16 [2048, 4096], P(('node', 'local'), 'edata')
- grad_gates: float32 [2048, 2], P(('node', 'local'))
- grad_w_in: float32 [4096, 2048], P('edata', ('node', 'local'))
- grad_w_out: float32 [2048, 4096], P(('node', 'local'), 'edata')
Inputs may be any that keep to these rules, and one draw needn't show every extreme that they name: `routes`: each token names two different experts.
All inputs are finite; a program needn't handle non-finite values.
Results may differ from a plain program's by a relative error of at most 0.0049.
Values may be sent and summed in bfloat16 or wider, within the bound.
No kernel may reach another device: no remote copies, remote signals or barrier semaphores. Data moves between devices by JAX's collectives and lax.ppermute only.
A program may use at most 64 MiB of HBM per device.

v0:
```python
import functools

import jax
import jax.numpy as jnp
from jax import lax
from jax.experimental import pallas as pl
from jax.experimental.pallas import tpu as pltpu
from jax.sharding import PartitionSpec as P

EXPERTS = 64
WINDOW = 2
LANES = 128
PIECES = 4
VMEM_LIMIT = 40 * 1024 * 1024

BF16 = jnp.bfloat16
F32 = jnp.float32
I16 = jnp.int16
ROWS_BY_ROWS = (((0,), (0,)), ((), ()))
COLS_BY_COLS = (((1,), (1,)), ((), ()))


def gelu_pair(pre_act):
    coefficient = 0.7978845608028654
    square = pre_act * pre_act
    tanh_val = jnp.tanh(coefficient * (pre_act + 0.044715 * pre_act * square))
    half = 0.5 * (1.0 + tanh_val)
    activation = pre_act * half
    slopes = half + 0.5 * pre_act * (1.0 - tanh_val * tanh_val) * coefficient * (
        1.0 + 3.0 * 0.044715 * square
    )
    return (activation, slopes)


def call(kernel, out_shape, flops, moved, limit=VMEM_LIMIT, in_specs=None, after=(), **more):
    def run(*operands):
        given = in_specs or [pl.BlockSpec(memory_space=pltpu.VMEM)] * len(operands)
        return pl.pallas_call(
            lambda *refs: kernel(*refs[len(after) :]),
            out_shape=out_shape,
            in_specs=[pl.BlockSpec(memory_space=pl.ANY)] * len(after) + list(given),
            compiler_params=pltpu.CompilerParams(vmem_limit_bytes=limit),
            cost_estimate=pl.CostEstimate(flops=flops, bytes_accessed=moved, transcendentals=0),
            **more,
        )(*after, *operands)

    return run


def own_expert():
    half_nodes = lax.axis_size("node") // WINDOW
    return lax.axis_index("node") // half_nodes


def split_value(value):
    high = value.astype(BF16).astype(F32)
    lane = lax.broadcasted_iota(jnp.int32, (value.shape[0], LANES), 1)
    return jnp.where(lane == 0, high, jnp.where(lane == 1, value - high, 0.0))


def encode(values):
    top = jnp.max(jnp.abs(values), axis=1, keepdims=True)
    power = jnp.ceil(jnp.log2(jnp.maximum(top, 1e-30)))
    codes = jnp.round(values * (1.999 * jnp.exp2(14.0 - power)))
    return codes.astype(jnp.int32).astype(I16), power


def decode(codes, power):
    return codes.astype(jnp.int32).astype(F32) * (jnp.exp2(power - 14.0) / 1.999)


def store_codes(out_ref, pair):
    hidden = pair[0].shape[1]
    lane = lax.broadcasted_iota(jnp.int32, (pair[0].shape[0], LANES), 1)
    powers = []
    for index, values in enumerate(pair):
        codes, power = encode(values)
        out_ref[:, index * hidden : (index + 1) * hidden] = codes
        powers.append(power)
    powers = jnp.where(lane == 0, powers[0], powers[1])
    out_ref[:, 2 * hidden :] = powers.astype(jnp.int32).astype(I16)


def load_codes(ref):
    hidden = (ref.shape[1] - LANES) // 2
    powers = ref[:, 2 * hidden :].astype(jnp.int32).astype(F32)
    return [
        decode(ref[:, index * hidden : (index + 1) * hidden], powers[:, index : index + 1])
        for index in range(2)
    ]


def gather_kernel(routes_hbm, gates_hbm, tokens_hbm, grads_hbm, w_in_hbm, w_out_hbm, own_ref,
                  other_ref, place_ref, spread_ref, w_ref, routes_ref, gates_ref, tokens_ref,
                  grads_ref, sems):
    tok_rows, feats = tokens_ref.shape
    capacity = own_ref.shape[0] // 2
    slots = WINDOW * capacity
    copies = [
        pltpu.make_async_copy(routes_hbm, routes_ref, sems.at[0]),
        pltpu.make_async_copy(gates_hbm, gates_ref, sems.at[1]),
    ]
    count = tok_rows // PIECES
    for source, target in ((tokens_hbm, tokens_ref), (grads_hbm, grads_ref)):
        for piece in range(PIECES):
            span = pl.ds(piece * count, count)
            copies.append(
                pltpu.make_async_copy(source.at[span], target.at[span], sems.at[len(copies)])
            )
    hidden = w_out_hbm.shape[0]
    upper, lower = pl.ds(0, hidden), pl.ds(hidden, hidden)
    moves = [(w_out_hbm, w_ref.at[upper])]
    for block in range(0, feats, hidden):
        span = pl.ds(block, hidden)
        moves.append((w_in_hbm.at[span], w_ref.at[lower, span]))
    for source, target in moves:
        copies.append(pltpu.make_async_copy(source, target, sems.at[len(copies)]))
    for copy in copies:
        copy.start()
    earlier = lax.broadcasted_iota(jnp.int32, (tok_rows, tok_rows), 0) < lax.broadcasted_iota(
        jnp.int32, (tok_rows, tok_rows), 1
    )
    earlier = earlier.astype(F32).astype(BF16)
    slot_of = lax.broadcasted_iota(jnp.int32, (capacity, tok_rows), 0).astype(F32)
    row_of = lax.broadcasted_iota(jnp.int32, (8, tok_rows), 0)
    own = own_expert()
    copies[0].wait()
    copies[1].wait()
    routes = routes_ref[...]
    gates = gates_ref[...].astype(F32)
    hits = [(routes == expert).astype(F32) for expert in (own, 1 - own)]
    named = [hit[0:1] + hit[1:2] for hit in hits]
    weight = [hit * gates for hit in hits]
    weight = [value[0:1] + value[1:2] for value in weight]
    names = jnp.where(row_of == 0, named[0], jnp.where(row_of == 1, named[1], 0.0)).astype(BF16)
    before = jnp.dot(names, earlier, preferred_element_type=F32)
    parts = [jnp.where(before[e : e + 1] == slot_of, named[e], 0.0) for e in range(WINDOW)]
    place = jnp.concatenate(parts, axis=0).astype(BF16)
    place_ref[:slots] = place
    spread_ref[...] = jnp.concatenate(parts + parts, axis=0).T.astype(BF16)
    masks = jnp.zeros((16, tok_rows), F32)
    row_of = lax.broadcasted_iota(jnp.int32, masks.shape, 0)
    for index, hit in enumerate(hits):
        for k in range(2):
            masks = jnp.where(row_of == 2 * index + k, hit[k : k + 1], masks)
    place_ref[slots:] = masks.astype(BF16)
    for copy in copies[2 : 2 + PIECES]:
        copy.wait()
    rows_x = jnp.dot(place, tokens_ref[...], preferred_element_type=F32)
    for copy in copies[2 + PIECES : 2 + 2 * PIECES]:
        copy.wait()
    rows_dy = jnp.dot(place, grads_ref[...], preferred_element_type=F32)
    for expert, out_ref in ((0, own_ref), (1, other_ref)):
        span = slice(expert * capacity, (expert + 1) * capacity)
        out_ref[:, :feats] = jnp.concatenate([rows_x[span], rows_dy[span]], axis=0).astype(BF16)
        gate = jnp.sum(parts[expert] * weight[expert], axis=1, keepdims=True)
        gate = jnp.concatenate([gate, gate], axis=0)
        out_ref[:, feats:] = jnp.broadcast_to(gate, (2 * capacity, LANES)).astype(BF16)
    for copy in copies[2 + 2 * PIECES :]:
        copy.wait()


def join_kernel(*refs):
    *pieces, out_ref = refs
    rows = pieces[0].shape[0]
    for index, ref in enumerate(pieces):
        out_ref[index * rows : (index + 1) * rows] = ref[...]


def part_kernel(capacity, rows_ref, w_ref, w_other_ref, part_ref, gate_ref):
    feats = w_ref.shape[1]
    hidden = w_ref.shape[0] // 2
    groups = rows_ref.shape[0] // (2 * capacity)
    gate = rows_ref[:, feats:].astype(F32).reshape(groups, 2 * capacity, LANES)
    gate_ref[...] = gate[:, :capacity].reshape(groups * capacity, LANES)
    rows = rows_ref[:, :feats]
    pre = []
    back = []
    for ref in (w_ref, w_other_ref):
        pre.append(
            sum(
                jnp.dot(
                    rows[:, block : block + hidden],
                    ref[hidden:, block : block + hidden],
                    preferred_element_type=F32,
                )
                for block in range(0, feats, hidden)
            )
        )
        back.append(
            lax.dot_general(rows, ref[:hidden], COLS_BY_COLS, preferred_element_type=F32)
        )
    pair = []
    for values, span in ((pre, slice(0, capacity)), (back, slice(capacity, 2 * capacity))):
        values = jnp.concatenate(values, axis=1).reshape(groups, 2 * capacity, 2 * hidden)
        pair.append(values[:, span].reshape(groups * capacity, 2 * hidden))
    store_codes(part_ref, pair)


def add_codes_kernel(first_ref, second_ref, out_ref):
    pairs = zip(load_codes(first_ref), load_codes(second_ref))
    store_codes(out_ref, [first + second for first, second in pairs])


def deal(total, refs):
    each, wide = refs[0].shape
    feats = wide - LANES
    gate = split_value(jnp.sum(total[:, feats:], axis=1, keepdims=True))
    for index, ref in enumerate(refs):
        span = slice(index * each, (index + 1) * each)
        ref[:, :feats] = total[span, :feats].astype(ref.dtype)
        ref[:, feats:] = gate[span].astype(ref.dtype)


def slot_kernel(capacity, first_ref, second_ref, gate_ref, w_ref, w_other_ref, mine_ref,
                theirs_ref, *slot_refs):
    hidden = w_ref.shape[0] // 2
    pairs = zip(load_codes(first_ref), load_codes(second_ref))
    pre, back = [first + second for first, second in pairs]
    gate = gate_ref[:, :1]
    activation, slopes = gelu_pair(pre)
    dpre = (gate * back * slopes).astype(BF16)
    act = gate * activation
    slot = []
    for block in range(0, w_ref.shape[1], hidden):
        span = slice(block, block + hidden)
        slot.append(
            sum(
                lax.dot_general(
                    part, ref[hidden:, span], COLS_BY_COLS, preferred_element_type=F32
                )
                for part, ref in ((dpre[:, :hidden], w_ref), (dpre[:, hidden:], w_other_ref))
            )
        )
    slot_gate = split_value(jnp.sum(activation * back, axis=1, keepdims=True))
    total = jnp.concatenate(slot + [slot_gate], axis=1)
    if len(slot_refs) == 1:
        slot_refs[0][...] = total
    else:
        deal(total, slot_refs)
    rows = dpre.shape[0]
    both = [
        value.reshape(rows // capacity, capacity, 2 * hidden) for value in (dpre.astype(F32), act)
    ]
    both = jnp.concatenate(both, axis=1).reshape(2 * rows, 2 * hidden).astype(BF16)
    mine_ref[...] = both[:, :hidden]
    theirs_ref[...] = both[:, hidden:]


def halve_kernel(kept_ref, came_ref, keep_ref, send_ref):
    half = keep_ref.shape[0]
    total = kept_ref[...] + came_ref[...]
    keep_ref[...] = total[:half]
    send_ref[...] = total[half:]


def deal_kernel(kept_ref, came_ref, *refs):
    deal(kept_ref[...] + came_ref[...], refs)


def weight_kernel(capacity, *refs):
    rows_refs, both_refs = refs[:4], refs[4:8]
    w_in_hbm, w_out_hbm, written_ref, w_in_ref, w_out_ref, sems = refs[8:]
    feats, hidden = w_in_ref.shape
    rows = jnp.concatenate([ref[:, :feats] for ref in rows_refs], axis=0)
    both = jnp.concatenate([ref[...] for ref in both_refs], axis=0).astype(F32)
    of_x = lax.broadcasted_iota(jnp.int32, both.shape, 0) % (2 * capacity) < capacity
    dpre = jnp.where(of_x, both, 0.0).astype(BF16)
    act = jnp.where(of_x, 0.0, both).astype(BF16)
    count = feats // PIECES
    copies = []
    for piece in range(PIECES):
        span = slice(piece * count, (piece + 1) * count)
        part = rows[:, span]
        w_in_ref[span] = lax.dot_general(part, dpre, ROWS_BY_ROWS, preferred_element_type=F32)
        w_out_ref[:, span] = lax.dot_general(act, part, ROWS_BY_ROWS, preferred_element_type=F32)
        span = pl.ds(piece * count, count)
        for source, target in (
            (w_in_ref.at[span], w_in_hbm.at[span]),
            (w_out_ref.at[:, span], w_out_hbm.at[:, span]),
        ):
            copy = pltpu.make_async_copy(source, target, sems.at[len(copies)])
            copy.start()
            copies.append(copy)
    for copy in copies:
        copy.wait()
    written_ref[...] = jnp.zeros(written_ref.shape, F32)


def combine_kernel(steps, *refs):
    kept_ref, came_refs = refs[0], refs[1:steps]
    place_ref, spread_ref, tokens_ref, gate_out_ref = refs[steps:]
    feats = tokens_ref.shape[1]
    capacity = kept_ref.shape[0]
    came = [ref[...].astype(F32) for ref in came_refs]
    half = steps // WINDOW
    own = sum(came[: half - 1], kept_ref[...])
    other = sum(came[half:], came[half - 1])
    slots = jnp.concatenate([own, other], axis=0)
    grads = slots[:, :feats]
    high = grads.astype(BF16)
    low = (grads - high.astype(F32)).astype(BF16)
    both = jnp.concatenate([high, low], axis=0)
    tokens_ref[...] = jnp.dot(spread_ref[...], both, preferred_element_type=F32).astype(BF16)
    slot_gate = jnp.sum(slots[:, feats:], axis=1, keepdims=True)
    picked = place_ref[: WINDOW * capacity].astype(F32) * slot_gate
    masks = place_ref[WINDOW * capacity :].astype(F32)
    result = jnp.zeros(gate_out_ref.shape, F32)
    for index in range(WINDOW):
        span = slice(index * capacity, (index + 1) * capacity)
        value = jnp.sum(picked[span], axis=0, keepdims=True)
        result = result + masks[2 * index : 2 * index + 2] * value
    gate_out_ref[...] = result


def swap(array, axes, bit):
    size = lax.axis_size(axes)
    return lax.ppermute(array, axes, [(index, index ^ bit) for index in range(size)])


def join(pieces, after=()):
    rows, wide = pieces[0].shape
    rows *= len(pieces)
    shape = jax.ShapeDtypeStruct((rows, wide), BF16)
    return call(join_kernel, shape, 0, 4 * rows * wide, after=after)(*pieces)


def body(tokens, grad_out, routes, gates, w_in, w_out):
    nodes = lax.axis_size("node")
    locals_ = lax.axis_size("local")
    edatas = lax.axis_size("edata")
    tok_rows, feats = tokens.shape
    hidden = w_in.shape[1]
    capacity = 2 * tok_rows // EXPERTS
    slots = WINDOW * capacity
    wide = feats + LANES
    coded = 4 * hidden + LANES
    shape = jax.ShapeDtypeStruct
    hbm = pl.BlockSpec(memory_space=pltpu.HBM)
    vmem = pl.BlockSpec(memory_space=pltpu.VMEM)

    inputs = [
        pltpu.with_memory_space_constraint(value, pltpu.HBM)
        for value in (routes.T, gates.T, tokens, grad_out, w_in, w_out)
    ]
    own_rows, other_rows, place, spread, weights = call(
        gather_kernel,
        (
            pltpu.VMEM((2 * capacity, wide), BF16),
            pltpu.VMEM((2 * capacity, wide), BF16),
            pltpu.VMEM((slots + 16, tok_rows), BF16),
            pltpu.VMEM((tok_rows, 2 * slots), BF16),
            pltpu.VMEM((2 * hidden, feats), BF16),
        ),
        4 * slots * tok_rows * feats,
        4 * tok_rows * feats + 4 * hidden * feats,
        in_specs=[hbm] * 6,
        scratch_shapes=[
            pltpu.VMEM((2, tok_rows), jnp.int32),
            pltpu.VMEM((2, tok_rows), BF16),
            pltpu.VMEM((tok_rows, feats), BF16),
            pltpu.VMEM((tok_rows, feats), BF16),
            pltpu.SemaphoreType.DMA((3 + 2 * PIECES + feats // hidden,)),
        ],
    )(*inputs)

    other_weights = swap(weights, "local", 1)

    half_nodes = nodes // WINDOW
    pieces = [own_rows]
    for step in range(1, nodes):
        pieces.append(swap(own_rows if step < half_nodes else other_rows, "node", step))
    rows = half_nodes * (locals_ // 2) * capacity
    last = ()
    chains = []
    held = []
    for chunk in (pieces[:half_nodes], pieces[half_nodes:]):
        chunk = join(chunk, last)
        bit = 2
        while bit < locals_:
            chunk = join([chunk, swap(chunk, "local", bit)])
            bit *= 2
        held.append(chunk)
        part, gate_rows = call(
            functools.partial(part_kernel, capacity),
            (shape((rows, coded), I16), shape((rows, LANES), F32)),
            16 * rows * feats * hidden,
            4 * rows * feats + 8 * feats * hidden,
            after=last,
        )(chunk, weights, other_weights)
        last = (part,)
        chains.append((part, swap(part, "edata", 1), gate_rows))
    bit = 2
    while bit < edatas:
        for index, (part, other, gate_rows) in enumerate(chains):
            part = call(
                add_codes_kernel,
                shape((rows, coded), I16),
                16 * rows * hidden,
                6 * rows * coded,
                after=last,
            )(part, other)
            last = (part,)
            chains[index] = (part, swap(part, "edata", bit), gate_rows)
        bit *= 2

    mine = []
    back = []
    slots_back = []
    for index, (part, other, gate_rows) in enumerate(chains):
        dealt = [shape((capacity, wide), BF16)] * half_nodes
        if index == 0:
            dealt[0] = shape((capacity, wide), F32)
        own, theirs, *slot_parts = call(
            functools.partial(slot_kernel, capacity),
            [shape((2 * rows, hidden), BF16)] * 2
            + (dealt if locals_ == 2 else [shape((rows, wide), F32)]),
            4 * rows * feats * hidden,
            4 * feats * hidden + 4 * rows * feats,
            after=last,
        )(part, other, gate_rows, weights, other_weights)
        last = (own,)
        mine.append(own)
        back.append(swap(theirs, "local", 1))
        if locals_ > 2:
            half = rows // 2
            keep, send = slot_parts[0][:half], slot_parts[0][half:]
            bit = locals_ // 2
            while bit > 2:
                half //= 2
                keep, send = call(
                    halve_kernel,
                    (shape((half, wide), F32),) * 2,
                    4 * half * wide,
                    24 * half * wide,
                )(keep, swap(send, "local", bit))
                bit //= 2
            slot_parts = call(deal_kernel, dealt, 4 * half * wide, 12 * half * wide)(
                keep, swap(send, "local", bit)
            )
        for step, send in enumerate(slot_parts, index * half_nodes):
            slots_back.append(swap(send, "node", step) if step else send)
    came = [swap(chunk, "local", 1) for chunk in held]
    grad_w_in, grad_w_out, written = call(
        functools.partial(weight_kernel, capacity),
        (shape((feats, hidden), F32), shape((hidden, feats), F32), shape((8, LANES), F32)),
        32 * rows * feats * hidden,
        8 * feats * hidden,
        in_specs=[vmem] * 8,
        after=slots_back[1:half_nodes],
        out_specs=[hbm, hbm, vmem],
        scratch_shapes=[
            pltpu.VMEM((feats, hidden), F32),
            pltpu.VMEM((hidden, feats), F32),
            pltpu.SemaphoreType.DMA((2 * PIECES,)),
        ],
    )(*held, *came, *mine, *back)
    grad_tokens, grad_gates = call(
        functools.partial(combine_kernel, nodes),
        (shape((tok_rows, feats), BF16), shape((2, tok_rows), F32)),
        4 * slots * tok_rows * feats,
        2 * tok_rows * feats,
        after=(written,),
    )(*slots_back[:half_nodes], *reversed(slots_back[half_nodes:]), place, spread)
    return (grad_tokens, grad_gates.T, grad_w_in, grad_w_out)


def solution(mesh):
    in_specs = (
        P(("node", "local"), "edata"),
        P(("node", "local"), "edata"),
        P(("node", "local"), None),
        P(("node", "local"), None),
        P("edata", ("node", "local")),
        P(("node", "local"), "edata"),
    )
    out_specs = (
        P(("node", "local"), "edata"),
        P(("node", "local"), None),
        P("edata", ("node", "local")),
        P(("node", "local"), "edata"),
    )
    return jax.shard_map(body, mesh=mesh, in_specs=in_specs, out_specs=out_specs, check_vma=False)
```

profile of v0, /device:TPU:0, one launch (start us, length us, event | category | flops | bytes accessed | tf_op | source)
XLA Modules:
  0.0 29.0 jit_solution(10495697648084487022)
XLA Ops:
  0.6 1.8 %shard_map.93 = (bf16[16,1152]{1,0:T(8,128)(2,1)S(1)}, bf16[16,1152]{1,0:T(8,128)(2,1)S(1)}, bf16[32,256]{1,0:T(8,128)(2,1)S(1)}, bf16[256,32]{1,0:T(8,128)(2,1)S(1)}, bf16[512,1024]{1,0:T(8,128)(2,1)S(1)}) custom-call(s32[2,256]{1,0:T(2,128)} %bitcast.3, bf16[2,256]{1,0:T(2,128)(2,1)} %bitcast.4, bf16[256,1024]{1,0:T(8,128)(2,1)} %refs_2_.1, ...), custom_call_target="tpu_custom_call" | custom-call | flops 16777216 | bytes 2097152 | tf_op jit(solution)/shard_map/pallas_call | solution.py:38
  2.4 0.5 %collective-permute-start.1 = (bf16[512,1024]{1,0:T(8,128)(2,1)S(1)}, bf16[512,1024]{1,0:T(8,128)(2,1)S(1)}, u32[]{:S(2)}, u32[]{:S(2)}) collective-permute-start(bf16[512,1024]{1,0:T(8,128)(2,1)S(1)} %get-tuple-element.27.refs_1_.refs_2_.refs_4_), channel_id=1, source_target_pairs={{0,4},{4,0},{1,5},{5,1},{2,6},{6,2},{3,7},{7,3},{8,12},{12,8},{9,1... | collective-permute-start | bytes 3145736 | tf_op jit(solution)/shard_map/ppermute | solution.py:318
  2.9 2.6 %collective-permute-start = (bf16[16,1152]{1,0:T(8,128)(2,1)S(1)}, bf16[16,1152]{1,0:T(8,128)(2,1)S(1)}, u32[]{:S(2)}, u32[]{:S(2)}) collective-permute-start(bf16[16,1152]{1,0:T(8,128)(2,1)S(1)} %get-tuple-element.26.refs_0_), channel_id=1, source_target_pairs={{0,8},{8,0},{16,24},{24,16},{1,9},{9,1},{17,25},{25,17},{2,10},{10... | collective-permute-start | bytes 110600 | tf_op jit(solution)/shard_map/ppermute | solution.py:318
  5.5 1.5 %collective-permute-start.3 = (bf16[16,1152]{1,0:T(8,128)(2,1)S(1)}, bf16[16,1152]{1,0:T(8,128)(2,1)S(1)}, u32[]{:S(2)}, u32[]{:S(2)}) collective-permute-start(bf16[16,1152]{1,0:T(8,128)(2,1)S(1)} %get-tuple-element.29), channel_id=1, source_target_pairs={{0,24},{8,16},{16,8},{24,0},{1,25},{9,17},{17,9},{25,1},{2,26},{10... | collective-permute-start | bytes 110600 | tf_op jit(solution)/shard_map/ppermute | solution.py:318
  7.0 0.1 collective-permute-start.2
  7.0 0.5 %collective-permute-done.refs_1_ = bf16[16,1152]{1,0:T(8,128)(2,1)S(1)} collective-permute-done((bf16[16,1152]{1,0:T(8,128)(2,1)S(1)}, bf16[16,1152]{1,0:T(8,128)(2,1)S(1)}, u32[]{:S(2)}, u32[]{:S(2)}) %collective-permute-start) | collective-permute-done | bytes 36896 | tf_op jit(solution)/shard_map/ppermute | solution.py:318
  7.6 0.0 collective-permute-done.1.refs_2_.refs_3_.refs_5_
  7.6 0.7 %shard_map.95 = (s16[16,1152]{1,0:T(8,128)(2,1)S(1)}, f32[16,128]{1,0:T(8,128)S(1)}) custom-call(bf16[32,1152]{1,0:T(8,128)(2,1)S(1)} %shard_map.94.refs_0_.refs_1_, bf16[512,1024]{1,0:T(8,128)(2,1)S(1)} %get-tuple-element.27.refs_1_.refs_2_.refs_4_, bf16[512,1024]{1,0:T(8,128)(2,1)S(1)} %collective-permute-done.1.refs_2_.refs_3_.refs_5_), custom_call_target="tpu_custom_call" | custom-call | flops 67108864 | bytes 2162688 | tf_op jit(solution)/shard_map/pallas_call | solution.py:38
  8.2 2.0 %collective-permute-start.4 = (s16[16,1152]{1,0:T(8,128)(2,1)S(1)}, s16[16,1152]{1,0:T(8,128)(2,1)S(1)}, u32[]{:S(2)}, u32[]{:S(2)}) collective-permute-start(s16[16,1152]{1,0:T(8,128)(2,1)S(1)} %get-tuple-element.28.refs_0_.refs_1_), channel_id=1, source_target_pairs={{0,1},{1,0},{2,3},{3,2},{4,5},{5,4},{6,7},{7,6},{8,9},{9,8},{10,11... | collective-permute-start | bytes 110600 | tf_op jit(solution)/shard_map/ppermute | solution.py:318
  10.3 0.1 collective-permute-done.3.refs_2_
  10.3 0.6 %collective-permute-done.2.refs_1_ = bf16[16,1152]{1,0:T(8,128)(2,1)S(1)} collective-permute-done((bf16[16,1152]{1,0:T(8,128)(2,1)S(1)}, bf16[16,1152]{1,0:T(8,128)(2,1)S(1)}, u32[]{:S(2)}, u32[]{:S(2)}) %collective-permute-start.2) | collective-permute-done | bytes 36896 | tf_op jit(solution)/shard_map/ppermute | solution.py:318
  10.9 0.7 %shard_map.97 = (s16[16,1152]{1,0:T(8,128)(2,1)S(1)}, f32[16,128]{1,0:T(8,128)S(1)}) custom-call(s16[16,1152]{1,0:T(8,128)(2,1)S(1)} %get-tuple-element.28.refs_0_.refs_1_, bf16[32,1152]{1,0:T(8,128)(2,1)S(1)} %shard_map.96.refs_1_.refs_2_, bf16[512,1024]{1,0:T(8,128)(2,1)S(1)} %get-tuple-element.27.refs_1_.refs_2_.refs_4_, ...), custom_call_target="tpu_custom_call" | custom-call | flops 67108864 | bytes 2162688 | tf_op jit(solution)/shard_map/pallas_call | solution.py:38
  11.6 1.6 %collective-permute-start.5 = (s16[16,1152]{1,0:T(8,128)(2,1)S(1)}, s16[16,1152]{1,0:T(8,128)(2,1)S(1)}, u32[]{:S(2)}, u32[]{:S(2)}) collective-permute-start(s16[16,1152]{1,0:T(8,128)(2,1)S(1)} %get-tuple-element.30.refs_0_.refs_1_), channel_id=1, source_target_pairs={{0,1},{1,0},{2,3},{3,2},{4,5},{5,4},{6,7},{7,6},{8,9},{9,8},{10,11... | collective-permute-start | bytes 110600 | tf_op jit(solution)/shard_map/ppermute | solution.py:318
  13.3 0.0 collective-permute-start.8
  13.3 0.5 %collective-permute-start.9 = (bf16[32,1152]{1,0:T(8,128)(2,1)S(1)}, bf16[32,1152]{1,0:T(8,128)(2,1)S(1)}, u32[]{:S(2)}, u32[]{:S(2)}) collective-permute-start(bf16[32,1152]{1,0:T(8,128)(2,1)S(1)} %shard_map.96.refs_1_.refs_2_), channel_id=1, source_target_pairs={{0,4},{4,0},{1,5},{5,1},{2,6},{6,2},{3,7},{7,3},{8,12},{12,8},{9,1... | collective-permute-start | bytes 221192 | tf_op jit(solution)/shard_map/ppermute | solution.py:318
  13.8 0.0 collective-permute-done.4.refs_2_
  13.8 0.2 shard_map.98.refs_0_.refs_1_
  14.0 2.7 %collective-permute-start.6 = (s16[16,1152]{1,0:T(8,128)(2,1)S(1)}, s16[16,1152]{1,0:T(8,128)(2,1)S(1)}, u32[]{:S(2)}, u32[]{:S(2)}) collective-permute-start(s16[16,1152]{1,0:T(8,128)(2,1)S(1)} %shard_map.98.refs_0_.refs_1_), channel_id=1, source_target_pairs={{0,2},{1,3},{2,0},{3,1},{4,6},{5,7},{6,4},{7,5},{8,10},{9,11},{10,... | collective-permute-start | bytes 110600 | tf_op jit(solution)/shard_map/ppermute | solution.py:318
  16.6 0.0 collective-permute-done.5.refs_2_
  16.6 0.2 shard_map.99.refs_0_.refs_1_
  16.8 1.9 %collective-permute-start.10 = (s16[16,1152]{1,0:T(8,128)(2,1)S(1)}, s16[16,1152]{1,0:T(8,128)(2,1)S(1)}, u32[]{:S(2)}, u32[]{:S(2)}) collective-permute-start(s16[16,1152]{1,0:T(8,128)(2,1)S(1)} %shard_map.99.refs_0_.refs_1_), channel_id=1, source_target_pairs={{0,2},{1,3},{2,0},{3,1},{4,6},{5,7},{6,4},{7,5},{8,10},{9,11},{10,... | collective-permute-start | bytes 110600 | tf_op jit(solution)/shard_map/ppermute | solution.py:318
  18.7 0.4 %collective-permute-done.6.refs_2_ = s16[16,1152]{1,0:T(8,128)(2,1)S(1)} collective-permute-done((s16[16,1152]{1,0:T(8,128)(2,1)S(1)}, s16[16,1152]{1,0:T(8,128)(2,1)S(1)}, u32[]{:S(2)}, u32[]{:S(2)}) %collective-permute-start.6) | collective-permute-done | bytes 36896 | tf_op jit(solution)/shard_map/ppermute | solution.py:318
  19.2 0.4 %shard_map.100 = (bf16[32,256]{1,0:T(8,128)(2,1)S(1)}, bf16[32,256]{1,0:T(8,128)(2,1)S(1)}, f32[8,1152]{1,0:T(8,128)S(1)}, bf16[8,1152]{1,0:T(8,128)(2,1)S(1)}) custom-call(s16[16,1152]{1,0:T(8,128)(2,1)S(1)} %shard_map.99.refs_0_.refs_1_, s16[16,1152]{1,0:T(8,128)(2,1)S(1)} %shard_map.98.refs_0_.refs_1_, ...), custom_call_target="tpu_custom_call" | custom-call | flops 16777216 | bytes 1114112 | tf_op jit(solution)/shard_map/pallas_call | solution.py:38
  19.6 1.5 %collective-permute-start.7 = (bf16[8,1152]{1,0:T(8,128)(2,1)S(1)}, bf16[8,1152]{1,0:T(8,128)(2,1)S(1)}, u32[]{:S(2)}, u32[]{:S(2)}) collective-permute-start(bf16[8,1152]{1,0:T(8,128)(2,1)S(1)} %get-tuple-element.32), channel_id=1, source_target_pairs={{0,8},{8,0},{16,24},{24,16},{1,9},{9,1},{17,25},{25,17},{2,10},{10... | collective-permute-start | bytes 55304 | tf_op jit(solution)/shard_map/ppermute | solution.py:318
  21.1 0.0 collective-permute-start.11
  21.1 1.0 %collective-permute-done.10.refs_2_ = s16[16,1152]{1,0:T(8,128)(2,1)S(1)} collective-permute-done((s16[16,1152]{1,0:T(8,128)(2,1)S(1)}, s16[16,1152]{1,0:T(8,128)(2,1)S(1)}, u32[]{:S(2)}, u32[]{:S(2)}) %collective-permute-start.10) | collective-permute-done | bytes 36896 | tf_op jit(solution)/shard_map/ppermute | solution.py:318
  22.1 0.4 %shard_map.101 = (bf16[32,256]{1,0:T(8,128)(2,1)S(1)}, bf16[32,256]{1,0:T(8,128)(2,1)S(1)}, bf16[8,1152]{1,0:T(8,128)(2,1)S(1)}, bf16[8,1152]{1,0:T(8,128)(2,1)S(1)}) custom-call(bf16[32,256]{1,0:T(8,128)(2,1)S(1)} %get-tuple-element.33.refs_0_.refs_5_, s16[16,1152]{1,0:T(8,128)(2,1)S(1)} %shard_map.99.refs_0_.refs_1_, ...), custom_call_target="tpu_custom_call" | custom-call | flops 16777216 | bytes 1114112 | tf_op jit(solution)/shard_map/pallas_call | solution.py:38
  22.5 0.0 collective-permute-start.12
  22.5 0.0 collective-permute-done.8.refs_3_
  22.6 1.6 %collective-permute-start.13 = (bf16[8,1152]{1,0:T(8,128)(2,1)S(1)}, bf16[8,1152]{1,0:T(8,128)(2,1)S(1)}, u32[]{:S(2)}, u32[]{:S(2)}) collective-permute-start(bf16[8,1152]{1,0:T(8,128)(2,1)S(1)} %get-tuple-element.40), channel_id=1, source_target_pairs={{0,24},{8,16},{16,8},{24,0},{1,25},{9,17},{17,9},{25,1},{2,26},{10... | collective-permute-start | bytes 55304 | tf_op jit(solution)/shard_map/ppermute | solution.py:318
  24.1 0.0 collective-permute-done.9.refs_4_
  24.1 1.5 %collective-permute-start.14 = (bf16[8,1152]{1,0:T(8,128)(2,1)S(1)}, bf16[8,1152]{1,0:T(8,128)(2,1)S(1)}, u32[]{:S(2)}, u32[]{:S(2)}) collective-permute-start(bf16[8,1152]{1,0:T(8,128)(2,1)S(1)} %get-tuple-element.41), channel_id=1, source_target_pairs={{0,16},{8,24},{16,0},{24,8},{1,17},{9,25},{17,1},{25,9},{2,18},{10... | collective-permute-start | bytes 55304 | tf_op jit(solution)/shard_map/ppermute | solution.py:318
  25.6 0.0 collective-permute-done.11.refs_7_
  25.6 0.0 collective-permute-done.12.refs_8_
  25.6 0.0 collective-permute-done.7.refs_0_.refs_2_
  25.6 1.6 %shard_map.102 = (f32[1024,256]{1,0:T(8,128)}, f32[256,1024]{1,0:T(8,128)}, f32[8,128]{1,0:T(8,128)S(1)}) custom-call(bf16[8,1152]{1,0:T(8,128)(2,1)S(1)} %collective-permute-done.7.refs_0_.refs_2_, bf16[32,1152]{1,0:T(8,128)(2,1)S(1)} %shard_map.94.refs_0_.refs_1_, bf16[32,1152]{1,0:T(8,128)(2,1)S(1)} %shard_map.96.refs_1_.refs_2_, ...), custom_call_target="tpu_custom_call" | custom-call | flops 134217728 | bytes 2097152 | tf_op jit(solution)/shard_map/pallas_call | solution.py:38
  27.3 0.0 collective-permute-done.13.refs_3_
  27.3 0.6 %collective-permute-done.14.refs_4_ = bf16[8,1152]{1,0:T(8,128)(2,1)S(1)} collective-permute-done((bf16[8,1152]{1,0:T(8,128)(2,1)S(1)}, bf16[8,1152]{1,0:T(8,128)(2,1)S(1)}, u32[]{:S(2)}, u32[]{:S(2)}) %collective-permute-start.14) | collective-permute-done | bytes 18464 | tf_op jit(solution)/shard_map/ppermute | solution.py:318
  27.9 1.1 %shard_map.103 = (bf16[256,1024]{1,0:T(8,128)(2,1)}, f32[2,256]{1,0:T(2,128)}) custom-call(f32[8,128]{1,0:T(8,128)S(1)} %get-tuple-element.38.refs_0_, f32[8,1152]{1,0:T(8,128)S(1)} %get-tuple-element.39.refs_1_, bf16[8,1152]{1,0:T(8,128)(2,1)S(1)} %collective-permute-done.7.refs_0_.refs_2_, bf16[8,1152]{1,0:T(8,128)(2,1)S(1)} %collective-permute-done.13.refs_3_, ...), custom_call_target="tpu_custom_call" | custom-call | flops 16777216 | bytes 524288 | tf_op jit(solution)/shard_map/pallas_call | solution.py:38
  (2 shorter events, 0.0 us)
Async XLA Ops:
  2.4 5.2 %collective-permute-start.1 = (bf16[512,1024]{1,0:T(8,128)(2,1)S(1)}, bf16[512,1024]{1,0:T(8,128)(2,1)S(1)}, u32[]{:S(2)}, u32[]{:S(2)}) collective-permute-start(bf16[512,1024]{1,0:T(8,128)(2,1)S(1)} %get-tuple-element.27.refs_1_.refs_2_.refs_4_), channel_id=1, source_target_pairs={{0,4},{4,0},{1,5},{5,1},{2,6},{6,2},{3,7},{7,3},{8,12},{12,8},{9,1... | collective-permute-start | bytes 3145736 | tf_op jit(solution)/shard_map/ppermute | solution.py:318
  2.9 4.6 %collective-permute-start = (bf16[16,1152]{1,0:T(8,128)(2,1)S(1)}, bf16[16,1152]{1,0:T(8,128)(2,1)S(1)}, u32[]{:S(2)}, u32[]{:S(2)}) collective-permute-start(bf16[16,1152]{1,0:T(8,128)(2,1)S(1)} %get-tuple-element.26.refs_0_), channel_id=1, source_target_pairs={{0,8},{8,0},{16,24},{24,16},{1,9},{9,1},{17,25},{25,17},{2,10},{10... | collective-permute-start | bytes 110600 | tf_op jit(solution)/shard_map/ppermute | solution.py:318
  5.5 4.9 %collective-permute-start.3 = (bf16[16,1152]{1,0:T(8,128)(2,1)S(1)}, bf16[16,1152]{1,0:T(8,128)(2,1)S(1)}, u32[]{:S(2)}, u32[]{:S(2)}) collective-permute-start(bf16[16,1152]{1,0:T(8,128)(2,1)S(1)} %get-tuple-element.29), channel_id=1, source_target_pairs={{0,24},{8,16},{16,8},{24,0},{1,25},{9,17},{17,9},{25,1},{2,26},{10... | collective-permute-start | bytes 110600 | tf_op jit(solution)/shard_map/ppermute | solution.py:318
  7.0 4.0 %collective-permute-start.2 = (bf16[16,1152]{1,0:T(8,128)(2,1)S(1)}, bf16[16,1152]{1,0:T(8,128)(2,1)S(1)}, u32[]{:S(2)}, u32[]{:S(2)}) collective-permute-start(bf16[16,1152]{1,0:T(8,128)(2,1)S(1)} %get-tuple-element.29), channel_id=1, source_target_pairs={{0,16},{8,24},{16,0},{24,8},{1,17},{9,25},{17,1},{25,9},{2,18},{10... | collective-permute-start | bytes 110600 | tf_op jit(solution)/shard_map/ppermute | solution.py:318
  8.2 5.5 %collective-permute-start.4 = (s16[16,1152]{1,0:T(8,128)(2,1)S(1)}, s16[16,1152]{1,0:T(8,128)(2,1)S(1)}, u32[]{:S(2)}, u32[]{:S(2)}) collective-permute-start(s16[16,1152]{1,0:T(8,128)(2,1)S(1)} %get-tuple-element.28.refs_0_.refs_1_), channel_id=1, source_target_pairs={{0,1},{1,0},{2,3},{3,2},{4,5},{5,4},{6,7},{7,6},{8,9},{9,8},{10,11... | collective-permute-start | bytes 110600 | tf_op jit(solution)/shard_map/ppermute | solution.py:318
  11.6 5.0 %collective-permute-start.5 = (s16[16,1152]{1,0:T(8,128)(2,1)S(1)}, s16[16,1152]{1,0:T(8,128)(2,1)S(1)}, u32[]{:S(2)}, u32[]{:S(2)}) collective-permute-start(s16[16,1152]{1,0:T(8,128)(2,1)S(1)} %get-tuple-element.30.refs_0_.refs_1_), channel_id=1, source_target_pairs={{0,1},{1,0},{2,3},{3,2},{4,5},{5,4},{6,7},{7,6},{8,9},{9,8},{10,11... | collective-permute-start | bytes 110600 | tf_op jit(solution)/shard_map/ppermute | solution.py:318
  13.3 9.3 %collective-permute-start.8 = (bf16[32,1152]{1,0:T(8,128)(2,1)S(1)}, bf16[32,1152]{1,0:T(8,128)(2,1)S(1)}, u32[]{:S(2)}, u32[]{:S(2)}) collective-permute-start(bf16[32,1152]{1,0:T(8,128)(2,1)S(1)} %shard_map.94.refs_0_.refs_1_), channel_id=1, source_target_pairs={{0,4},{4,0},{1,5},{5,1},{2,6},{6,2},{3,7},{7,3},{8,12},{12,8},{9,1... | collective-permute-start | bytes 221192 | tf_op jit(solution)/shard_map/ppermute | solution.py:318
  13.3 10.9 %collective-permute-start.9 = (bf16[32,1152]{1,0:T(8,128)(2,1)S(1)}, bf16[32,1152]{1,0:T(8,128)(2,1)S(1)}, u32[]{:S(2)}, u32[]{:S(2)}) collective-permute-start(bf16[32,1152]{1,0:T(8,128)(2,1)S(1)} %shard_map.96.refs_1_.refs_2_), channel_id=1, source_target_pairs={{0,4},{4,0},{1,5},{5,1},{2,6},{6,2},{3,7},{7,3},{8,12},{12,8},{9,1... | collective-permute-start | bytes 221192 | tf_op jit(solution)/shard_map/ppermute | solution.py:318
  14.0 5.2 %collective-permute-start.6 = (s16[16,1152]{1,0:T(8,128)(2,1)S(1)}, s16[16,1152]{1,0:T(8,128)(2,1)S(1)}, u32[]{:S(2)}, u32[]{:S(2)}) collective-permute-start(s16[16,1152]{1,0:T(8,128)(2,1)S(1)} %shard_map.98.refs_0_.refs_1_), channel_id=1, source_target_pairs={{0,2},{1,3},{2,0},{3,1},{4,6},{5,7},{6,4},{7,5},{8,10},{9,11},{10,... | collective-permute-start | bytes 110600 | tf_op jit(solution)/shard_map/ppermute | solution.py:318
  16.8 5.3 %collective-permute-start.10 = (s16[16,1152]{1,0:T(8,128)(2,1)S(1)}, s16[16,1152]{1,0:T(8,128)(2,1)S(1)}, u32[]{:S(2)}, u32[]{:S(2)}) collective-permute-start(s16[16,1152]{1,0:T(8,128)(2,1)S(1)} %shard_map.99.refs_0_.refs_1_), channel_id=1, source_target_pairs={{0,2},{1,3},{2,0},{3,1},{4,6},{5,7},{6,4},{7,5},{8,10},{9,11},{10,... | collective-permute-start | bytes 110600 | tf_op jit(solution)/shard_map/ppermute | solution.py:318
  19.6 6.0 %collective-permute-start.7 = (bf16[8,1152]{1,0:T(8,128)(2,1)S(1)}, bf16[8,1152]{1,0:T(8,128)(2,1)S(1)}, u32[]{:S(2)}, u32[]{:S(2)}) collective-permute-start(bf16[8,1152]{1,0:T(8,128)(2,1)S(1)} %get-tuple-element.32), channel_id=1, source_target_pairs={{0,8},{8,0},{16,24},{24,16},{1,9},{9,1},{17,25},{25,17},{2,10},{10... | collective-permute-start | bytes 55304 | tf_op jit(solution)/shard_map/ppermute | solution.py:318
  21.1 4.5 %collective-permute-start.11 = (bf16[32,256]{1,0:T(8,128)(2,1)S(1)}, bf16[32,256]{1,0:T(8,128)(2,1)S(1)}, u32[]{:S(2)}, u32[]{:S(2)}) collective-permute-start(bf16[32,256]{1,0:T(8,128)(2,1)S(1)} %get-tuple-element.36), channel_id=1, source_target_pairs={{0,4},{4,0},{1,5},{5,1},{2,6},{6,2},{3,7},{7,3},{8,12},{12,8},{9,1... | collective-permute-start | bytes 49160 | tf_op jit(solution)/shard_map/ppermute | solution.py:318
  22.5 3.1 %collective-permute-start.12 = (bf16[32,256]{1,0:T(8,128)(2,1)S(1)}, bf16[32,256]{1,0:T(8,128)(2,1)S(1)}, u32[]{:S(2)}, u32[]{:S(2)}) collective-permute-start(bf16[32,256]{1,0:T(8,128)(2,1)S(1)} %get-tuple-element.37), channel_id=1, source_target_pairs={{0,4},{4,0},{1,5},{5,1},{2,6},{6,2},{3,7},{7,3},{8,12},{12,8},{9,1... | collective-permute-start | bytes 49160 | tf_op jit(solution)/shard_map/ppermute | solution.py:318
  22.6 4.7 %collective-permute-start.13 = (bf16[8,1152]{1,0:T(8,128)(2,1)S(1)}, bf16[8,1152]{1,0:T(8,128)(2,1)S(1)}, u32[]{:S(2)}, u32[]{:S(2)}) collective-permute-start(bf16[8,1152]{1,0:T(8,128)(2,1)S(1)} %get-tuple-element.40), channel_id=1, source_target_pairs={{0,24},{8,16},{16,8},{24,0},{1,25},{9,17},{17,9},{25,1},{2,26},{10... | collective-permute-start | bytes 55304 | tf_op jit(solution)/shard_map/ppermute | solution.py:318
  24.1 3.8 %collective-permute-start.14 = (bf16[8,1152]{1,0:T(8,128)(2,1)S(1)}, bf16[8,1152]{1,0:T(8,128)(2,1)S(1)}, u32[]{:S(2)}, u32[]{:S(2)}) collective-permute-start(bf16[8,1152]{1,0:T(8,128)(2,1)S(1)} %get-tuple-element.41), channel_id=1, source_target_pairs={{0,16},{8,24},{16,0},{24,8},{1,17},{9,25},{17,1},{25,9},{2,18},{10... | collective-permute-start | bytes 55304 | tf_op jit(solution)/shard_map/ppermute | solution.py:318
where the time goes:
time: 29.1 us; the launch traced here: 29 us
  starting transfers between devices  17.9 us (62%)
  Pallas kernels  7.02 us (24%)
  waiting for transfers between devices  3.31 us (11%)
  between operations  0.7 us (2%)
    ppermute x15, starting transfers between devices, swap(): lax.ppermute(array, axes, [(index, index ^ bit) for index in range(size)])  17.9 us
    pallas_call x11, Pallas kernels, run(): pl.pallas_call(lambda *refs: kernel(*refs[len(after):]), out_shape=out_sh...  7.02 us
    ppermute x15, waiting for transfers between devices, swap(): lax.ppermute(array, axes, [(index, index ^ bit) for index in range(size)])  3.31 us
  transfers between devices with their start and end apart: 15, of which 6 were waited for; matrix products, arithmetic and copies ran while one was open for 0% of the time, Pallas kernels for 14%

commit v1 on v0

--- a/solution.py
+++ b/solution.py
@@ -212,8 +212,8 @@
         ref[:, feats:] = gate[span].astype(ref.dtype)
 
 
-def slot_kernel(capacity, first_ref, second_ref, gate_ref, w_ref, w_other_ref, mine_ref,
-                theirs_ref, *slot_refs):
+def slot_kernel(capacity, before, first_ref, second_ref, gate_ref, w_ref, w_other_ref, *refs):
+    before_refs, (mine_ref, theirs_ref, *slot_refs) = refs[:before], refs[before:]
     hidden = w_ref.shape[0] // 2
     pairs = zip(load_codes(first_ref), load_codes(second_ref))
     pre, back = [first + second for first, second in pairs]
@@ -244,7 +244,10 @@
     ]
     both = jnp.concatenate(both, axis=1).reshape(2 * rows, 2 * hidden).astype(BF16)
     mine_ref[...] = both[:, :hidden]
-    theirs_ref[...] = both[:, hidden:]
+    count = 2 * rows
+    for index, ref in enumerate(before_refs):
+        theirs_ref[index * count : (index + 1) * count] = ref[...]
+    theirs_ref[before * count :] = both[:, hidden:]
 
 
 def halve_kernel(kept_ref, came_ref, keep_ref, send_ref):
@@ -259,8 +262,8 @@
 
 
 def weight_kernel(capacity, *refs):
-    rows_refs, both_refs = refs[:4], refs[4:8]
-    w_in_hbm, w_out_hbm, written_ref, w_in_ref, w_out_ref, sems = refs[8:]
+    rows_refs, both_refs = refs[:4], refs[4:7]
+    w_in_hbm, w_out_hbm, written_ref, w_in_ref, w_out_ref, sems = refs[7:]
     feats, hidden = w_in_ref.shape
     rows = jnp.concatenate([ref[:, :feats] for ref in rows_refs], axis=0)
     both = jnp.concatenate([ref[...] for ref in both_refs], axis=0).astype(F32)
@@ -318,6 +321,10 @@
     return lax.ppermute(array, axes, [(index, index ^ bit) for index in range(size)])
 
 
+def swap_nodes(array, step):
+    return swap(array, ("node", "local"), step * lax.axis_size("local") + 1)
+
+
 def join(pieces, after=()):
     rows, wide = pieces[0].shape
     rows *= len(pieces)
@@ -369,7 +376,7 @@
     half_nodes = nodes // WINDOW
     pieces = [own_rows]
     for step in range(1, nodes):
-        pieces.append(swap(own_rows if step < half_nodes else other_rows, "node", step))
+        pieces.append(swap_nodes(own_rows if step < half_nodes else other_rows, step))
     rows = half_nodes * (locals_ // 2) * capacity
     last = ()
     chains = []
@@ -405,23 +412,24 @@
         bit *= 2
 
     mine = []
-    back = []
+    theirs = ()
     slots_back = []
     for index, (part, other, gate_rows) in enumerate(chains):
-        dealt = [shape((capacity, wide), BF16)] * half_nodes
-        if index == 0:
-            dealt[0] = shape((capacity, wide), F32)
-        own, theirs, *slot_parts = call(
-            functools.partial(slot_kernel, capacity),
-            [shape((2 * rows, hidden), BF16)] * 2
-            + (dealt if locals_ == 2 else [shape((rows, wide), F32)]),
+        dealt = [shape((capacity, wide), BF16 if index else F32)] * half_nodes
+        own, packed, *slot_parts = call(
+            functools.partial(slot_kernel, capacity, len(theirs)),
+            [
+                shape((2 * rows, hidden), BF16),
+                shape(((1 + len(theirs)) * 2 * rows, hidden), BF16),
+                *(dealt if locals_ == 2 else [shape((rows, wide), F32)]),
+            ],
             4 * rows * feats * hidden,
             4 * feats * hidden + 4 * rows * feats,
             after=last,
-        )(part, other, gate_rows, weights, other_weights)
+        )(part, other, gate_rows, weights, other_weights, *theirs)
         last = (own,)
         mine.append(own)
-        back.append(swap(theirs, "local", 1))
+        theirs = (packed,)
         if locals_ > 2:
             half = rows // 2
             keep, send = slot_parts[0][:half], slot_parts[0][half:]
@@ -439,14 +447,15 @@
                 keep, swap(send, "local", bit)
             )
         for step, send in enumerate(slot_parts, index * half_nodes):
-            slots_back.append(swap(send, "node", step) if step else send)
+            slots_back.append(swap_nodes(send, step) if step else send)
     came = [swap(chunk, "local", 1) for chunk in held]
+    back = swap(theirs[0], "local", 1)
     grad_w_in, grad_w_out, written = call(
         functools.partial(weight_kernel, capacity),
         (shape((feats, hidden), F32), shape((hidden, feats), F32), shape((8, LANES), F32)),
         32 * rows * feats * hidden,
         8 * feats * hidden,
-        in_specs=[vmem] * 8,
+        in_specs=[vmem] * 7,
         after=slots_back[1:half_nodes],
         out_specs=[hbm, hbm, vmem],
         scratch_shapes=[
@@ -454,7 +463,7 @@
             pltpu.VMEM((hidden, feats), F32),
             pltpu.SemaphoreType.DMA((2 * PIECES,)),
         ],
-    )(*held, *came, *mine, *back)
+    )(*held, *came, *mine, back)
     grad_tokens, grad_gates = call(
         functools.partial(combine_kernel, nodes),
         (shape((tok_rows, feats), BF16), shape((2, tok_rows), F32)),

time: 29.1 us -> 28.7 us (0.986)
  starting transfers between devices: 17.9 us -> 15.5 us
  waiting for transfers between devices: 3.31 us -> 5.35 us
    ppermute x15 -> x14, starting transfers between devices: 17.9 us -> 15.5 us  [swap(): lax.ppermute(array, axes, [(index, index ^ bit) for index in range(size)])]
    ppermute x15 -> x14, waiting for transfers between devices: 3.31 us -> 5.35 us  [swap(): lax.ppermute(array, axes, [(index, index ^ bit) for index in range(size)])]
  transfers between devices with their start and end apart: 15 -> 14, of which waited for: 6 -> 6; matrix products, arithmetic and copies ran while one was open for 0% -> 0% of each run, Pallas kernels for 14% -> 15%
where the time goes in v1:
time: 28.7 us; the launch traced here: 28.5 us
  starting transfers between devices  15.5 us (54%)
  Pallas kernels  7.01 us (24%)
  waiting for transfers between devices  5.35 us (19%)
  between operations  0.7 us (2%)
    ppermute x14, starting transfers between devices, swap(): lax.ppermute(array, axes, [(index, index ^ bit) for index in range(size)])  15.5 us
    pallas_call x11, Pallas kernels, run(): pl.pallas_call(lambda *refs: kernel(*refs[len(after):]), out_shape=out_sh...  7.01 us
    ppermute x14, waiting for transfers between devices, swap(): lax.ppermute(array, axes, [(index, index ^ bit) for index in range(size)])  5.35 us
  transfers between devices with their start and end apart: 14, of which 6 were waited for; matrix products, arithmetic and copies ran while one was open for 0% of the time, Pallas kernels for 15%

profile of v1, /device:TPU:0, one launch (start us, length us, event | category | flops | bytes accessed | tf_op | source)
XLA Modules:
  0.0 28.5 jit_solution(6057046793503024933)
XLA Ops:
  0.6 1.8 %shard_map.93 = (bf16[16,1152]{1,0:T(8,128)(2,1)S(1)}, bf16[16,1152]{1,0:T(8,128)(2,1)S(1)}, bf16[32,256]{1,0:T(8,128)(2,1)S(1)}, bf16[256,32]{1,0:T(8,128)(2,1)S(1)}, bf16[512,1024]{1,0:T(8,128)(2,1)S(1)}) custom-call(s32[2,256]{1,0:T(2,128)} %bitcast.3, bf16[2,256]{1,0:T(2,128)(2,1)} %bitcast.4, bf16[256,1024]{1,0:T(8,128)(2,1)} %refs_2_.1, ...), custom_call_target="tpu_custom_call" | custom-call | flops 16777216 | bytes 2097152 | tf_op jit(solution)/shard_map/pallas_call | solution.py:38
  2.4 0.5 %collective-permute-start.1 = (bf16[512,1024]{1,0:T(8,128)(2,1)S(1)}, bf16[512,1024]{1,0:T(8,128)(2,1)S(1)}, u32[]{:S(2)}, u32[]{:S(2)}) collective-permute-start(bf16[512,1024]{1,0:T(8,128)(2,1)S(1)} %get-tuple-element.27.refs_1_.refs_2_.refs_4_), channel_id=1, source_target_pairs={{0,4},{4,0},{1,5},{5,1},{2,6},{6,2},{3,7},{7,3},{8,12},{12,8},{9,1... | collective-permute-start | bytes 3145736 | tf_op jit(solution)/shard_map/ppermute | solution.py:321
  2.9 2.6 %collective-permute-start = (bf16[16,1152]{1,0:T(8,128)(2,1)S(1)}, bf16[16,1152]{1,0:T(8,128)(2,1)S(1)}, u32[]{:S(2)}, u32[]{:S(2)}) collective-permute-start(bf16[16,1152]{1,0:T(8,128)(2,1)S(1)} %get-tuple-element.26.refs_0_), channel_id=1, source_target_pairs={{0,12},{4,8},{8,4},{12,0},{16,28},{20,24},{24,20},{28,16},{1,13},{... | collective-permute-start | bytes 110600 | tf_op jit(solution)/shard_map/ppermute | solution.py:321
  5.5 1.2 %collective-permute-start.3 = (bf16[16,1152]{1,0:T(8,128)(2,1)S(1)}, bf16[16,1152]{1,0:T(8,128)(2,1)S(1)}, u32[]{:S(2)}, u32[]{:S(2)}) collective-permute-start(bf16[16,1152]{1,0:T(8,128)(2,1)S(1)} %get-tuple-element.29), channel_id=1, source_target_pairs={{0,28},{4,24},{8,20},{12,16},{16,12},{20,8},{24,4},{28,0},{1,29},{... | collective-permute-start | bytes 110600 | tf_op jit(solution)/shard_map/ppermute | solution.py:321
  6.7 0.1 collective-permute-start.2
  6.7 0.5 %collective-permute-done.refs_1_ = bf16[16,1152]{1,0:T(8,128)(2,1)S(1)} collective-permute-done((bf16[16,1152]{1,0:T(8,128)(2,1)S(1)}, bf16[16,1152]{1,0:T(8,128)(2,1)S(1)}, u32[]{:S(2)}, u32[]{:S(2)}) %collective-permute-start) | collective-permute-done | bytes 36896 | tf_op jit(solution)/shard_map/ppermute | solution.py:321
  7.3 0.0 collective-permute-done.1.refs_2_.refs_3_.refs_5_
  7.3 0.7 %shard_map.95 = (s16[16,1152]{1,0:T(8,128)(2,1)S(1)}, f32[16,128]{1,0:T(8,128)S(1)}) custom-call(bf16[32,1152]{1,0:T(8,128)(2,1)S(1)} %shard_map.94.refs_0_.refs_1_, bf16[512,1024]{1,0:T(8,128)(2,1)S(1)} %get-tuple-element.27.refs_1_.refs_2_.refs_4_, bf16[512,1024]{1,0:T(8,128)(2,1)S(1)} %collective-permute-done.1.refs_2_.refs_3_.refs_5_), custom_call_target="tpu_custom_call" | custom-call | flops 67108864 | bytes 2162688 | tf_op jit(solution)/shard_map/pallas_call | solution.py:38
  8.0 1.7 %collective-permute-start.4 = (s16[16,1152]{1,0:T(8,128)(2,1)S(1)}, s16[16,1152]{1,0:T(8,128)(2,1)S(1)}, u32[]{:S(2)}, u32[]{:S(2)}) collective-permute-start(s16[16,1152]{1,0:T(8,128)(2,1)S(1)} %get-tuple-element.28.refs_0_.refs_1_), channel_id=1, source_target_pairs={{0,1},{1,0},{2,3},{3,2},{4,5},{5,4},{6,7},{7,6},{8,9},{9,8},{10,11... | collective-permute-start | bytes 110600 | tf_op jit(solution)/shard_map/ppermute | solution.py:321
  9.7 0.3 collective-permute-done.3.refs_2_
  10.0 0.9 %collective-permute-done.2.refs_1_ = bf16[16,1152]{1,0:T(8,128)(2,1)S(1)} collective-permute-done((bf16[16,1152]{1,0:T(8,128)(2,1)S(1)}, bf16[16,1152]{1,0:T(8,128)(2,1)S(1)}, u32[]{:S(2)}, u32[]{:S(2)}) %collective-permute-start.2) | collective-permute-done | bytes 36896 | tf_op jit(solution)/shard_map/ppermute | solution.py:321
  10.9 0.7 %shard_map.97 = (s16[16,1152]{1,0:T(8,128)(2,1)S(1)}, f32[16,128]{1,0:T(8,128)S(1)}) custom-call(s16[16,1152]{1,0:T(8,128)(2,1)S(1)} %get-tuple-element.28.refs_0_.refs_1_, bf16[32,1152]{1,0:T(8,128)(2,1)S(1)} %shard_map.96.refs_1_.refs_2_, bf16[512,1024]{1,0:T(8,128)(2,1)S(1)} %get-tuple-element.27.refs_1_.refs_2_.refs_4_, ...), custom_call_target="tpu_custom_call" | custom-call | flops 67108864 | bytes 2162688 | tf_op jit(solution)/shard_map/pallas_call | solution.py:38
  11.6 1.6 %collective-permute-start.5 = (s16[16,1152]{1,0:T(8,128)(2,1)S(1)}, s16[16,1152]{1,0:T(8,128)(2,1)S(1)}, u32[]{:S(2)}, u32[]{:S(2)}) collective-permute-start(s16[16,1152]{1,0:T(8,128)(2,1)S(1)} %get-tuple-element.30.refs_0_.refs_1_), channel_id=1, source_target_pairs={{0,1},{1,0},{2,3},{3,2},{4,5},{5,4},{6,7},{7,6},{8,9},{9,8},{10,11... | collective-permute-start | bytes 110600 | tf_op jit(solution)/shard_map/ppermute | solution.py:321
  13.2 0.0 collective-permute-start.8
  13.2 0.0 collective-permute-done.4.refs_2_
  13.2 0.2 shard_map.98.refs_0_.refs_1_
  13.4 2.7 %collective-permute-start.6 = (s16[16,1152]{1,0:T(8,128)(2,1)S(1)}, s16[16,1152]{1,0:T(8,128)(2,1)S(1)}, u32[]{:S(2)}, u32[]{:S(2)}) collective-permute-start(s16[16,1152]{1,0:T(8,128)(2,1)S(1)} %shard_map.98.refs_0_.refs_1_), channel_id=1, source_target_pairs={{0,2},{1,3},{2,0},{3,1},{4,6},{5,7},{6,4},{7,5},{8,10},{9,11},{10,... | collective-permute-start | bytes 110600 | tf_op jit(solution)/shard_map/ppermute | solution.py:321
  16.1 0.2 collective-permute-start.9
  16.3 0.0 collective-permute-done.5.refs_2_
  16.3 0.2 shard_map.99.refs_0_.refs_1_
  16.5 2.2 %collective-permute-start.10 = (s16[16,1152]{1,0:T(8,128)(2,1)S(1)}, s16[16,1152]{1,0:T(8,128)(2,1)S(1)}, u32[]{:S(2)}, u32[]{:S(2)}) collective-permute-start(s16[16,1152]{1,0:T(8,128)(2,1)S(1)} %shard_map.99.refs_0_.refs_1_), channel_id=1, source_target_pairs={{0,2},{1,3},{2,0},{3,1},{4,6},{5,7},{6,4},{7,5},{8,10},{9,11},{10,... | collective-permute-start | bytes 110600 | tf_op jit(solution)/shard_map/ppermute | solution.py:321
  18.7 0.3 %collective-permute-done.6.refs_2_ = s16[16,1152]{1,0:T(8,128)(2,1)S(1)} collective-permute-done((s16[16,1152]{1,0:T(8,128)(2,1)S(1)}, s16[16,1152]{1,0:T(8,128)(2,1)S(1)}, u32[]{:S(2)}, u32[]{:S(2)}) %collective-permute-start.6) | collective-permute-done | bytes 36896 | tf_op jit(solution)/shard_map/ppermute | solution.py:321
  19.0 0.4 %shard_map.100 = (bf16[32,256]{1,0:T(8,128)(2,1)S(1)}, bf16[32,256]{1,0:T(8,128)(2,1)S(1)}, f32[8,1152]{1,0:T(8,128)S(1)}, f32[8,1152]{1,0:T(8,128)S(1)}) custom-call(s16[16,1152]{1,0:T(8,128)(2,1)S(1)} %shard_map.99.refs_0_.refs_1_, s16[16,1152]{1,0:T(8,128)(2,1)S(1)} %shard_map.98.refs_0_.refs_1_, s16[16,1152]{1,0:T(8,128)(2,1)S(1)} %collective-permute-done.6.refs_2_, ...), custom_call_target="tpu_custom_call" | custom-call | flops 16777216 | bytes 1114112 | tf_op jit(solution)/shard_map/pallas_call | solution.py:38
  19.4 0.0 collective-permute-start.7
  19.4 2.0 %collective-permute-done.10.refs_2_ = s16[16,1152]{1,0:T(8,128)(2,1)S(1)} collective-permute-done((s16[16,1152]{1,0:T(8,128)(2,1)S(1)}, s16[16,1152]{1,0:T(8,128)(2,1)S(1)}, u32[]{:S(2)}, u32[]{:S(2)}) %collective-permute-start.10) | collective-permute-done | bytes 36896 | tf_op jit(solution)/shard_map/ppermute | solution.py:321
  21.4 0.4 %shard_map.101 = (bf16[32,256]{1,0:T(8,128)(2,1)S(1)}, bf16[64,256]{1,0:T(8,128)(2,1)S(1)}, bf16[8,1152]{1,0:T(8,128)(2,1)S(1)}, bf16[8,1152]{1,0:T(8,128)(2,1)S(1)}) custom-call(bf16[32,256]{1,0:T(8,128)(2,1)S(1)} %get-tuple-element.33.refs_0_.refs_5_, s16[16,1152]{1,0:T(8,128)(2,1)S(1)} %shard_map.99.refs_0_.refs_1_, ...), custom_call_target="tpu_custom_call" | custom-call | flops 16777216 | bytes 1114112 | tf_op jit(solution)/shard_map/pallas_call | solution.py:38
  21.8 0.0 collective-permute-start.11
  21.8 2.4 %collective-permute-start.12 = (bf16[8,1152]{1,0:T(8,128)(2,1)S(1)}, bf16[8,1152]{1,0:T(8,128)(2,1)S(1)}, u32[]{:S(2)}, u32[]{:S(2)}) collective-permute-start(bf16[8,1152]{1,0:T(8,128)(2,1)S(1)} %get-tuple-element.40), channel_id=1, source_target_pairs={{0,28},{4,24},{8,20},{12,16},{16,12},{20,8},{24,4},{28,0},{1,29},{... | collective-permute-start | bytes 55304 | tf_op jit(solution)/shard_map/ppermute | solution.py:321
  24.3 0.0 collective-permute-done.8.refs_3_
  24.3 0.2 collective-permute-start.13
  24.5 0.0 collective-permute-done.9.refs_4_
  24.5 0.0 collective-permute-done.11.refs_7_
  24.5 0.0 collective-permute-done.7.refs_0_.refs_2_
  24.5 1.6 %shard_map.102 = (f32[1024,256]{1,0:T(8,128)}, f32[256,1024]{1,0:T(8,128)}, f32[8,128]{1,0:T(8,128)S(1)}) custom-call(f32[8,1152]{1,0:T(8,128)S(1)} %collective-permute-done.7.refs_0_.refs_2_, bf16[32,1152]{1,0:T(8,128)(2,1)S(1)} %shard_map.94.refs_0_.refs_1_, bf16[32,1152]{1,0:T(8,128)(2,1)S(1)} %shard_map.96.refs_1_.refs_2_, ...), custom_call_target="tpu_custom_call" | custom-call | flops 134217728 | bytes 2097152 | tf_op jit(solution)/shard_map/pallas_call | solution.py:38
  26.2 0.0 collective-permute-done.12.refs_3_
  26.2 1.3 %collective-permute-done.13.refs_4_ = bf16[8,1152]{1,0:T(8,128)(2,1)S(1)} collective-permute-done((bf16[8,1152]{1,0:T(8,128)(2,1)S(1)}, bf16[8,1152]{1,0:T(8,128)(2,1)S(1)}, u32[]{:S(2)}, u32[]{:S(2)}) %collective-permute-start.13) | collective-permute-done | bytes 18464 | tf_op jit(solution)/shard_map/ppermute | solution.py:321
  27.5 1.1 %shard_map.103 = (bf16[256,1024]{1,0:T(8,128)(2,1)}, f32[2,256]{1,0:T(2,128)}) custom-call(f32[8,128]{1,0:T(8,128)S(1)} %get-tuple-element.38.refs_0_, f32[8,1152]{1,0:T(8,128)S(1)} %get-tuple-element.39.refs_1_, f32[8,1152]{1,0:T(8,128)S(1)} %collective-permute-done.7.refs_0_.refs_2_, bf16[8,1152]{1,0:T(8,128)(2,1)S(1)} %collective-permute-done.12.refs_3_, ...), custom_call_target="tpu_custom_call" | custom-call | flops 16777216 | bytes 524288 | tf_op jit(solution)/shard_map/pallas_call | solution.py:38
  (2 shorter events, 0.0 us)
Async XLA Ops:
  2.4 4.9 %collective-permute-start.1 = (bf16[512,1024]{1,0:T(8,128)(2,1)S(1)}, bf16[512,1024]{1,0:T(8,128)(2,1)S(1)}, u32[]{:S(2)}, u32[]{:S(2)}) collective-permute-start(bf16[512,1024]{1,0:T(8,128)(2,1)S(1)} %get-tuple-element.27.refs_1_.refs_2_.refs_4_), channel_id=1, source_target_pairs={{0,4},{4,0},{1,5},{5,1},{2,6},{6,2},{3,7},{7,3},{8,12},{12,8},{9,1... | collective-permute-start | bytes 3145736 | tf_op jit(solution)/shard_map/ppermute | solution.py:321
  2.9 4.4 %collective-permute-start = (bf16[16,1152]{1,0:T(8,128)(2,1)S(1)}, bf16[16,1152]{1,0:T(8,128)(2,1)S(1)}, u32[]{:S(2)}, u32[]{:S(2)}) collective-permute-start(bf16[16,1152]{1,0:T(8,128)(2,1)S(1)} %get-tuple-element.26.refs_0_), channel_id=1, source_target_pairs={{0,12},{4,8},{8,4},{12,0},{16,28},{20,24},{24,20},{28,16},{1,13},{... | collective-permute-start | bytes 110600 | tf_op jit(solution)/shard_map/ppermute | solution.py:321
  5.5 4.5 %collective-permute-start.3 = (bf16[16,1152]{1,0:T(8,128)(2,1)S(1)}, bf16[16,1152]{1,0:T(8,128)(2,1)S(1)}, u32[]{:S(2)}, u32[]{:S(2)}) collective-permute-start(bf16[16,1152]{1,0:T(8,128)(2,1)S(1)} %get-tuple-element.29), channel_id=1, source_target_pairs={{0,28},{4,24},{8,20},{12,16},{16,12},{20,8},{24,4},{28,0},{1,29},{... | collective-permute-start | bytes 110600 | tf_op jit(solution)/shard_map/ppermute | solution.py:321
  6.7 4.2 %collective-permute-start.2 = (bf16[16,1152]{1,0:T(8,128)(2,1)S(1)}, bf16[16,1152]{1,0:T(8,128)(2,1)S(1)}, u32[]{:S(2)}, u32[]{:S(2)}) collective-permute-start(bf16[16,1152]{1,0:T(8,128)(2,1)S(1)} %get-tuple-element.29), channel_id=1, source_target_pairs={{0,20},{4,16},{8,28},{12,24},{16,4},{20,0},{24,12},{28,8},{1,21},{... | collective-permute-start | bytes 110600 | tf_op jit(solution)/shard_map/ppermute | solution.py:321
  8.0 5.3 %collective-permute-start.4 = (s16[16,1152]{1,0:T(8,128)(2,1)S(1)}, s16[16,1152]{1,0:T(8,128)(2,1)S(1)}, u32[]{:S(2)}, u32[]{:S(2)}) collective-permute-start(s16[16,1152]{1,0:T(8,128)(2,1)S(1)} %get-tuple-element.28.refs_0_.refs_1_), channel_id=1, source_target_pairs={{0,1},{1,0},{2,3},{3,2},{4,5},{5,4},{6,7},{7,6},{8,9},{9,8},{10,11... | collective-permute-start | bytes 110600 | tf_op jit(solution)/shard_map/ppermute | solution.py:321
  11.6 4.7 %collective-permute-start.5 = (s16[16,1152]{1,0:T(8,128)(2,1)S(1)}, s16[16,1152]{1,0:T(8,128)(2,1)S(1)}, u32[]{:S(2)}, u32[]{:S(2)}) collective-permute-start(s16[16,1152]{1,0:T(8,128)(2,1)S(1)} %get-tuple-element.30.refs_0_.refs_1_), channel_id=1, source_target_pairs={{0,1},{1,0},{2,3},{3,2},{4,5},{5,4},{6,7},{7,6},{8,9},{9,8},{10,11... | collective-permute-start | bytes 110600 | tf_op jit(solution)/shard_map/ppermute | solution.py:321
  13.2 11.1 %collective-permute-start.8 = (bf16[32,1152]{1,0:T(8,128)(2,1)S(1)}, bf16[32,1152]{1,0:T(8,128)(2,1)S(1)}, u32[]{:S(2)}, u32[]{:S(2)}) collective-permute-start(bf16[32,1152]{1,0:T(8,128)(2,1)S(1)} %shard_map.94.refs_0_.refs_1_), channel_id=1, source_target_pairs={{0,4},{4,0},{1,5},{5,1},{2,6},{6,2},{3,7},{7,3},{8,12},{12,8},{9,1... | collective-permute-start | bytes 221192 | tf_op jit(solution)/shard_map/ppermute | solution.py:321
  13.4 5.6 %collective-permute-start.6 = (s16[16,1152]{1,0:T(8,128)(2,1)S(1)}, s16[16,1152]{1,0:T(8,128)(2,1)S(1)}, u32[]{:S(2)}, u32[]{:S(2)}) collective-permute-start(s16[16,1152]{1,0:T(8,128)(2,1)S(1)} %shard_map.98.refs_0_.refs_1_), channel_id=1, source_target_pairs={{0,2},{1,3},{2,0},{3,1},{4,6},{5,7},{6,4},{7,5},{8,10},{9,11},{10,... | collective-permute-start | bytes 110600 | tf_op jit(solution)/shard_map/ppermute | solution.py:321
  16.1 8.4 %collective-permute-start.9 = (bf16[32,1152]{1,0:T(8,128)(2,1)S(1)}, bf16[32,1152]{1,0:T(8,128)(2,1)S(1)}, u32[]{:S(2)}, u32[]{:S(2)}) collective-permute-start(bf16[32,1152]{1,0:T(8,128)(2,1)S(1)} %shard_map.96.refs_1_.refs_2_), channel_id=1, source_target_pairs={{0,4},{4,0},{1,5},{5,1},{2,6},{6,2},{3,7},{7,3},{8,12},{12,8},{9,1... | collective-permute-start | bytes 221192 | tf_op jit(solution)/shard_map/ppermute | solution.py:321
  16.5 4.9 %collective-permute-start.10 = (s16[16,1152]{1,0:T(8,128)(2,1)S(1)}, s16[16,1152]{1,0:T(8,128)(2,1)S(1)}, u32[]{:S(2)}, u32[]{:S(2)}) collective-permute-start(s16[16,1152]{1,0:T(8,128)(2,1)S(1)} %shard_map.99.refs_0_.refs_1_), channel_id=1, source_target_pairs={{0,2},{1,3},{2,0},{3,1},{4,6},{5,7},{6,4},{7,5},{8,10},{9,11},{10,... | collective-permute-start | bytes 110600 | tf_op jit(solution)/shard_map/ppermute | solution.py:321
  19.4 5.1 %collective-permute-start.7 = (f32[8,1152]{1,0:T(8,128)S(1)}, f32[8,1152]{1,0:T(8,128)S(1)}, u32[]{:S(2)}, u32[]{:S(2)}) collective-permute-start(f32[8,1152]{1,0:T(8,128)S(1)} %get-tuple-element.32), channel_id=1, source_target_pairs={{0,12},{4,8},{8,4},{12,0},{16,28},{20,24},{24,20},{28,16},{1,13},{... | collective-permute-start | bytes 110600 | tf_op jit(solution)/shard_map/ppermute | solution.py:321
  21.8 2.7 %collective-permute-start.11 = (bf16[64,256]{1,0:T(8,128)(2,1)S(1)}, bf16[64,256]{1,0:T(8,128)(2,1)S(1)}, u32[]{:S(2)}, u32[]{:S(2)}) collective-permute-start(bf16[64,256]{1,0:T(8,128)(2,1)S(1)} %get-tuple-element.37), channel_id=1, source_target_pairs={{0,4},{4,0},{1,5},{5,1},{2,6},{6,2},{3,7},{7,3},{8,12},{12,8},{9,1... | collective-permute-start | bytes 98312 | tf_op jit(solution)/shard_map/ppermute | solution.py:321
  21.8 4.3 %collective-permute-start.12 = (bf16[8,1152]{1,0:T(8,128)(2,1)S(1)}, bf16[8,1152]{1,0:T(8,128)(2,1)S(1)}, u32[]{:S(2)}, u32[]{:S(2)}) collective-permute-start(bf16[8,1152]{1,0:T(8,128)(2,1)S(1)} %get-tuple-element.40), channel_id=1, source_target_pairs={{0,28},{4,24},{8,20},{12,16},{16,12},{20,8},{24,4},{28,0},{1,29},{... | collective-permute-start | bytes 55304 | tf_op jit(solution)/shard_map/ppermute | solution.py:321
  24.3 3.2 %collective-permute-start.13 = (bf16[8,1152]{1,0:T(8,128)(2,1)S(1)}, bf16[8,1152]{1,0:T(8,128)(2,1)S(1)}, u32[]{:S(2)}, u32[]{:S(2)}) collective-permute-start(bf16[8,1152]{1,0:T(8,128)(2,1)S(1)} %get-tuple-element.41), channel_id=1, source_target_pairs={{0,20},{4,16},{8,28},{12,24},{16,4},{20,0},{24,12},{28,8},{1,21},{... | collective-permute-start | bytes 55304 | tf_op jit(solution)/shard_map/ppermute | solution.py:321

commit v2 on v1

--- a/solution.py
+++ b/solution.py
@@ -396,9 +396,9 @@
             after=last,
         )(chunk, weights, other_weights)
         last = (part,)
-        chains.append((part, swap(part, "edata", 1), gate_rows))
-    bit = 2
-    while bit < edatas:
+        chains.append((part, swap(part, "edata", edatas // 2), gate_rows))
+    bit = edatas // 4
+    while bit:
         for index, (part, other, gate_rows) in enumerate(chains):
             part = call(
                 add_codes_kernel,
@@ -409,7 +409,7 @@
             )(part, other)
             last = (part,)
             chains[index] = (part, swap(part, "edata", bit), gate_rows)
-        bit *= 2
+        bit //= 2
 
     mine = []
     theirs = ()

time: 28.7 us -> 28 us (0.976)
  waiting for transfers between devices: 5.35 us -> 4.69 us
    ppermute x14, waiting for transfers between devices: 5.35 us -> 4.69 us  [swap(): lax.ppermute(array, axes, [(index, index ^ bit) for index in range(size)])]
where the time goes in v2:
time: 28 us; the launch traced here: 27.8 us
  starting transfers between devices  15.4 us (55%)
  Pallas kernels  7.01 us (25%)
  waiting for transfers between devices  4.69 us (17%)
  between operations  0.7 us (2%)
    ppermute x14, starting transfers between devices, swap(): lax.ppermute(array, axes, [(index, index ^ bit) for index in range(size)])  15.4 us
    pallas_call x11, Pallas kernels, run(): pl.pallas_call(lambda *refs: kernel(*refs[len(after):]), out_shape=out_sh...  7.01 us
    ppermute x14, waiting for transfers between devices, swap(): lax.ppermute(array, axes, [(index, index ^ bit) for index in range(size)])  4.69 us
  transfers between devices with their start and end apart: 14, of which 6 were waited for; matrix products, arithmetic and copies ran while one was open for 0% of the time, Pallas kernels for 15%

profile of v2, /device:TPU:0, one launch (start us, length us, event | category | flops | bytes accessed | tf_op | source)
XLA Modules:
  0.0 27.8 jit_solution(8080083724878637839)
XLA Ops:
  0.6 1.8 %shard_map.93 = (bf16[16,1152]{1,0:T(8,128)(2,1)S(1)}, bf16[16,1152]{1,0:T(8,128)(2,1)S(1)}, bf16[32,256]{1,0:T(8,128)(2,1)S(1)}, bf16[256,32]{1,0:T(8,128)(2,1)S(1)}, bf16[512,1024]{1,0:T(8,128)(2,1)S(1)}) custom-call(s32[2,256]{1,0:T(2,128)} %bitcast.3, bf16[2,256]{1,0:T(2,128)(2,1)} %bitcast.4, bf16[256,1024]{1,0:T(8,128)(2,1)} %refs_2_.1, ...), custom_call_target="tpu_custom_call" | custom-call | flops 16777216 | bytes 2097152 | tf_op jit(solution)/shard_map/pallas_call | solution.py:38
  2.4 0.5 %collective-permute-start.1 = (bf16[512,1024]{1,0:T(8,128)(2,1)S(1)}, bf16[512,1024]{1,0:T(8,128)(2,1)S(1)}, u32[]{:S(2)}, u32[]{:S(2)}) collective-permute-start(bf16[512,1024]{1,0:T(8,128)(2,1)S(1)} %get-tuple-element.27.refs_1_.refs_2_.refs_4_), channel_id=1, source_target_pairs={{0,4},{4,0},{1,5},{5,1},{2,6},{6,2},{3,7},{7,3},{8,12},{12,8},{9,1... | collective-permute-start | bytes 3145736 | tf_op jit(solution)/shard_map/ppermute | solution.py:321
  2.9 2.6 %collective-permute-start = (bf16[16,1152]{1,0:T(8,128)(2,1)S(1)}, bf16[16,1152]{1,0:T(8,128)(2,1)S(1)}, u32[]{:S(2)}, u32[]{:S(2)}) collective-permute-start(bf16[16,1152]{1,0:T(8,128)(2,1)S(1)} %get-tuple-element.26.refs_0_), channel_id=1, source_target_pairs={{0,12},{4,8},{8,4},{12,0},{16,28},{20,24},{24,20},{28,16},{1,13},{... | collective-permute-start | bytes 110600 | tf_op jit(solution)/shard_map/ppermute | solution.py:321
  5.5 1.2 %collective-permute-start.3 = (bf16[16,1152]{1,0:T(8,128)(2,1)S(1)}, bf16[16,1152]{1,0:T(8,128)(2,1)S(1)}, u32[]{:S(2)}, u32[]{:S(2)}) collective-permute-start(bf16[16,1152]{1,0:T(8,128)(2,1)S(1)} %get-tuple-element.29), channel_id=1, source_target_pairs={{0,28},{4,24},{8,20},{12,16},{16,12},{20,8},{24,4},{28,0},{1,29},{... | collective-permute-start | bytes 110600 | tf_op jit(solution)/shard_map/ppermute | solution.py:321
  6.7 0.1 collective-permute-start.2
  6.7 0.5 %collective-permute-done.refs_1_ = bf16[16,1152]{1,0:T(8,128)(2,1)S(1)} collective-permute-done((bf16[16,1152]{1,0:T(8,128)(2,1)S(1)}, bf16[16,1152]{1,0:T(8,128)(2,1)S(1)}, u32[]{:S(2)}, u32[]{:S(2)}) %collective-permute-start) | collective-permute-done | bytes 36896 | tf_op jit(solution)/shard_map/ppermute | solution.py:321
  7.3 0.0 collective-permute-done.1.refs_2_.refs_3_.refs_5_
  7.3 0.7 %shard_map.95 = (s16[16,1152]{1,0:T(8,128)(2,1)S(1)}, f32[16,128]{1,0:T(8,128)S(1)}) custom-call(bf16[32,1152]{1,0:T(8,128)(2,1)S(1)} %shard_map.94.refs_0_.refs_1_, bf16[512,1024]{1,0:T(8,128)(2,1)S(1)} %get-tuple-element.27.refs_1_.refs_2_.refs_4_, bf16[512,1024]{1,0:T(8,128)(2,1)S(1)} %collective-permute-done.1.refs_2_.refs_3_.refs_5_), custom_call_target="tpu_custom_call" | custom-call | flops 67108864 | bytes 2162688 | tf_op jit(solution)/shard_map/pallas_call | solution.py:38
  8.0 2.7 %collective-permute-start.4 = (s16[16,1152]{1,0:T(8,128)(2,1)S(1)}, s16[16,1152]{1,0:T(8,128)(2,1)S(1)}, u32[]{:S(2)}, u32[]{:S(2)}) collective-permute-start(s16[16,1152]{1,0:T(8,128)(2,1)S(1)} %get-tuple-element.28.refs_0_.refs_1_), channel_id=1, source_target_pairs={{0,2},{1,3},{2,0},{3,1},{4,6},{5,7},{6,4},{7,5},{8,10},{9,11},{10,... | collective-permute-start | bytes 110600 | tf_op jit(solution)/shard_map/ppermute | solution.py:321
  10.7 0.0 collective-permute-done.3.refs_2_
  10.7 0.2 collective-permute-done.2.refs_1_
  10.9 0.7 %shard_map.97 = (s16[16,1152]{1,0:T(8,128)(2,1)S(1)}, f32[16,128]{1,0:T(8,128)S(1)}) custom-call(s16[16,1152]{1,0:T(8,128)(2,1)S(1)} %get-tuple-element.28.refs_0_.refs_1_, bf16[32,1152]{1,0:T(8,128)(2,1)S(1)} %shard_map.96.refs_1_.refs_2_, bf16[512,1024]{1,0:T(8,128)(2,1)S(1)} %get-tuple-element.27.refs_1_.refs_2_.refs_4_, ...), custom_call_target="tpu_custom_call" | custom-call | flops 67108864 | bytes 2162688 | tf_op jit(solution)/shard_map/pallas_call | solution.py:38
  11.6 2.7 %collective-permute-start.5 = (s16[16,1152]{1,0:T(8,128)(2,1)S(1)}, s16[16,1152]{1,0:T(8,128)(2,1)S(1)}, u32[]{:S(2)}, u32[]{:S(2)}) collective-permute-start(s16[16,1152]{1,0:T(8,128)(2,1)S(1)} %get-tuple-element.30.refs_0_.refs_1_), channel_id=1, source_target_pairs={{0,2},{1,3},{2,0},{3,1},{4,6},{5,7},{6,4},{7,5},{8,10},{9,11},{10,... | collective-permute-start | bytes 110600 | tf_op jit(solution)/shard_map/ppermute | solution.py:321
  14.2 0.0 collective-permute-start.8
  14.2 0.0 collective-permute-done.4.refs_2_
  14.2 0.2 shard_map.98.refs_0_.refs_1_
  14.4 1.6 %collective-permute-start.6 = (s16[16,1152]{1,0:T(8,128)(2,1)S(1)}, s16[16,1152]{1,0:T(8,128)(2,1)S(1)}, u32[]{:S(2)}, u32[]{:S(2)}) collective-permute-start(s16[16,1152]{1,0:T(8,128)(2,1)S(1)} %shard_map.98.refs_0_.refs_1_), channel_id=1, source_target_pairs={{0,1},{1,0},{2,3},{3,2},{4,5},{5,4},{6,7},{7,6},{8,9},{9,8},{10,11... | collective-permute-start | bytes 110600 | tf_op jit(solution)/shard_map/ppermute | solution.py:321
  16.1 0.2 collective-permute-start.9
  16.3 0.6 %collective-permute-done.5.refs_2_ = s16[16,1152]{1,0:T(8,128)(2,1)S(1)} collective-permute-done((s16[16,1152]{1,0:T(8,128)(2,1)S(1)}, s16[16,1152]{1,0:T(8,128)(2,1)S(1)}, u32[]{:S(2)}, u32[]{:S(2)}) %collective-permute-start.5) | collective-permute-done | bytes 36896 | tf_op jit(solution)/shard_map/ppermute | solution.py:321
  16.9 0.2 shard_map.99.refs_0_.refs_1_
  17.1 1.2 %collective-permute-start.10 = (s16[16,1152]{1,0:T(8,128)(2,1)S(1)}, s16[16,1152]{1,0:T(8,128)(2,1)S(1)}, u32[]{:S(2)}, u32[]{:S(2)}) collective-permute-start(s16[16,1152]{1,0:T(8,128)(2,1)S(1)} %shard_map.99.refs_0_.refs_1_), channel_id=1, source_target_pairs={{0,1},{1,0},{2,3},{3,2},{4,5},{5,4},{6,7},{7,6},{8,9},{9,8},{10,11... | collective-permute-start | bytes 110600 | tf_op jit(solution)/shard_map/ppermute | solution.py:321
  18.3 0.1 collective-permute-done.6.refs_2_
  18.5 0.4 %shard_map.100 = (bf16[32,256]{1,0:T(8,128)(2,1)S(1)}, bf16[32,256]{1,0:T(8,128)(2,1)S(1)}, f32[8,1152]{1,0:T(8,128)S(1)}, f32[8,1152]{1,0:T(8,128)S(1)}) custom-call(s16[16,1152]{1,0:T(8,128)(2,1)S(1)} %shard_map.99.refs_0_.refs_1_, s16[16,1152]{1,0:T(8,128)(2,1)S(1)} %shard_map.98.refs_0_.refs_1_, s16[16,1152]{1,0:T(8,128)(2,1)S(1)} %collective-permute-done.6.refs_2_, ...), custom_call_target="tpu_custom_call" | custom-call | flops 16777216 | bytes 1114112 | tf_op jit(solution)/shard_map/pallas_call | solution.py:38
  18.9 0.0 collective-permute-start.7
  18.9 2.2 %collective-permute-done.10.refs_2_ = s16[16,1152]{1,0:T(8,128)(2,1)S(1)} collective-permute-done((s16[16,1152]{1,0:T(8,128)(2,1)S(1)}, s16[16,1152]{1,0:T(8,128)(2,1)S(1)}, u32[]{:S(2)}, u32[]{:S(2)}) %collective-permute-start.10) | collective-permute-done | bytes 36896 | tf_op jit(solution)/shard_map/ppermute | solution.py:321
  21.1 0.4 %shard_map.101 = (bf16[32,256]{1,0:T(8,128)(2,1)S(1)}, bf16[64,256]{1,0:T(8,128)(2,1)S(1)}, bf16[8,1152]{1,0:T(8,128)(2,1)S(1)}, bf16[8,1152]{1,0:T(8,128)(2,1)S(1)}) custom-call(bf16[32,256]{1,0:T(8,128)(2,1)S(1)} %get-tuple-element.33.refs_0_.refs_5_, s16[16,1152]{1,0:T(8,128)(2,1)S(1)} %shard_map.99.refs_0_.refs_1_, ...), custom_call_target="tpu_custom_call" | custom-call | flops 16777216 | bytes 1114112 | tf_op jit(solution)/shard_map/pallas_call | solution.py:38
  21.5 0.0 collective-permute-start.11
  21.5 2.0 %collective-permute-start.12 = (bf16[8,1152]{1,0:T(8,128)(2,1)S(1)}, bf16[8,1152]{1,0:T(8,128)(2,1)S(1)}, u32[]{:S(2)}, u32[]{:S(2)}) collective-permute-start(bf16[8,1152]{1,0:T(8,128)(2,1)S(1)} %get-tuple-element.40), channel_id=1, source_target_pairs={{0,28},{4,24},{8,20},{12,16},{16,12},{20,8},{24,4},{28,0},{1,29},{... | collective-permute-start | bytes 55304 | tf_op jit(solution)/shard_map/ppermute | solution.py:321
  23.5 0.0 collective-permute-done.8.refs_3_
  23.5 0.5 %collective-permute-start.13 = (bf16[8,1152]{1,0:T(8,128)(2,1)S(1)}, bf16[8,1152]{1,0:T(8,128)(2,1)S(1)}, u32[]{:S(2)}, u32[]{:S(2)}) collective-permute-start(bf16[8,1152]{1,0:T(8,128)(2,1)S(1)} %get-tuple-element.41), channel_id=1, source_target_pairs={{0,20},{4,16},{8,28},{12,24},{16,4},{20,0},{24,12},{28,8},{1,21},{... | collective-permute-start | bytes 55304 | tf_op jit(solution)/shard_map/ppermute | solution.py:321
  24.1 0.0 collective-permute-done.9.refs_4_
  24.1 0.0 collective-permute-done.11.refs_7_
  24.1 0.0 collective-permute-done.7.refs_0_.refs_2_
  24.1 1.6 %shard_map.102 = (f32[1024,256]{1,0:T(8,128)}, f32[256,1024]{1,0:T(8,128)}, f32[8,128]{1,0:T(8,128)S(1)}) custom-call(f32[8,1152]{1,0:T(8,128)S(1)} %collective-permute-done.7.refs_0_.refs_2_, bf16[32,1152]{1,0:T(8,128)(2,1)S(1)} %shard_map.94.refs_0_.refs_1_, bf16[32,1152]{1,0:T(8,128)(2,1)S(1)} %shard_map.96.refs_1_.refs_2_, ...), custom_call_target="tpu_custom_call" | custom-call | flops 134217728 | bytes 2097152 | tf_op jit(solution)/shard_map/pallas_call | solution.py:38
  25.7 0.0 collective-permute-done.12.refs_3_
  25.7 1.0 %collective-permute-done.13.refs_4_ = bf16[8,1152]{1,0:T(8,128)(2,1)S(1)} collective-permute-done((bf16[8,1152]{1,0:T(8,128)(2,1)S(1)}, bf16[8,1152]{1,0:T(8,128)(2,1)S(1)}, u32[]{:S(2)}, u32[]{:S(2)}) %collective-permute-start.13) | collective-permute-done | bytes 18464 | tf_op jit(solution)/shard_map/ppermute | solution.py:321
  26.7 1.1 %shard_map.103 = (bf16[256,1024]{1,0:T(8,128)(2,1)}, f32[2,256]{1,0:T(2,128)}) custom-call(f32[8,128]{1,0:T(8,128)S(1)} %get-tuple-element.38.refs_0_, f32[8,1152]{1,0:T(8,128)S(1)} %get-tuple-element.39.refs_1_, f32[8,1152]{1,0:T(8,128)S(1)} %collective-permute-done.7.refs_0_.refs_2_, bf16[8,1152]{1,0:T(8,128)(2,1)S(1)} %collective-permute-done.12.refs_3_, ...), custom_call_target="tpu_custom_call" | custom-call | flops 16777216 | bytes 524288 | tf_op jit(solution)/shard_map/pallas_call | solution.py:38
  (2 shorter events, 0.0 us)
Async XLA Ops:
  2.4 4.9 %collective-permute-start.1 = (bf16[512,1024]{1,0:T(8,128)(2,1)S(1)}, bf16[512,1024]{1,0:T(8,128)(2,1)S(1)}, u32[]{:S(2)}, u32[]{:S(2)}) collective-permute-start(bf16[512,1024]{1,0:T(8,128)(2,1)S(1)} %get-tuple-element.27.refs_1_.refs_2_.refs_4_), channel_id=1, source_target_pairs={{0,4},{4,0},{1,5},{5,1},{2,6},{6,2},{3,7},{7,3},{8,12},{12,8},{9,1... | collective-permute-start | bytes 3145736 | tf_op jit(solution)/shard_map/ppermute | solution.py:321
  2.9 4.4 %collective-permute-start = (bf16[16,1152]{1,0:T(8,128)(2,1)S(1)}, bf16[16,1152]{1,0:T(8,128)(2,1)S(1)}, u32[]{:S(2)}, u32[]{:S(2)}) collective-permute-start(bf16[16,1152]{1,0:T(8,128)(2,1)S(1)} %get-tuple-element.26.refs_0_), channel_id=1, source_target_pairs={{0,12},{4,8},{8,4},{12,0},{16,28},{20,24},{24,20},{28,16},{1,13},{... | collective-permute-start | bytes 110600 | tf_op jit(solution)/shard_map/ppermute | solution.py:321
  5.5 5.2 %collective-permute-start.3 = (bf16[16,1152]{1,0:T(8,128)(2,1)S(1)}, bf16[16,1152]{1,0:T(8,128)(2,1)S(1)}, u32[]{:S(2)}, u32[]{:S(2)}) collective-permute-start(bf16[16,1152]{1,0:T(8,128)(2,1)S(1)} %get-tuple-element.29), channel_id=1, source_target_pairs={{0,28},{4,24},{8,20},{12,16},{16,12},{20,8},{24,4},{28,0},{1,29},{... | collective-permute-start | bytes 110600 | tf_op jit(solution)/shard_map/ppermute | solution.py:321
  6.7 4.2 %collective-permute-start.2 = (bf16[16,1152]{1,0:T(8,128)(2,1)S(1)}, bf16[16,1152]{1,0:T(8,128)(2,1)S(1)}, u32[]{:S(2)}, u32[]{:S(2)}) collective-permute-start(bf16[16,1152]{1,0:T(8,128)(2,1)S(1)} %get-tuple-element.29), channel_id=1, source_target_pairs={{0,20},{4,16},{8,28},{12,24},{16,4},{20,0},{24,12},{28,8},{1,21},{... | collective-permute-start | bytes 110600 | tf_op jit(solution)/shard_map/ppermute | solution.py:321
  8.0 6.3 %collective-permute-start.4 = (s16[16,1152]{1,0:T(8,128)(2,1)S(1)}, s16[16,1152]{1,0:T(8,128)(2,1)S(1)}, u32[]{:S(2)}, u32[]{:S(2)}) collective-permute-start(s16[16,1152]{1,0:T(8,128)(2,1)S(1)} %get-tuple-element.28.refs_0_.refs_1_), channel_id=1, source_target_pairs={{0,2},{1,3},{2,0},{3,1},{4,6},{5,7},{6,4},{7,5},{8,10},{9,11},{10,... | collective-permute-start | bytes 110600 | tf_op jit(solution)/shard_map/ppermute | solution.py:321
  11.6 5.3 %collective-permute-start.5 = (s16[16,1152]{1,0:T(8,128)(2,1)S(1)}, s16[16,1152]{1,0:T(8,128)(2,1)S(1)}, u32[]{:S(2)}, u32[]{:S(2)}) collective-permute-start(s16[16,1152]{1,0:T(8,128)(2,1)S(1)} %get-tuple-element.30.refs_0_.refs_1_), channel_id=1, source_target_pairs={{0,2},{1,3},{2,0},{3,1},{4,6},{5,7},{6,4},{7,5},{8,10},{9,11},{10,... | collective-permute-start | bytes 110600 | tf_op jit(solution)/shard_map/ppermute | solution.py:321
  14.2 9.3 %collective-permute-start.8 = (bf16[32,1152]{1,0:T(8,128)(2,1)S(1)}, bf16[32,1152]{1,0:T(8,128)(2,1)S(1)}, u32[]{:S(2)}, u32[]{:S(2)}) collective-permute-start(bf16[32,1152]{1,0:T(8,128)(2,1)S(1)} %shard_map.94.refs_0_.refs_1_), channel_id=1, source_target_pairs={{0,4},{4,0},{1,5},{5,1},{2,6},{6,2},{3,7},{7,3},{8,12},{12,8},{9,1... | collective-permute-start | bytes 221192 | tf_op jit(solution)/shard_map/ppermute | solution.py:321
  14.4 4.0 %collective-permute-start.6 = (s16[16,1152]{1,0:T(8,128)(2,1)S(1)}, s16[16,1152]{1,0:T(8,128)(2,1)S(1)}, u32[]{:S(2)}, u32[]{:S(2)}) collective-permute-start(s16[16,1152]{1,0:T(8,128)(2,1)S(1)} %shard_map.98.refs_0_.refs_1_), channel_id=1, source_target_pairs={{0,1},{1,0},{2,3},{3,2},{4,5},{5,4},{6,7},{7,6},{8,9},{9,8},{10,11... | collective-permute-start | bytes 110600 | tf_op jit(solution)/shard_map/ppermute | solution.py:321
  16.1 8.0 %collective-permute-start.9 = (bf16[32,1152]{1,0:T(8,128)(2,1)S(1)}, bf16[32,1152]{1,0:T(8,128)(2,1)S(1)}, u32[]{:S(2)}, u32[]{:S(2)}) collective-permute-start(bf16[32,1152]{1,0:T(8,128)(2,1)S(1)} %shard_map.96.refs_1_.refs_2_), channel_id=1, source_target_pairs={{0,4},{4,0},{1,5},{5,1},{2,6},{6,2},{3,7},{7,3},{8,12},{12,8},{9,1... | collective-permute-start | bytes 221192 | tf_op jit(solution)/shard_map/ppermute | solution.py:321
  17.1 4.0 %collective-permute-start.10 = (s16[16,1152]{1,0:T(8,128)(2,1)S(1)}, s16[16,1152]{1,0:T(8,128)(2,1)S(1)}, u32[]{:S(2)}, u32[]{:S(2)}) collective-permute-start(s16[16,1152]{1,0:T(8,128)(2,1)S(1)} %shard_map.99.refs_0_.refs_1_), channel_id=1, source_target_pairs={{0,1},{1,0},{2,3},{3,2},{4,5},{5,4},{6,7},{7,6},{8,9},{9,8},{10,11... | collective-permute-start | bytes 110600 | tf_op jit(solution)/shard_map/ppermute | solution.py:321
  18.9 5.2 %collective-permute-start.7 = (f32[8,1152]{1,0:T(8,128)S(1)}, f32[8,1152]{1,0:T(8,128)S(1)}, u32[]{:S(2)}, u32[]{:S(2)}) collective-permute-start(f32[8,1152]{1,0:T(8,128)S(1)} %get-tuple-element.32), channel_id=1, source_target_pairs={{0,12},{4,8},{8,4},{12,0},{16,28},{20,24},{24,20},{28,16},{1,13},{... | collective-permute-start | bytes 110600 | tf_op jit(solution)/shard_map/ppermute | solution.py:321
  21.5 2.6 %collective-permute-start.11 = (bf16[64,256]{1,0:T(8,128)(2,1)S(1)}, bf16[64,256]{1,0:T(8,128)(2,1)S(1)}, u32[]{:S(2)}, u32[]{:S(2)}) collective-permute-start(bf16[64,256]{1,0:T(8,128)(2,1)S(1)} %get-tuple-element.37), channel_id=1, source_target_pairs={{0,4},{4,0},{1,5},{5,1},{2,6},{6,2},{3,7},{7,3},{8,12},{12,8},{9,1... | collective-permute-start | bytes 98312 | tf_op jit(solution)/shard_map/ppermute | solution.py:321
  21.5 4.2 %collective-permute-start.12 = (bf16[8,1152]{1,0:T(8,128)(2,1)S(1)}, bf16[8,1152]{1,0:T(8,128)(2,1)S(1)}, u32[]{:S(2)}, u32[]{:S(2)}) collective-permute-start(bf16[8,1152]{1,0:T(8,128)(2,1)S(1)} %get-tuple-element.40), channel_id=1, source_target_pairs={{0,28},{4,24},{8,20},{12,16},{16,12},{20,8},{24,4},{28,0},{1,29},{... | collective-permute-start | bytes 55304 | tf_op jit(solution)/shard_map/ppermute | solution.py:321
  23.5 3.2 %collective-permute-start.13 = (bf16[8,1152]{1,0:T(8,128)(2,1)S(1)}, bf16[8,1152]{1,0:T(8,128)(2,1)S(1)}, u32[]{:S(2)}, u32[]{:S(2)}) collective-permute-start(bf16[8,1152]{1,0:T(8,128)(2,1)S(1)} %get-tuple-element.41), channel_id=1, source_target_pairs={{0,20},{4,16},{8,28},{12,24},{16,4},{20,0},{24,12},{28,8},{1,21},{... | collective-permute-start | bytes 55304 | tf_op jit(solution)/shard_map/ppermute | solution.py:321

commit v3 on v2

--- a/solution.py
+++ b/solution.py
@@ -373,6 +373,9 @@
 
     other_weights = swap(weights, "local", 1)
 
+    quarter = nodes // 4
+    far = [*range(quarter), *range(nodes - quarter, nodes)]
+    near = list(range(quarter, nodes - quarter))
     half_nodes = nodes // WINDOW
     pieces = [own_rows]
     for step in range(1, nodes):
@@ -381,8 +384,8 @@
     last = ()
     chains = []
     held = []
-    for chunk in (pieces[:half_nodes], pieces[half_nodes:]):
-        chunk = join(chunk, last)
+    for steps in (far, near):
+        chunk = join([pieces[step] for step in steps], last)
         bit = 2
         while bit < locals_:
             chunk = join([chunk, swap(chunk, "local", bit)])
@@ -413,7 +416,7 @@
 
     mine = []
     theirs = ()
-    slots_back = []
+    slots_back = {}
     for index, (part, other, gate_rows) in enumerate(chains):
         dealt = [shape((capacity, wide), BF16 if index else F32)] * half_nodes
         own, packed, *slot_parts = call(
@@ -446,8 +449,8 @@
             slot_parts = call(deal_kernel, dealt, 4 * half * wide, 12 * half * wide)(
                 keep, swap(send, "local", bit)
             )
-        for step, send in enumerate(slot_parts, index * half_nodes):
-            slots_back.append(swap_nodes(send, step) if step else send)
+        for step, send in zip(near if index else far, slot_parts):
+            slots_back[step] = swap_nodes(send, step) if step else send
     came = [swap(chunk, "local", 1) for chunk in held]
     back = swap(theirs[0], "local", 1)
     grad_w_in, grad_w_out, written = call(
@@ -456,7 +459,7 @@
         32 * rows * feats * hidden,
         8 * feats * hidden,
         in_specs=[vmem] * 7,
-        after=slots_back[1:half_nodes],
+        after=[slots_back[step] for step in far[1:]],
         out_specs=[hbm, hbm, vmem],
         scratch_shapes=[
             pltpu.VMEM((feats, hidden), F32),
@@ -470,7 +473,7 @@
         4 * slots * tok_rows * feats,
         2 * tok_rows * feats,
         after=(written,),
-    )(*slots_back[:half_nodes], *reversed(slots_back[half_nodes:]), place, spread)
+    )(*[slots_back[step] for step in range(nodes)], place, spread)
     return (grad_tokens, grad_gates.T, grad_w_in, grad_w_out)
 
 

time: 28 us -> 28 us (level)
  waiting for transfers between devices: 4.69 us -> 5.04 us
  starting transfers between devices: 15.4 us -> 15.1 us
    ppermute x14, waiting for transfers between devices: 4.69 us -> 5.04 us  [swap(): lax.ppermute(array, axes, [(index, index ^ bit) for index in range(size)])]
    ppermute x14, starting transfers between devices: 15.4 us -> 15.1 us  [swap(): lax.ppermute(array, axes, [(index, index ^ bit) for index in range(size)])]
  transfers between devices with their start and end apart: 14 -> 14, of which waited for: 6 -> 5; matrix products, arithmetic and copies ran while one was open for 0% -> 0% of each run, Pallas kernels for 15% -> 15%
where the time goes in v3:
time: 28 us; the launch traced here: 27.9 us
  starting transfers between devices  15.1 us (54%)
  Pallas kernels  7.01 us (25%)
  waiting for transfers between devices  5.04 us (18%)
  between operations  0.71 us (3%)
    ppermute x14, starting transfers between devices, swap(): lax.ppermute(array, axes, [(index, index ^ bit) for index in range(size)])  15.1 us
    pallas_call x11, Pallas kernels, run(): pl.pallas_call(lambda *refs: kernel(*refs[len(after):]), out_shape=out_sh...  7.01 us
    ppermute x14, waiting for transfers between devices, swap(): lax.ppermute(array, axes, [(index, index ^ bit) for index in range(size)])  5.04 us
  transfers between devices with their start and end apart: 14, of which 5 were waited for; matrix products, arithmetic and copies ran while one was open for 0% of the time, Pallas kernels for 15%

profile of v3, /device:TPU:0, one launch (start us, length us, event | category | flops | bytes accessed | tf_op | source)
XLA Modules:
  0.0 27.9 jit_solution(9656552423044817362)
XLA Ops:
  0.6 1.8 %shard_map.93 = (bf16[16,1152]{1,0:T(8,128)(2,1)S(1)}, bf16[16,1152]{1,0:T(8,128)(2,1)S(1)}, bf16[32,256]{1,0:T(8,128)(2,1)S(1)}, bf16[256,32]{1,0:T(8,128)(2,1)S(1)}, bf16[512,1024]{1,0:T(8,128)(2,1)S(1)}) custom-call(s32[2,256]{1,0:T(2,128)} %bitcast.3, bf16[2,256]{1,0:T(2,128)(2,1)} %bitcast.4, bf16[256,1024]{1,0:T(8,128)(2,1)} %refs_2_.1, ...), custom_call_target="tpu_custom_call" | custom-call | flops 16777216 | bytes 2097152 | tf_op jit(solution)/shard_map/pallas_call | solution.py:38
  2.4 0.5 %collective-permute-start.1 = (bf16[512,1024]{1,0:T(8,128)(2,1)S(1)}, bf16[512,1024]{1,0:T(8,128)(2,1)S(1)}, u32[]{:S(2)}, u32[]{:S(2)}) collective-permute-start(bf16[512,1024]{1,0:T(8,128)(2,1)S(1)} %get-tuple-element.28.refs_1_.refs_2_.refs_4_), channel_id=1, source_target_pairs={{0,4},{4,0},{1,5},{5,1},{2,6},{6,2},{3,7},{7,3},{8,12},{12,8},{9,1... | collective-permute-start | bytes 3145736 | tf_op jit(solution)/shard_map/ppermute | solution.py:321
  2.9 3.6 %collective-permute-start = (bf16[16,1152]{1,0:T(8,128)(2,1)S(1)}, bf16[16,1152]{1,0:T(8,128)(2,1)S(1)}, u32[]{:S(2)}, u32[]{:S(2)}) collective-permute-start(bf16[16,1152]{1,0:T(8,128)(2,1)S(1)} %get-tuple-element.27), channel_id=1, source_target_pairs={{0,28},{4,24},{8,20},{12,16},{16,12},{20,8},{24,4},{28,0},{1,29},{... | collective-permute-start | bytes 110600 | tf_op jit(solution)/shard_map/ppermute | solution.py:321
  6.5 0.2 collective-permute-start.2
  6.7 0.1 collective-permute-start.3
  6.8 1.5 %collective-permute-done.refs_1_ = bf16[16,1152]{1,0:T(8,128)(2,1)S(1)} collective-permute-done((bf16[16,1152]{1,0:T(8,128)(2,1)S(1)}, bf16[16,1152]{1,0:T(8,128)(2,1)S(1)}, u32[]{:S(2)}, u32[]{:S(2)}) %collective-permute-start) | collective-permute-done | bytes 36896 | tf_op jit(solution)/shard_map/ppermute | solution.py:321
  8.3 0.0 collective-permute-done.1.refs_2_.refs_3_.refs_5_
  8.4 0.7 %shard_map.95 = (s16[16,1152]{1,0:T(8,128)(2,1)S(1)}, f32[16,128]{1,0:T(8,128)S(1)}) custom-call(bf16[32,1152]{1,0:T(8,128)(2,1)S(1)} %shard_map.94.refs_0_.refs_1_, bf16[512,1024]{1,0:T(8,128)(2,1)S(1)} %get-tuple-element.28.refs_1_.refs_2_.refs_4_, bf16[512,1024]{1,0:T(8,128)(2,1)S(1)} %collective-permute-done.1.refs_2_.refs_3_.refs_5_), custom_call_target="tpu_custom_call" | custom-call | flops 67108864 | bytes 2162688 | tf_op jit(solution)/shard_map/pallas_call | solution.py:38
  9.0 2.7 %collective-permute-start.4 = (s16[16,1152]{1,0:T(8,128)(2,1)S(1)}, s16[16,1152]{1,0:T(8,128)(2,1)S(1)}, u32[]{:S(2)}, u32[]{:S(2)}) collective-permute-start(s16[16,1152]{1,0:T(8,128)(2,1)S(1)} %get-tuple-element.29.refs_0_.refs_1_), channel_id=1, source_target_pairs={{0,2},{1,3},{2,0},{3,1},{4,6},{5,7},{6,4},{7,5},{8,10},{9,11},{10,... | collective-permute-start | bytes 110600 | tf_op jit(solution)/shard_map/ppermute | solution.py:321
  11.7 0.0 collective-permute-done.2.refs_1_
  11.7 0.0 collective-permute-done.3.refs_2_
  11.7 0.7 %shard_map.97 = (s16[16,1152]{1,0:T(8,128)(2,1)S(1)}, f32[16,128]{1,0:T(8,128)S(1)}) custom-call(s16[16,1152]{1,0:T(8,128)(2,1)S(1)} %get-tuple-element.29.refs_0_.refs_1_, bf16[32,1152]{1,0:T(8,128)(2,1)S(1)} %shard_map.96.refs_1_.refs_2_, bf16[512,1024]{1,0:T(8,128)(2,1)S(1)} %get-tuple-element.28.refs_1_.refs_2_.refs_4_, ...), custom_call_target="tpu_custom_call" | custom-call | flops 67108864 | bytes 2162688 | tf_op jit(solution)/shard_map/pallas_call | solution.py:38
  12.4 1.0 %collective-permute-start.5 = (s16[16,1152]{1,0:T(8,128)(2,1)S(1)}, s16[16,1152]{1,0:T(8,128)(2,1)S(1)}, u32[]{:S(2)}, u32[]{:S(2)}) collective-permute-start(s16[16,1152]{1,0:T(8,128)(2,1)S(1)} %get-tuple-element.30.refs_0_.refs_1_), channel_id=1, source_target_pairs={{0,2},{1,3},{2,0},{3,1},{4,6},{5,7},{6,4},{7,5},{8,10},{9,11},{10,... | collective-permute-start | bytes 110600 | tf_op jit(solution)/shard_map/ppermute | solution.py:321
  13.4 0.2 collective-permute-start.8
  13.6 0.4 %collective-permute-done.4.refs_2_ = s16[16,1152]{1,0:T(8,128)(2,1)S(1)} collective-permute-done((s16[16,1152]{1,0:T(8,128)(2,1)S(1)}, s16[16,1152]{1,0:T(8,128)(2,1)S(1)}, u32[]{:S(2)}, u32[]{:S(2)}) %collective-permute-start.4) | collective-permute-done | bytes 36896 | tf_op jit(solution)/shard_map/ppermute | solution.py:321
  14.0 0.2 shard_map.98.refs_0_.refs_1_
  14.1 1.7 %collective-permute-start.6 = (s16[16,1152]{1,0:T(8,128)(2,1)S(1)}, s16[16,1152]{1,0:T(8,128)(2,1)S(1)}, u32[]{:S(2)}, u32[]{:S(2)}) collective-permute-start(s16[16,1152]{1,0:T(8,128)(2,1)S(1)} %shard_map.98.refs_0_.refs_1_), channel_id=1, source_target_pairs={{0,1},{1,0},{2,3},{3,2},{4,5},{5,4},{6,7},{7,6},{8,9},{9,8},{10,11... | collective-permute-start | bytes 110600 | tf_op jit(solution)/shard_map/ppermute | solution.py:321
  15.8 0.0 collective-permute-start.9
  15.8 1.9 %collective-permute-done.5.refs_2_ = s16[16,1152]{1,0:T(8,128)(2,1)S(1)} collective-permute-done((s16[16,1152]{1,0:T(8,128)(2,1)S(1)}, s16[16,1152]{1,0:T(8,128)(2,1)S(1)}, u32[]{:S(2)}, u32[]{:S(2)}) %collective-permute-start.5) | collective-permute-done | bytes 36896 | tf_op jit(solution)/shard_map/ppermute | solution.py:321
  17.7 0.2 shard_map.99.refs_0_.refs_1_
  17.9 1.2 %collective-permute-start.10 = (s16[16,1152]{1,0:T(8,128)(2,1)S(1)}, s16[16,1152]{1,0:T(8,128)(2,1)S(1)}, u32[]{:S(2)}, u32[]{:S(2)}) collective-permute-start(s16[16,1152]{1,0:T(8,128)(2,1)S(1)} %shard_map.99.refs_0_.refs_1_), channel_id=1, source_target_pairs={{0,1},{1,0},{2,3},{3,2},{4,5},{5,4},{6,7},{7,6},{8,9},{9,8},{10,11... | collective-permute-start | bytes 110600 | tf_op jit(solution)/shard_map/ppermute | solution.py:321
  19.2 0.0 collective-permute-done.6.refs_2_
  19.2 0.4 %shard_map.100 = (bf16[32,256]{1,0:T(8,128)(2,1)S(1)}, bf16[32,256]{1,0:T(8,128)(2,1)S(1)}, f32[8,1152]{1,0:T(8,128)S(1)}, f32[8,1152]{1,0:T(8,128)S(1)}) custom-call(s16[16,1152]{1,0:T(8,128)(2,1)S(1)} %shard_map.99.refs_0_.refs_1_, s16[16,1152]{1,0:T(8,128)(2,1)S(1)} %shard_map.98.refs_0_.refs_1_, s16[16,1152]{1,0:T(8,128)(2,1)S(1)} %collective-permute-done.6.refs_2_, ...), custom_call_target="tpu_custom_call" | custom-call | flops 16777216 | bytes 1114112 | tf_op jit(solution)/shard_map/pallas_call | solution.py:38
  19.6 1.6 %collective-permute-start.7 = (f32[8,1152]{1,0:T(8,128)S(1)}, f32[8,1152]{1,0:T(8,128)S(1)}, u32[]{:S(2)}, u32[]{:S(2)}) collective-permute-start(f32[8,1152]{1,0:T(8,128)S(1)} %get-tuple-element.32), channel_id=1, source_target_pairs={{0,28},{4,24},{8,20},{12,16},{16,12},{20,8},{24,4},{28,0},{1,29},{... | collective-permute-start | bytes 110600 | tf_op jit(solution)/shard_map/ppermute | solution.py:321
  21.2 0.7 %collective-permute-done.10.refs_2_ = s16[16,1152]{1,0:T(8,128)(2,1)S(1)} collective-permute-done((s16[16,1152]{1,0:T(8,128)(2,1)S(1)}, s16[16,1152]{1,0:T(8,128)(2,1)S(1)}, u32[]{:S(2)}, u32[]{:S(2)}) %collective-permute-start.10) | collective-permute-done | bytes 36896 | tf_op jit(solution)/shard_map/ppermute | solution.py:321
  21.9 0.4 %shard_map.101 = (bf16[32,256]{1,0:T(8,128)(2,1)S(1)}, bf16[64,256]{1,0:T(8,128)(2,1)S(1)}, bf16[8,1152]{1,0:T(8,128)(2,1)S(1)}, bf16[8,1152]{1,0:T(8,128)(2,1)S(1)}) custom-call(bf16[32,256]{1,0:T(8,128)(2,1)S(1)} %get-tuple-element.33.refs_0_.refs_5_, s16[16,1152]{1,0:T(8,128)(2,1)S(1)} %shard_map.99.refs_0_.refs_1_, ...), custom_call_target="tpu_custom_call" | custom-call | flops 16777216 | bytes 1114112 | tf_op jit(solution)/shard_map/pallas_call | solution.py:38
  22.3 0.2 collective-permute-start.11
  22.5 1.0 %collective-permute-start.12 = (bf16[8,1152]{1,0:T(8,128)(2,1)S(1)}, bf16[8,1152]{1,0:T(8,128)(2,1)S(1)}, u32[]{:S(2)}, u32[]{:S(2)}) collective-permute-start(bf16[8,1152]{1,0:T(8,128)(2,1)S(1)} %get-tuple-element.40), channel_id=1, source_target_pairs={{0,12},{4,8},{8,4},{12,0},{16,28},{20,24},{24,20},{28,16},{1,13},{... | collective-permute-start | bytes 55304 | tf_op jit(solution)/shard_map/ppermute | solution.py:321
  23.6 0.0 collective-permute-done.8.refs_3_
  23.6 1.1 %collective-permute-start.13 = (bf16[8,1152]{1,0:T(8,128)(2,1)S(1)}, bf16[8,1152]{1,0:T(8,128)(2,1)S(1)}, u32[]{:S(2)}, u32[]{:S(2)}) collective-permute-start(bf16[8,1152]{1,0:T(8,128)(2,1)S(1)} %get-tuple-element.41), channel_id=1, source_target_pairs={{0,20},{4,16},{8,28},{12,24},{16,4},{20,0},{24,12},{28,8},{1,21},{... | collective-permute-start | bytes 55304 | tf_op jit(solution)/shard_map/ppermute | solution.py:321
  24.7 0.0 collective-permute-done.9.refs_4_
  24.7 0.0 collective-permute-done.11.refs_7_
  24.7 0.0 collective-permute-done.7.refs_0_.refs_4_
  24.7 1.6 %shard_map.102 = (f32[1024,256]{1,0:T(8,128)}, f32[256,1024]{1,0:T(8,128)}, f32[8,128]{1,0:T(8,128)S(1)}) custom-call(f32[8,1152]{1,0:T(8,128)S(1)} %collective-permute-done.7.refs_0_.refs_4_, bf16[32,1152]{1,0:T(8,128)(2,1)S(1)} %shard_map.94.refs_0_.refs_1_, bf16[32,1152]{1,0:T(8,128)(2,1)S(1)} %shard_map.96.refs_1_.refs_2_, ...), custom_call_target="tpu_custom_call" | custom-call | flops 134217728 | bytes 2097152 | tf_op jit(solution)/shard_map/pallas_call | solution.py:38
  26.3 0.0 collective-permute-done.12.refs_2_
  26.4 0.4 %collective-permute-done.13.refs_3_ = bf16[8,1152]{1,0:T(8,128)(2,1)S(1)} collective-permute-done((bf16[8,1152]{1,0:T(8,128)(2,1)S(1)}, bf16[8,1152]{1,0:T(8,128)(2,1)S(1)}, u32[]{:S(2)}, u32[]{:S(2)}) %collective-permute-start.13) | collective-permute-done | bytes 18464 | tf_op jit(solution)/shard_map/ppermute | solution.py:321
  26.8 1.1 %shard_map.103 = (bf16[256,1024]{1,0:T(8,128)(2,1)}, f32[2,256]{1,0:T(2,128)}) custom-call(f32[8,128]{1,0:T(8,128)S(1)} %get-tuple-element.38.refs_0_, f32[8,1152]{1,0:T(8,128)S(1)} %get-tuple-element.39.refs_1_, bf16[8,1152]{1,0:T(8,128)(2,1)S(1)} %collective-permute-done.12.refs_2_, bf16[8,1152]{1,0:T(8,128)(2,1)S(1)} %collective-permute-done.13.refs_3_, ...), custom_call_target="tpu_custom_call" | custom-call | flops 16777216 | bytes 524288 | tf_op jit(solution)/shard_map/pallas_call | solution.py:38
  (2 shorter events, 0.0 us)
Async XLA Ops:
  2.4 6.0 %collective-permute-start.1 = (bf16[512,1024]{1,0:T(8,128)(2,1)S(1)}, bf16[512,1024]{1,0:T(8,128)(2,1)S(1)}, u32[]{:S(2)}, u32[]{:S(2)}) collective-permute-start(bf16[512,1024]{1,0:T(8,128)(2,1)S(1)} %get-tuple-element.28.refs_1_.refs_2_.refs_4_), channel_id=1, source_target_pairs={{0,4},{4,0},{1,5},{5,1},{2,6},{6,2},{3,7},{7,3},{8,12},{12,8},{9,1... | collective-permute-start | bytes 3145736 | tf_op jit(solution)/shard_map/ppermute | solution.py:321
  2.9 5.4 %collective-permute-start = (bf16[16,1152]{1,0:T(8,128)(2,1)S(1)}, bf16[16,1152]{1,0:T(8,128)(2,1)S(1)}, u32[]{:S(2)}, u32[]{:S(2)}) collective-permute-start(bf16[16,1152]{1,0:T(8,128)(2,1)S(1)} %get-tuple-element.27), channel_id=1, source_target_pairs={{0,28},{4,24},{8,20},{12,16},{16,12},{20,8},{24,4},{28,0},{1,29},{... | collective-permute-start | bytes 110600 | tf_op jit(solution)/shard_map/ppermute | solution.py:321
  6.5 5.2 %collective-permute-start.2 = (bf16[16,1152]{1,0:T(8,128)(2,1)S(1)}, bf16[16,1152]{1,0:T(8,128)(2,1)S(1)}, u32[]{:S(2)}, u32[]{:S(2)}) collective-permute-start(bf16[16,1152]{1,0:T(8,128)(2,1)S(1)} %get-tuple-element.26.refs_0_), channel_id=1, source_target_pairs={{0,12},{4,8},{8,4},{12,0},{16,28},{20,24},{24,20},{28,16},{1,13},{... | collective-permute-start | bytes 110600 | tf_op jit(solution)/shard_map/ppermute | solution.py:321
  6.7 5.0 %collective-permute-start.3 = (bf16[16,1152]{1,0:T(8,128)(2,1)S(1)}, bf16[16,1152]{1,0:T(8,128)(2,1)S(1)}, u32[]{:S(2)}, u32[]{:S(2)}) collective-permute-start(bf16[16,1152]{1,0:T(8,128)(2,1)S(1)} %get-tuple-element.27), channel_id=1, source_target_pairs={{0,20},{4,16},{8,28},{12,24},{16,4},{20,0},{24,12},{28,8},{1,21},{... | collective-permute-start | bytes 110600 | tf_op jit(solution)/shard_map/ppermute | solution.py:321
  9.0 4.9 %collective-permute-start.4 = (s16[16,1152]{1,0:T(8,128)(2,1)S(1)}, s16[16,1152]{1,0:T(8,128)(2,1)S(1)}, u32[]{:S(2)}, u32[]{:S(2)}) collective-permute-start(s16[16,1152]{1,0:T(8,128)(2,1)S(1)} %get-tuple-element.29.refs_0_.refs_1_), channel_id=1, source_target_pairs={{0,2},{1,3},{2,0},{3,1},{4,6},{5,7},{6,4},{7,5},{8,10},{9,11},{10,... | collective-permute-start | bytes 110600 | tf_op jit(solution)/shard_map/ppermute | solution.py:321
  12.4 5.3 %collective-permute-start.5 = (s16[16,1152]{1,0:T(8,128)(2,1)S(1)}, s16[16,1152]{1,0:T(8,128)(2,1)S(1)}, u32[]{:S(2)}, u32[]{:S(2)}) collective-permute-start(s16[16,1152]{1,0:T(8,128)(2,1)S(1)} %get-tuple-element.30.refs_0_.refs_1_), channel_id=1, source_target_pairs={{0,2},{1,3},{2,0},{3,1},{4,6},{5,7},{6,4},{7,5},{8,10},{9,11},{10,... | collective-permute-start | bytes 110600 | tf_op jit(solution)/shard_map/ppermute | solution.py:321
  13.4 10.2 %collective-permute-start.8 = (bf16[32,1152]{1,0:T(8,128)(2,1)S(1)}, bf16[32,1152]{1,0:T(8,128)(2,1)S(1)}, u32[]{:S(2)}, u32[]{:S(2)}) collective-permute-start(bf16[32,1152]{1,0:T(8,128)(2,1)S(1)} %shard_map.94.refs_0_.refs_1_), channel_id=1, source_target_pairs={{0,4},{4,0},{1,5},{5,1},{2,6},{6,2},{3,7},{7,3},{8,12},{12,8},{9,1... | collective-permute-start | bytes 221192 | tf_op jit(solution)/shard_map/ppermute | solution.py:321
  14.1 5.0 %collective-permute-start.6 = (s16[16,1152]{1,0:T(8,128)(2,1)S(1)}, s16[16,1152]{1,0:T(8,128)(2,1)S(1)}, u32[]{:S(2)}, u32[]{:S(2)}) collective-permute-start(s16[16,1152]{1,0:T(8,128)(2,1)S(1)} %shard_map.98.refs_0_.refs_1_), channel_id=1, source_target_pairs={{0,1},{1,0},{2,3},{3,2},{4,5},{5,4},{6,7},{7,6},{8,9},{9,8},{10,11... | collective-permute-start | bytes 110600 | tf_op jit(solution)/shard_map/ppermute | solution.py:321
  15.8 8.9 %collective-permute-start.9 = (bf16[32,1152]{1,0:T(8,128)(2,1)S(1)}, bf16[32,1152]{1,0:T(8,128)(2,1)S(1)}, u32[]{:S(2)}, u32[]{:S(2)}) collective-permute-start(bf16[32,1152]{1,0:T(8,128)(2,1)S(1)} %shard_map.96.refs_1_.refs_2_), channel_id=1, source_target_pairs={{0,4},{4,0},{1,5},{5,1},{2,6},{6,2},{3,7},{7,3},{8,12},{12,8},{9,1... | collective-permute-start | bytes 221192 | tf_op jit(solution)/shard_map/ppermute | solution.py:321
  17.9 4.0 %collective-permute-start.10 = (s16[16,1152]{1,0:T(8,128)(2,1)S(1)}, s16[16,1152]{1,0:T(8,128)(2,1)S(1)}, u32[]{:S(2)}, u32[]{:S(2)}) collective-permute-start(s16[16,1152]{1,0:T(8,128)(2,1)S(1)} %shard_map.99.refs_0_.refs_1_), channel_id=1, source_target_pairs={{0,1},{1,0},{2,3},{3,2},{4,5},{5,4},{6,7},{7,6},{8,9},{9,8},{10,11... | collective-permute-start | bytes 110600 | tf_op jit(solution)/shard_map/ppermute | solution.py:321
  19.6 5.1 %collective-permute-start.7 = (f32[8,1152]{1,0:T(8,128)S(1)}, f32[8,1152]{1,0:T(8,128)S(1)}, u32[]{:S(2)}, u32[]{:S(2)}) collective-permute-start(f32[8,1152]{1,0:T(8,128)S(1)} %get-tuple-element.32), channel_id=1, source_target_pairs={{0,28},{4,24},{8,20},{12,16},{16,12},{20,8},{24,4},{28,0},{1,29},{... | collective-permute-start | bytes 110600 | tf_op jit(solution)/shard_map/ppermute | solution.py:321
  22.3 2.4 %collective-permute-start.11 = (bf16[64,256]{1,0:T(8,128)(2,1)S(1)}, bf16[64,256]{1,0:T(8,128)(2,1)S(1)}, u32[]{:S(2)}, u32[]{:S(2)}) collective-permute-start(bf16[64,256]{1,0:T(8,128)(2,1)S(1)} %get-tuple-element.37), channel_id=1, source_target_pairs={{0,4},{4,0},{1,5},{5,1},{2,6},{6,2},{3,7},{7,3},{8,12},{12,8},{9,1... | collective-permute-start | bytes 98312 | tf_op jit(solution)/shard_map/ppermute | solution.py:321
  22.5 3.8 %collective-permute-start.12 = (bf16[8,1152]{1,0:T(8,128)(2,1)S(1)}, bf16[8,1152]{1,0:T(8,128)(2,1)S(1)}, u32[]{:S(2)}, u32[]{:S(2)}) collective-permute-start(bf16[8,1152]{1,0:T(8,128)(2,1)S(1)} %get-tuple-element.40), channel_id=1, source_target_pairs={{0,12},{4,8},{8,4},{12,0},{16,28},{20,24},{24,20},{28,16},{1,13},{... | collective-permute-start | bytes 55304 | tf_op jit(solution)/shard_map/ppermute | solution.py:321
  23.6 3.2 %collective-permute-start.13 = (bf16[8,1152]{1,0:T(8,128)(2,1)S(1)}, bf16[8,1152]{1,0:T(8,128)(2,1)S(1)}, u32[]{:S(2)}, u32[]{:S(2)}) collective-permute-start(bf16[8,1152]{1,0:T(8,128)(2,1)S(1)} %get-tuple-element.41), channel_id=1, source_target_pairs={{0,20},{4,16},{8,28},{12,24},{16,4},{20,0},{24,12},{28,8},{1,21},{... | collective-permute-start | bytes 55304 | tf_op jit(solution)/shard_map/ppermute | solution.py:321

commit v4 on v3

--- a/solution.py
+++ b/solution.py
@@ -381,10 +381,12 @@
     for step in range(1, nodes):
         pieces.append(swap_nodes(own_rows if step < half_nodes else other_rows, step))
     rows = half_nodes * (locals_ // 2) * capacity
+    bits = [1 << place for place in range(edatas.bit_length() - 1)]
+    orders = (bits[::-1], bits)
     last = ()
     chains = []
     held = []
-    for steps in (far, near):
+    for steps, order in zip((far, near), orders):
         chunk = join([pieces[step] for step in steps], last)
         bit = 2
         while bit < locals_:
@@ -399,9 +401,8 @@
             after=last,
         )(chunk, weights, other_weights)
         last = (part,)
-        chains.append((part, swap(part, "edata", edatas // 2), gate_rows))
-    bit = edatas // 4
-    while bit:
+        chains.append((part, swap(part, "edata", order[0]), gate_rows))
+    for stage in range(1, len(bits)):
         for index, (part, other, gate_rows) in enumerate(chains):
             part = call(
                 add_codes_kernel,
@@ -411,8 +412,7 @@
                 after=last,
             )(part, other)
             last = (part,)
-            chains[index] = (part, swap(part, "edata", bit), gate_rows)
-        bit //= 2
+            chains[index] = (part, swap(part, "edata", orders[index][stage]), gate_rows)
 
     mine = []
     theirs = ()

time: 28 us -> 28.3 us (1.011)
  starting transfers between devices: 15.1 us -> 18.2 us
  waiting for transfers between devices: 5.04 us -> 2.29 us
    ppermute x14, starting transfers between devices: 15.1 us -> 18.2 us  [swap(): lax.ppermute(array, axes, [(index, index ^ bit) for index in range(size)])]
    ppermute x14, waiting for transfers between devices: 5.04 us -> 2.29 us  [swap(): lax.ppermute(array, axes, [(index, index ^ bit) for index in range(size)])]
  transfers between devices with their start and end apart: 14 -> 14, of which waited for: 5 -> 3; matrix products, arithmetic and copies ran while one was open for 0% -> 0% of each run, Pallas kernels for 15% -> 15%
where the time goes in v4:
time: 28.3 us; the launch traced here: 28.2 us
  starting transfers between devices  18.2 us (64%)
  Pallas kernels  7.01 us (25%)
  waiting for transfers between devices  2.29 us (8%)
  between operations  0.71 us (3%)
    ppermute x14, starting transfers between devices, swap(): lax.ppermute(array, axes, [(index, index ^ bit) for index in range(size)])  18.2 us
    pallas_call x11, Pallas kernels, run(): pl.pallas_call(lambda *refs: kernel(*refs[len(after):]), out_shape=out_sh...  7.01 us
    ppermute x14, waiting for transfers between devices, swap(): lax.ppermute(array, axes, [(index, index ^ bit) for index in range(size)])  2.29 us
  transfers between devices with their start and end apart: 14, of which 3 were waited for; matrix products, arithmetic and copies ran while one was open for 0% of the time, Pallas kernels for 15%

profile of v4, /device:TPU:0, one launch (start us, length us, event | category | flops | bytes accessed | tf_op | source)
XLA Modules:
  0.0 28.2 jit_solution(1265060303412692643)
XLA Ops:
  0.6 1.8 %shard_map.93 = (bf16[16,1152]{1,0:T(8,128)(2,1)S(1)}, bf16[16,1152]{1,0:T(8,128)(2,1)S(1)}, bf16[32,256]{1,0:T(8,128)(2,1)S(1)}, bf16[256,32]{1,0:T(8,128)(2,1)S(1)}, bf16[512,1024]{1,0:T(8,128)(2,1)S(1)}) custom-call(s32[2,256]{1,0:T(2,128)} %bitcast.3, bf16[2,256]{1,0:T(2,128)(2,1)} %bitcast.4, bf16[256,1024]{1,0:T(8,128)(2,1)} %refs_2_.1, ...), custom_call_target="tpu_custom_call" | custom-call | flops 16777216 | bytes 2097152 | tf_op jit(solution)/shard_map/pallas_call | solution.py:38
  2.4 0.5 %collective-permute-start.1 = (bf16[512,1024]{1,0:T(8,128)(2,1)S(1)}, bf16[512,1024]{1,0:T(8,128)(2,1)S(1)}, u32[]{:S(2)}, u32[]{:S(2)}) collective-permute-start(bf16[512,1024]{1,0:T(8,128)(2,1)S(1)} %get-tuple-element.28.refs_1_.refs_2_.refs_4_), channel_id=1, source_target_pairs={{0,4},{4,0},{1,5},{5,1},{2,6},{6,2},{3,7},{7,3},{8,12},{12,8},{9,1... | collective-permute-start | bytes 3145736 | tf_op jit(solution)/shard_map/ppermute | solution.py:321
  2.9 3.6 %collective-permute-start = (bf16[16,1152]{1,0:T(8,128)(2,1)S(1)}, bf16[16,1152]{1,0:T(8,128)(2,1)S(1)}, u32[]{:S(2)}, u32[]{:S(2)}) collective-permute-start(bf16[16,1152]{1,0:T(8,128)(2,1)S(1)} %get-tuple-element.27), channel_id=1, source_target_pairs={{0,28},{4,24},{8,20},{12,16},{16,12},{20,8},{24,4},{28,0},{1,29},{... | collective-permute-start | bytes 110600 | tf_op jit(solution)/shard_map/ppermute | solution.py:321
  6.5 0.2 collective-permute-start.2
  6.7 0.1 collective-permute-start.3
  6.8 1.5 %collective-permute-done.refs_1_ = bf16[16,1152]{1,0:T(8,128)(2,1)S(1)} collective-permute-done((bf16[16,1152]{1,0:T(8,128)(2,1)S(1)}, bf16[16,1152]{1,0:T(8,128)(2,1)S(1)}, u32[]{:S(2)}, u32[]{:S(2)}) %collective-permute-start) | collective-permute-done | bytes 36896 | tf_op jit(solution)/shard_map/ppermute | solution.py:321
  8.3 0.0 collective-permute-done.1.refs_2_.refs_3_.refs_5_
  8.4 0.7 %shard_map.95 = (s16[16,1152]{1,0:T(8,128)(2,1)S(1)}, f32[16,128]{1,0:T(8,128)S(1)}) custom-call(bf16[32,1152]{1,0:T(8,128)(2,1)S(1)} %shard_map.94.refs_0_.refs_1_, bf16[512,1024]{1,0:T(8,128)(2,1)S(1)} %get-tuple-element.28.refs_1_.refs_2_.refs_4_, bf16[512,1024]{1,0:T(8,128)(2,1)S(1)} %collective-permute-done.1.refs_2_.refs_3_.refs_5_), custom_call_target="tpu_custom_call" | custom-call | flops 67108864 | bytes 2162688 | tf_op jit(solution)/shard_map/pallas_call | solution.py:38
  9.0 2.7 %collective-permute-start.4 = (s16[16,1152]{1,0:T(8,128)(2,1)S(1)}, s16[16,1152]{1,0:T(8,128)(2,1)S(1)}, u32[]{:S(2)}, u32[]{:S(2)}) collective-permute-start(s16[16,1152]{1,0:T(8,128)(2,1)S(1)} %get-tuple-element.29.refs_0_.refs_1_), channel_id=1, source_target_pairs={{0,2},{1,3},{2,0},{3,1},{4,6},{5,7},{6,4},{7,5},{8,10},{9,11},{10,... | collective-permute-start | bytes 110600 | tf_op jit(solution)/shard_map/ppermute | solution.py:321
  11.7 0.0 collective-permute-done.2.refs_1_
  11.7 0.0 collective-permute-done.3.refs_2_
  11.7 0.7 %shard_map.97 = (s16[16,1152]{1,0:T(8,128)(2,1)S(1)}, f32[16,128]{1,0:T(8,128)S(1)}) custom-call(s16[16,1152]{1,0:T(8,128)(2,1)S(1)} %get-tuple-element.29.refs_0_.refs_1_, bf16[32,1152]{1,0:T(8,128)(2,1)S(1)} %shard_map.96.refs_1_.refs_2_, bf16[512,1024]{1,0:T(8,128)(2,1)S(1)} %get-tuple-element.28.refs_1_.refs_2_.refs_4_, ...), custom_call_target="tpu_custom_call" | custom-call | flops 67108864 | bytes 2162688 | tf_op jit(solution)/shard_map/pallas_call | solution.py:38
  12.4 1.6 %collective-permute-start.5 = (s16[16,1152]{1,0:T(8,128)(2,1)S(1)}, s16[16,1152]{1,0:T(8,128)(2,1)S(1)}, u32[]{:S(2)}, u32[]{:S(2)}) collective-permute-start(s16[16,1152]{1,0:T(8,128)(2,1)S(1)} %get-tuple-element.30.refs_0_.refs_1_), channel_id=1, source_target_pairs={{0,1},{1,0},{2,3},{3,2},{4,5},{5,4},{6,7},{7,6},{8,9},{9,8},{10,11... | collective-permute-start | bytes 110600 | tf_op jit(solution)/shard_map/ppermute | solution.py:321
  14.0 0.0 collective-permute-start.8
  14.0 0.0 collective-permute-done.4.refs_2_
  14.0 0.2 shard_map.98.refs_0_.refs_1_
  14.2 1.6 %collective-permute-start.6 = (s16[16,1152]{1,0:T(8,128)(2,1)S(1)}, s16[16,1152]{1,0:T(8,128)(2,1)S(1)}, u32[]{:S(2)}, u32[]{:S(2)}) collective-permute-start(s16[16,1152]{1,0:T(8,128)(2,1)S(1)} %shard_map.98.refs_0_.refs_1_), channel_id=1, source_target_pairs={{0,1},{1,0},{2,3},{3,2},{4,5},{5,4},{6,7},{7,6},{8,9},{9,8},{10,11... | collective-permute-start | bytes 110600 | tf_op jit(solution)/shard_map/ppermute | solution.py:321
  15.8 0.0 collective-permute-start.9
  15.8 0.6 %collective-permute-done.5.refs_2_ = s16[16,1152]{1,0:T(8,128)(2,1)S(1)} collective-permute-done((s16[16,1152]{1,0:T(8,128)(2,1)S(1)}, s16[16,1152]{1,0:T(8,128)(2,1)S(1)}, u32[]{:S(2)}, u32[]{:S(2)}) %collective-permute-start.5) | collective-permute-done | bytes 36896 | tf_op jit(solution)/shard_map/ppermute | solution.py:321
  16.4 0.2 shard_map.99.refs_0_.refs_1_
  16.6 2.6 %collective-permute-start.10 = (s16[16,1152]{1,0:T(8,128)(2,1)S(1)}, s16[16,1152]{1,0:T(8,128)(2,1)S(1)}, u32[]{:S(2)}, u32[]{:S(2)}) collective-permute-start(s16[16,1152]{1,0:T(8,128)(2,1)S(1)} %shard_map.99.refs_0_.refs_1_), channel_id=1, source_target_pairs={{0,2},{1,3},{2,0},{3,1},{4,6},{5,7},{6,4},{7,5},{8,10},{9,11},{10,... | collective-permute-start | bytes 110600 | tf_op jit(solution)/shard_map/ppermute | solution.py:321
  19.2 0.0 collective-permute-done.6.refs_2_
  19.2 0.4 %shard_map.100 = (bf16[32,256]{1,0:T(8,128)(2,1)S(1)}, bf16[32,256]{1,0:T(8,128)(2,1)S(1)}, f32[8,1152]{1,0:T(8,128)S(1)}, f32[8,1152]{1,0:T(8,128)S(1)}) custom-call(s16[16,1152]{1,0:T(8,128)(2,1)S(1)} %shard_map.99.refs_0_.refs_1_, s16[16,1152]{1,0:T(8,128)(2,1)S(1)} %shard_map.98.refs_0_.refs_1_, s16[16,1152]{1,0:T(8,128)(2,1)S(1)} %collective-permute-done.6.refs_2_, ...), custom_call_target="tpu_custom_call" | custom-call | flops 16777216 | bytes 1114112 | tf_op jit(solution)/shard_map/pallas_call | solution.py:38
  19.6 2.7 %collective-permute-start.7 = (f32[8,1152]{1,0:T(8,128)S(1)}, f32[8,1152]{1,0:T(8,128)S(1)}, u32[]{:S(2)}, u32[]{:S(2)}) collective-permute-start(f32[8,1152]{1,0:T(8,128)S(1)} %get-tuple-element.32), channel_id=1, source_target_pairs={{0,28},{4,24},{8,20},{12,16},{16,12},{20,8},{24,4},{28,0},{1,29},{... | collective-permute-start | bytes 110600 | tf_op jit(solution)/shard_map/ppermute | solution.py:321
  22.3 0.0 collective-permute-done.10.refs_2_
  22.3 0.4 %shard_map.101 = (bf16[32,256]{1,0:T(8,128)(2,1)S(1)}, bf16[64,256]{1,0:T(8,128)(2,1)S(1)}, bf16[8,1152]{1,0:T(8,128)(2,1)S(1)}, bf16[8,1152]{1,0:T(8,128)(2,1)S(1)}) custom-call(bf16[32,256]{1,0:T(8,128)(2,1)S(1)} %get-tuple-element.33.refs_0_.refs_5_, s16[16,1152]{1,0:T(8,128)(2,1)S(1)} %shard_map.99.refs_0_.refs_1_, ...), custom_call_target="tpu_custom_call" | custom-call | flops 16777216 | bytes 1114112 | tf_op jit(solution)/shard_map/pallas_call | solution.py:38
  22.7 0.3 %collective-permute-start.11 = (bf16[64,256]{1,0:T(8,128)(2,1)S(1)}, bf16[64,256]{1,0:T(8,128)(2,1)S(1)}, u32[]{:S(2)}, u32[]{:S(2)}) collective-permute-start(bf16[64,256]{1,0:T(8,128)(2,1)S(1)} %get-tuple-element.37), channel_id=1, source_target_pairs={{0,4},{4,0},{1,5},{5,1},{2,6},{6,2},{3,7},{7,3},{8,12},{12,8},{9,1... | collective-permute-start | bytes 98312 | tf_op jit(solution)/shard_map/ppermute | solution.py:321
  23.0 0.9 %collective-permute-start.12 = (bf16[8,1152]{1,0:T(8,128)(2,1)S(1)}, bf16[8,1152]{1,0:T(8,128)(2,1)S(1)}, u32[]{:S(2)}, u32[]{:S(2)}) collective-permute-start(bf16[8,1152]{1,0:T(8,128)(2,1)S(1)} %get-tuple-element.40), channel_id=1, source_target_pairs={{0,12},{4,8},{8,4},{12,0},{16,28},{20,24},{24,20},{28,16},{1,13},{... | collective-permute-start | bytes 55304 | tf_op jit(solution)/shard_map/ppermute | solution.py:321
  23.9 0.0 collective-permute-done.8.refs_3_
  23.9 1.4 %collective-permute-start.13 = (bf16[8,1152]{1,0:T(8,128)(2,1)S(1)}, bf16[8,1152]{1,0:T(8,128)(2,1)S(1)}, u32[]{:S(2)}, u32[]{:S(2)}) collective-permute-start(bf16[8,1152]{1,0:T(8,128)(2,1)S(1)} %get-tuple-element.41), channel_id=1, source_target_pairs={{0,20},{4,16},{8,28},{12,24},{16,4},{20,0},{24,12},{28,8},{1,21},{... | collective-permute-start | bytes 55304 | tf_op jit(solution)/shard_map/ppermute | solution.py:321
  25.4 0.0 collective-permute-done.9.refs_4_
  25.4 0.0 collective-permute-done.11.refs_7_
  25.4 0.0 collective-permute-done.7.refs_0_.refs_4_
  25.4 1.6 %shard_map.102 = (f32[1024,256]{1,0:T(8,128)}, f32[256,1024]{1,0:T(8,128)}, f32[8,128]{1,0:T(8,128)S(1)}) custom-call(f32[8,1152]{1,0:T(8,128)S(1)} %collective-permute-done.7.refs_0_.refs_4_, bf16[32,1152]{1,0:T(8,128)(2,1)S(1)} %shard_map.94.refs_0_.refs_1_, bf16[32,1152]{1,0:T(8,128)(2,1)S(1)} %shard_map.96.refs_1_.refs_2_, ...), custom_call_target="tpu_custom_call" | custom-call | flops 134217728 | bytes 2097152 | tf_op jit(solution)/shard_map/pallas_call | solution.py:38
  27.0 0.0 collective-permute-done.12.refs_2_
  27.0 0.1 collective-permute-done.13.refs_3_
  27.1 1.1 %shard_map.103 = (bf16[256,1024]{1,0:T(8,128)(2,1)}, f32[2,256]{1,0:T(2,128)}) custom-call(f32[8,128]{1,0:T(8,128)S(1)} %get-tuple-element.38.refs_0_, f32[8,1152]{1,0:T(8,128)S(1)} %get-tuple-element.39.refs_1_, bf16[8,1152]{1,0:T(8,128)(2,1)S(1)} %collective-permute-done.12.refs_2_, bf16[8,1152]{1,0:T(8,128)(2,1)S(1)} %collective-permute-done.13.refs_3_, ...), custom_call_target="tpu_custom_call" | custom-call | flops 16777216 | bytes 524288 | tf_op jit(solution)/shard_map/pallas_call | solution.py:38
  (2 shorter events, 0.0 us)
Async XLA Ops:
  2.4 6.0 %collective-permute-start.1 = (bf16[512,1024]{1,0:T(8,128)(2,1)S(1)}, bf16[512,1024]{1,0:T(8,128)(2,1)S(1)}, u32[]{:S(2)}, u32[]{:S(2)}) collective-permute-start(bf16[512,1024]{1,0:T(8,128)(2,1)S(1)} %get-tuple-element.28.refs_1_.refs_2_.refs_4_), channel_id=1, source_target_pairs={{0,4},{4,0},{1,5},{5,1},{2,6},{6,2},{3,7},{7,3},{8,12},{12,8},{9,1... | collective-permute-start | bytes 3145736 | tf_op jit(solution)/shard_map/ppermute | solution.py:321
  2.9 5.4 %collective-permute-start = (bf16[16,1152]{1,0:T(8,128)(2,1)S(1)}, bf16[16,1152]{1,0:T(8,128)(2,1)S(1)}, u32[]{:S(2)}, u32[]{:S(2)}) collective-permute-start(bf16[16,1152]{1,0:T(8,128)(2,1)S(1)} %get-tuple-element.27), channel_id=1, source_target_pairs={{0,28},{4,24},{8,20},{12,16},{16,12},{20,8},{24,4},{28,0},{1,29},{... | collective-permute-start | bytes 110600 | tf_op jit(solution)/shard_map/ppermute | solution.py:321
  6.5 5.2 %collective-permute-start.2 = (bf16[16,1152]{1,0:T(8,128)(2,1)S(1)}, bf16[16,1152]{1,0:T(8,128)(2,1)S(1)}, u32[]{:S(2)}, u32[]{:S(2)}) collective-permute-start(bf16[16,1152]{1,0:T(8,128)(2,1)S(1)} %get-tuple-element.26.refs_0_), channel_id=1, source_target_pairs={{0,12},{4,8},{8,4},{12,0},{16,28},{20,24},{24,20},{28,16},{1,13},{... | collective-permute-start | bytes 110600 | tf_op jit(solution)/shard_map/ppermute | solution.py:321
  6.7 5.0 %collective-permute-start.3 = (bf16[16,1152]{1,0:T(8,128)(2,1)S(1)}, bf16[16,1152]{1,0:T(8,128)(2,1)S(1)}, u32[]{:S(2)}, u32[]{:S(2)}) collective-permute-start(bf16[16,1152]{1,0:T(8,128)(2,1)S(1)} %get-tuple-element.27), channel_id=1, source_target_pairs={{0,20},{4,16},{8,28},{12,24},{16,4},{20,0},{24,12},{28,8},{1,21},{... | collective-permute-start | bytes 110600 | tf_op jit(solution)/shard_map/ppermute | solution.py:321
  9.0 5.0 %collective-permute-start.4 = (s16[16,1152]{1,0:T(8,128)(2,1)S(1)}, s16[16,1152]{1,0:T(8,128)(2,1)S(1)}, u32[]{:S(2)}, u32[]{:S(2)}) collective-permute-start(s16[16,1152]{1,0:T(8,128)(2,1)S(1)} %get-tuple-element.29.refs_0_.refs_1_), channel_id=1, source_target_pairs={{0,2},{1,3},{2,0},{3,1},{4,6},{5,7},{6,4},{7,5},{8,10},{9,11},{10,... | collective-permute-start | bytes 110600 | tf_op jit(solution)/shard_map/ppermute | solution.py:321
  12.4 4.0 %collective-permute-start.5 = (s16[16,1152]{1,0:T(8,128)(2,1)S(1)}, s16[16,1152]{1,0:T(8,128)(2,1)S(1)}, u32[]{:S(2)}, u32[]{:S(2)}) collective-permute-start(s16[16,1152]{1,0:T(8,128)(2,1)S(1)} %get-tuple-element.30.refs_0_.refs_1_), channel_id=1, source_target_pairs={{0,1},{1,0},{2,3},{3,2},{4,5},{5,4},{6,7},{7,6},{8,9},{9,8},{10,11... | collective-permute-start | bytes 110600 | tf_op jit(solution)/shard_map/ppermute | solution.py:321
  14.0 9.9 %collective-permute-start.8 = (bf16[32,1152]{1,0:T(8,128)(2,1)S(1)}, bf16[32,1152]{1,0:T(8,128)(2,1)S(1)}, u32[]{:S(2)}, u32[]{:S(2)}) collective-permute-start(bf16[32,1152]{1,0:T(8,128)(2,1)S(1)} %shard_map.94.refs_0_.refs_1_), channel_id=1, source_target_pairs={{0,4},{4,0},{1,5},{5,1},{2,6},{6,2},{3,7},{7,3},{8,12},{12,8},{9,1... | collective-permute-start | bytes 221192 | tf_op jit(solution)/shard_map/ppermute | solution.py:321
  14.2 4.9 %collective-permute-start.6 = (s16[16,1152]{1,0:T(8,128)(2,1)S(1)}, s16[16,1152]{1,0:T(8,128)(2,1)S(1)}, u32[]{:S(2)}, u32[]{:S(2)}) collective-permute-start(s16[16,1152]{1,0:T(8,128)(2,1)S(1)} %shard_map.98.refs_0_.refs_1_), channel_id=1, source_target_pairs={{0,1},{1,0},{2,3},{3,2},{4,5},{5,4},{6,7},{7,6},{8,9},{9,8},{10,11... | collective-permute-start | bytes 110600 | tf_op jit(solution)/shard_map/ppermute | solution.py:321
  15.8 9.6 %collective-permute-start.9 = (bf16[32,1152]{1,0:T(8,128)(2,1)S(1)}, bf16[32,1152]{1,0:T(8,128)(2,1)S(1)}, u32[]{:S(2)}, u32[]{:S(2)}) collective-permute-start(bf16[32,1152]{1,0:T(8,128)(2,1)S(1)} %shard_map.96.refs_1_.refs_2_), channel_id=1, source_target_pairs={{0,4},{4,0},{1,5},{5,1},{2,6},{6,2},{3,7},{7,3},{8,12},{12,8},{9,1... | collective-permute-start | bytes 221192 | tf_op jit(solution)/shard_map/ppermute | solution.py:321
  16.6 5.7 %collective-permute-start.10 = (s16[16,1152]{1,0:T(8,128)(2,1)S(1)}, s16[16,1152]{1,0:T(8,128)(2,1)S(1)}, u32[]{:S(2)}, u32[]{:S(2)}) collective-permute-start(s16[16,1152]{1,0:T(8,128)(2,1)S(1)} %shard_map.99.refs_0_.refs_1_), channel_id=1, source_target_pairs={{0,2},{1,3},{2,0},{3,1},{4,6},{5,7},{6,4},{7,5},{8,10},{9,11},{10,... | collective-permute-start | bytes 110600 | tf_op jit(solution)/shard_map/ppermute | solution.py:321
  19.6 5.8 %collective-permute-start.7 = (f32[8,1152]{1,0:T(8,128)S(1)}, f32[8,1152]{1,0:T(8,128)S(1)}, u32[]{:S(2)}, u32[]{:S(2)}) collective-permute-start(f32[8,1152]{1,0:T(8,128)S(1)} %get-tuple-element.32), channel_id=1, source_target_pairs={{0,28},{4,24},{8,20},{12,16},{16,12},{20,8},{24,4},{28,0},{1,29},{... | collective-permute-start | bytes 110600 | tf_op jit(solution)/shard_map/ppermute | solution.py:321
  22.7 2.6 %collective-permute-start.11 = (bf16[64,256]{1,0:T(8,128)(2,1)S(1)}, bf16[64,256]{1,0:T(8,128)(2,1)S(1)}, u32[]{:S(2)}, u32[]{:S(2)}) collective-permute-start(bf16[64,256]{1,0:T(8,128)(2,1)S(1)} %get-tuple-element.37), channel_id=1, source_target_pairs={{0,4},{4,0},{1,5},{5,1},{2,6},{6,2},{3,7},{7,3},{8,12},{12,8},{9,1... | collective-permute-start | bytes 98312 | tf_op jit(solution)/shard_map/ppermute | solution.py:321
  23.0 4.0 %collective-permute-start.12 = (bf16[8,1152]{1,0:T(8,128)(2,1)S(1)}, bf16[8,1152]{1,0:T(8,128)(2,1)S(1)}, u32[]{:S(2)}, u32[]{:S(2)}) collective-permute-start(bf16[8,1152]{1,0:T(8,128)(2,1)S(1)} %get-tuple-element.40), channel_id=1, source_target_pairs={{0,12},{4,8},{8,4},{12,0},{16,28},{20,24},{24,20},{28,16},{1,13},{... | collective-permute-start | bytes 55304 | tf_op jit(solution)/shard_map/ppermute | solution.py:321
  23.9 3.2 %collective-permute-start.13 = (bf16[8,1152]{1,0:T(8,128)(2,1)S(1)}, bf16[8,1152]{1,0:T(8,128)(2,1)S(1)}, u32[]{:S(2)}, u32[]{:S(2)}) collective-permute-start(bf16[8,1152]{1,0:T(8,128)(2,1)S(1)} %get-tuple-element.41), channel_id=1, source_target_pairs={{0,20},{4,16},{8,28},{12,24},{16,4},{20,0},{24,12},{28,8},{1,21},{... | collective-permute-start | bytes 55304 | tf_op jit(solution)/shard_map/ppermute | solution.py:321

commit v5 on v1

--- a/solution.py
+++ b/solution.py
@@ -162,9 +162,10 @@
 
 def join_kernel(*refs):
     *pieces, out_ref = refs
-    rows = pieces[0].shape[0]
-    for index, ref in enumerate(pieces):
-        out_ref[index * rows : (index + 1) * rows] = ref[...]
+    start = 0
+    for ref in pieces:
+        out_ref[start : start + ref.shape[0]] = ref[...]
+        start += ref.shape[0]
 
 
 def part_kernel(capacity, rows_ref, w_ref, w_other_ref, part_ref, gate_ref):
@@ -262,8 +263,8 @@
 
 
 def weight_kernel(capacity, *refs):
-    rows_refs, both_refs = refs[:4], refs[4:7]
-    w_in_hbm, w_out_hbm, written_ref, w_in_ref, w_out_ref, sems = refs[7:]
+    rows_refs, both_refs = refs[:2], refs[2:4]
+    w_in_hbm, w_out_hbm, written_ref, w_in_ref, w_out_ref, sems = refs[4:]
     feats, hidden = w_in_ref.shape
     rows = jnp.concatenate([ref[:, :feats] for ref in rows_refs], axis=0)
     both = jnp.concatenate([ref[...] for ref in both_refs], axis=0).astype(F32)
@@ -291,14 +292,14 @@
 
 
 def combine_kernel(steps, *refs):
-    kept_ref, came_refs = refs[0], refs[1:steps]
-    place_ref, spread_ref, tokens_ref, gate_out_ref = refs[steps:]
+    slot_refs = dict(zip(steps, refs))
+    place_ref, spread_ref, tokens_ref, gate_out_ref = refs[len(steps) :]
     feats = tokens_ref.shape[1]
-    capacity = kept_ref.shape[0]
-    came = [ref[...].astype(F32) for ref in came_refs]
-    half = steps // WINDOW
-    own = sum(came[: half - 1], kept_ref[...])
-    other = sum(came[half:], came[half - 1])
+    capacity = slot_refs[0].shape[0]
+    half = len(steps) // WINDOW
+    came = [slot_refs[step][...].astype(F32) for step in range(len(steps))]
+    own = sum(came[1:half], came[0])
+    other = sum(came[half + 1 :], came[half])
     slots = jnp.concatenate([own, other], axis=0)
     grads = slots[:, :feats]
     high = grads.astype(BF16)
@@ -325,11 +326,10 @@
     return swap(array, ("node", "local"), step * lax.axis_size("local") + 1)
 
 
-def join(pieces, after=()):
-    rows, wide = pieces[0].shape
-    rows *= len(pieces)
-    shape = jax.ShapeDtypeStruct((rows, wide), BF16)
-    return call(join_kernel, shape, 0, 4 * rows * wide, after=after)(*pieces)
+def join(pieces):
+    wide = pieces[0].shape[1]
+    rows = sum(piece.shape[0] for piece in pieces)
+    return call(join_kernel, jax.ShapeDtypeStruct((rows, wide), BF16), 0, 4 * rows * wide)(*pieces)
 
 
 def body(tokens, grad_out, routes, gates, w_in, w_out):
@@ -373,104 +373,82 @@
 
     other_weights = swap(weights, "local", 1)
 
-    half_nodes = nodes // WINDOW
-    pieces = [own_rows]
-    for step in range(1, nodes):
-        pieces.append(swap_nodes(own_rows if step < half_nodes else other_rows, step))
-    rows = half_nodes * (locals_ // 2) * capacity
-    last = ()
-    chains = []
-    held = []
-    for chunk in (pieces[:half_nodes], pieces[half_nodes:]):
-        chunk = join(chunk, last)
-        bit = 2
-        while bit < locals_:
-            chunk = join([chunk, swap(chunk, "local", bit)])
-            bit *= 2
-        held.append(chunk)
-        part, gate_rows = call(
-            functools.partial(part_kernel, capacity),
-            (shape((rows, coded), I16), shape((rows, LANES), F32)),
-            16 * rows * feats * hidden,
-            4 * rows * feats + 8 * feats * hidden,
-            after=last,
-        )(chunk, weights, other_weights)
-        last = (part,)
-        chains.append((part, swap(part, "edata", 1), gate_rows))
+    quarter = nodes // 4
+    far = [*range(quarter), *range(nodes - quarter, nodes)]
+    steps = [*far, *range(quarter, nodes - quarter)]
+    pieces = [
+        swap_nodes(own_rows if step < nodes // WINDOW else other_rows, step) if step else own_rows
+        for step in steps
+    ]
+    held = join([join(pieces[: len(far)]), *pieces[len(far) :]])
     bit = 2
-    while bit < edatas:
-        for index, (part, other, gate_rows) in enumerate(chains):
-            part = call(
-                add_codes_kernel,
-                shape((rows, coded), I16),
-                16 * rows * hidden,
-                6 * rows * coded,
-                after=last,
-            )(part, other)
-            last = (part,)
-            chains[index] = (part, swap(part, "edata", bit), gate_rows)
+    while bit < locals_:
+        held = join([held, swap(held, "local", bit)])
         bit *= 2
-
-    mine = []
-    theirs = ()
-    slots_back = []
-    for index, (part, other, gate_rows) in enumerate(chains):
-        dealt = [shape((capacity, wide), BF16 if index else F32)] * half_nodes
-        own, packed, *slot_parts = call(
-            functools.partial(slot_kernel, capacity, len(theirs)),
-            [
-                shape((2 * rows, hidden), BF16),
-                shape(((1 + len(theirs)) * 2 * rows, hidden), BF16),
-                *(dealt if locals_ == 2 else [shape((rows, wide), F32)]),
-            ],
-            4 * rows * feats * hidden,
-            4 * feats * hidden + 4 * rows * feats,
-            after=last,
-        )(part, other, gate_rows, weights, other_weights, *theirs)
-        last = (own,)
-        mine.append(own)
-        theirs = (packed,)
-        if locals_ > 2:
-            half = rows // 2
-            keep, send = slot_parts[0][:half], slot_parts[0][half:]
-            bit = locals_ // 2
-            while bit > 2:
-                half //= 2
-                keep, send = call(
-                    halve_kernel,
-                    (shape((half, wide), F32),) * 2,
-                    4 * half * wide,
-                    24 * half * wide,
-                )(keep, swap(send, "local", bit))
-                bit //= 2
-            slot_parts = call(deal_kernel, dealt, 4 * half * wide, 12 * half * wide)(
-                keep, swap(send, "local", bit)
-            )
-        for step, send in enumerate(slot_parts, index * half_nodes):
-            slots_back.append(swap_nodes(send, step) if step else send)
-    came = [swap(chunk, "local", 1) for chunk in held]
-    back = swap(theirs[0], "local", 1)
+    rows = nodes * (locals_ // 2) * capacity
+    part, gate_rows = call(
+        functools.partial(part_kernel, capacity),
+        (shape((rows, coded), I16), shape((rows, LANES), F32)),
+        16 * rows * feats * hidden,
+        4 * rows * feats + 8 * feats * hidden,
+    )(held, weights, other_weights)
+    bit = edatas // 2
+    other = swap(part, "edata", bit)
+    came = swap(held, "local", 1)
+    while bit > 1:
+        part = call(
+            add_codes_kernel, shape((rows, coded), I16), 16 * rows * hidden, 6 * rows * coded
+        )(part, other)
+        bit //= 2
+        other = swap(part, "edata", bit)
+
+    dealt = [shape((capacity, wide), BF16 if step else F32) for step in steps]
+    mine, theirs, *slot_parts = call(
+        functools.partial(slot_kernel, capacity, 0),
+        [
+            *[shape((2 * rows, hidden), BF16)] * 2,
+            *(dealt if locals_ == 2 else [shape((rows, wide), F32)]),
+        ],
+        4 * rows * feats * hidden,
+        4 * feats * hidden + 4 * rows * feats,
+    )(part, other, gate_rows, weights, other_weights)
+    if locals_ > 2:
+        half = rows // 2
+        keep, send = slot_parts[0][:half], slot_parts[0][half:]
+        bit = locals_ // 2
+        while bit > 2:
+            half //= 2
+            keep, send = call(
+                halve_kernel, (shape((half, wide), F32),) * 2, 4 * half * wide, 24 * half * wide
+            )(keep, swap(send, "local", bit))
+            bit //= 2
+        slot_parts = call(deal_kernel, dealt, 4 * half * wide, 12 * half * wide)(
+            keep, swap(send, "local", bit)
+        )
+    returned = [
+        swap_nodes(send, step) if step else send for step, send in zip(steps, slot_parts)
+    ]
+    back = swap(theirs, "local", 1)
     grad_w_in, grad_w_out, written = call(
         functools.partial(weight_kernel, capacity),
         (shape((feats, hidden), F32), shape((hidden, feats), F32), shape((8, LANES), F32)),
-        32 * rows * feats * hidden,
+        16 * rows * feats * hidden,
         8 * feats * hidden,
-        in_specs=[vmem] * 7,
-        after=slots_back[1:half_nodes],
+        in_specs=[vmem] * 4,
         out_specs=[hbm, hbm, vmem],
         scratch_shapes=[
             pltpu.VMEM((feats, hidden), F32),
             pltpu.VMEM((hidden, feats), F32),
             pltpu.SemaphoreType.DMA((2 * PIECES,)),
         ],
-    )(*held, *came, *mine, back)
+    )(held, came, mine, back)
     grad_tokens, grad_gates = call(
-        functools.partial(combine_kernel, nodes),
+        functools.partial(combine_kernel, steps),
         (shape((tok_rows, feats), BF16), shape((2, tok_rows), F32)),
         4 * slots * tok_rows * feats,
         2 * tok_rows * feats,
         after=(written,),
-    )(*slots_back[:half_nodes], *reversed(slots_back[half_nodes:]), place, spread)
+    )(*returned, place, spread)
     return (grad_tokens, grad_gates.T, grad_w_in, grad_w_out)
 
 

time: 28.7 us -> 29.5 us (1.028)
  waiting for transfers between devices: 5.35 us -> 11.5 us
  starting transfers between devices: 15.5 us -> 11.3 us
  Pallas kernels: 7.01 us -> 5.84 us
    ppermute x14 -> x11, waiting for transfers between devices: 5.35 us -> 11.5 us  [swap(): lax.ppermute(array, axes, [(index, index ^ bit) for index in range(size)])]
    ppermute x14 -> x11, starting transfers between devices: 15.5 us -> 11.3 us  [swap(): lax.ppermute(array, axes, [(index, index ^ bit) for index in range(size)])]
    pallas_call x11 -> x8, Pallas kernels: 7.01 us -> 5.84 us  [run(): pl.pallas_call(lambda *refs: kernel(*refs[len(after):]), out_shape=out_sh...]
  transfers between devices with their start and end apart: 14 -> 11, of which waited for: 6 -> 6; matrix products, arithmetic and copies ran while one was open for 0% -> 0% of each run, Pallas kernels for 15% -> 8%
where the time goes in v5:
time: 29.5 us; the launch traced here: 29.4 us
  waiting for transfers between devices  11.5 us (39%)
  starting transfers between devices  11.3 us (38%)
  Pallas kernels  5.84 us (20%)
  between operations  0.71 us (2%)
    ppermute x11, waiting for transfers between devices, swap(): lax.ppermute(array, axes, [(index, index ^ bit) for index in range(size)])  11.5 us
    ppermute x11, starting transfers between devices, swap(): lax.ppermute(array, axes, [(index, index ^ bit) for index in range(size)])  11.3 us
    pallas_call x8, Pallas kernels, run(): pl.pallas_call(lambda *refs: kernel(*refs[len(after):]), out_shape=out_sh...  5.84 us
  transfers between devices with their start and end apart: 11, of which 6 were waited for; matrix products, arithmetic and copies ran while one was open for 0% of the time, Pallas kernels for 8%

profile of v5, /device:TPU:0, one launch (start us, length us, event | category | flops | bytes accessed | tf_op | source)
XLA Modules:
  0.0 29.4 jit_solution(3378651550803925266)
XLA Ops:
  0.6 1.8 %shard_map.93 = (bf16[16,1152]{1,0:T(8,128)(2,1)S(1)}, bf16[16,1152]{1,0:T(8,128)(2,1)S(1)}, bf16[32,256]{1,0:T(8,128)(2,1)S(1)}, bf16[256,32]{1,0:T(8,128)(2,1)S(1)}, bf16[512,1024]{1,0:T(8,128)(2,1)S(1)}) custom-call(s32[2,256]{1,0:T(2,128)} %bitcast.3, bf16[2,256]{1,0:T(2,128)(2,1)} %bitcast.4, bf16[256,1024]{1,0:T(8,128)(2,1)} %refs_2_.1, ...), custom_call_target="tpu_custom_call" | custom-call | flops 16777216 | bytes 2097152 | tf_op jit(solution)/shard_map/pallas_call | solution.py:38
  2.4 0.5 %collective-permute-start.4 = (bf16[512,1024]{1,0:T(8,128)(2,1)S(1)}, bf16[512,1024]{1,0:T(8,128)(2,1)S(1)}, u32[]{:S(2)}, u32[]{:S(2)}) collective-permute-start(bf16[512,1024]{1,0:T(8,128)(2,1)S(1)} %get-tuple-element.24.refs_1_.refs_3_), channel_id=1, source_target_pairs={{0,4},{4,0},{1,5},{5,1},{2,6},{6,2},{3,7},{7,3},{8,12},{12,8},{9,1... | collective-permute-start | bytes 3145736 | tf_op jit(solution)/shard_map/ppermute | solution.py:322
  2.9 3.6 %collective-permute-start = (bf16[16,1152]{1,0:T(8,128)(2,1)S(1)}, bf16[16,1152]{1,0:T(8,128)(2,1)S(1)}, u32[]{:S(2)}, u32[]{:S(2)}) collective-permute-start(bf16[16,1152]{1,0:T(8,128)(2,1)S(1)} %get-tuple-element.23), channel_id=1, source_target_pairs={{0,28},{4,24},{8,20},{12,16},{16,12},{20,8},{24,4},{28,0},{1,29},{... | collective-permute-start | bytes 110600 | tf_op jit(solution)/shard_map/ppermute | solution.py:322
  6.5 0.2 collective-permute-start.1
  6.7 0.1 collective-permute-start.2
  6.8 1.5 %collective-permute-done.refs_1_ = bf16[16,1152]{1,0:T(8,128)(2,1)S(1)} collective-permute-done((bf16[16,1152]{1,0:T(8,128)(2,1)S(1)}, bf16[16,1152]{1,0:T(8,128)(2,1)S(1)}, u32[]{:S(2)}, u32[]{:S(2)}) %collective-permute-start) | collective-permute-done | bytes 36896 | tf_op jit(solution)/shard_map/ppermute | solution.py:322
  8.3 1.7 %collective-permute-done.1.refs_1_ = bf16[16,1152]{1,0:T(8,128)(2,1)S(1)} collective-permute-done((bf16[16,1152]{1,0:T(8,128)(2,1)S(1)}, bf16[16,1152]{1,0:T(8,128)(2,1)S(1)}, u32[]{:S(2)}, u32[]{:S(2)}) %collective-permute-start.1) | collective-permute-done | bytes 36896 | tf_op jit(solution)/shard_map/ppermute | solution.py:322
  10.0 0.1 collective-permute-done.2.refs_2_
  10.1 0.0 collective-permute-done.4.refs_2_.refs_4_
  10.1 0.7 %shard_map.96 = (s16[32,1152]{1,0:T(8,128)(2,1)S(1)}, f32[32,128]{1,0:T(8,128)S(1)}) custom-call(bf16[64,1152]{1,0:T(8,128)(2,1)S(1)} %shard_map.95.refs_0_, bf16[512,1024]{1,0:T(8,128)(2,1)S(1)} %get-tuple-element.24.refs_1_.refs_3_, bf16[512,1024]{1,0:T(8,128)(2,1)S(1)} %collective-permute-done.4.refs_2_.refs_4_), custom_call_target="tpu_custom_call" | custom-call | flops 134217728 | bytes 2228224 | tf_op jit(solution)/shard_map/pallas_call | solution.py:38
  10.8 2.6 %collective-permute-start.5 = (s16[32,1152]{1,0:T(8,128)(2,1)S(1)}, s16[32,1152]{1,0:T(8,128)(2,1)S(1)}, u32[]{:S(2)}, u32[]{:S(2)}) collective-permute-start(s16[32,1152]{1,0:T(8,128)(2,1)S(1)} %get-tuple-element.25.refs_0_), channel_id=1, source_target_pairs={{0,2},{1,3},{2,0},{3,1},{4,6},{5,7},{6,4},{7,5},{8,10},{9,11},{10,... | collective-permute-start | bytes 221192 | tf_op jit(solution)/shard_map/ppermute | solution.py:322
  13.5 0.2 collective-permute-start.3
  13.6 4.3 %collective-permute-done.5.refs_1_ = s16[32,1152]{1,0:T(8,128)(2,1)S(1)} collective-permute-done((s16[32,1152]{1,0:T(8,128)(2,1)S(1)}, s16[32,1152]{1,0:T(8,128)(2,1)S(1)}, u32[]{:S(2)}, u32[]{:S(2)}) %collective-permute-start.5) | collective-permute-done | bytes 73760 | tf_op jit(solution)/shard_map/ppermute | solution.py:322
  18.0 0.2 shard_map.97.refs_0_
  18.2 0.8 %collective-permute-start.6 = (s16[32,1152]{1,0:T(8,128)(2,1)S(1)}, s16[32,1152]{1,0:T(8,128)(2,1)S(1)}, u32[]{:S(2)}, u32[]{:S(2)}) collective-permute-start(s16[32,1152]{1,0:T(8,128)(2,1)S(1)} %shard_map.97.refs_0_), channel_id=1, source_target_pairs={{0,1},{1,0},{2,3},{3,2},{4,5},{5,4},{6,7},{7,6},{8,9},{9,8},{10,11... | collective-permute-start | bytes 221192 | tf_op jit(solution)/shard_map/ppermute | solution.py:322
  18.9 3.7 %collective-permute-done.6.refs_1_ = s16[32,1152]{1,0:T(8,128)(2,1)S(1)} collective-permute-done((s16[32,1152]{1,0:T(8,128)(2,1)S(1)}, s16[32,1152]{1,0:T(8,128)(2,1)S(1)}, u32[]{:S(2)}, u32[]{:S(2)}) %collective-permute-start.6) | collective-permute-done | bytes 73760 | tf_op jit(solution)/shard_map/ppermute | solution.py:322
  22.6 0.5 %shard_map.98 = (bf16[64,256]{1,0:T(8,128)(2,1)S(1)}, bf16[64,256]{1,0:T(8,128)(2,1)S(1)}, f32[8,1152]{1,0:T(8,128)S(1)}, bf16[8,1152]{1,0:T(8,128)(2,1)S(1)}, b...) custom-call(s16[32,1152]{1,0:T(8,128)(2,1)S(1)} %shard_map.97.refs_0_, ...), custom_call_target="tpu_custom_call" | custom-call | flops 33554432 | bytes 1179648 | tf_op jit(solution)/shard_map/pallas_call | solution.py:38
  23.1 0.0 collective-permute-start.7
  23.1 1.6 %collective-permute-start.8 = (bf16[8,1152]{1,0:T(8,128)(2,1)S(1)}, bf16[8,1152]{1,0:T(8,128)(2,1)S(1)}, u32[]{:S(2)}, u32[]{:S(2)}) collective-permute-start(bf16[8,1152]{1,0:T(8,128)(2,1)S(1)} %get-tuple-element.31), channel_id=1, source_target_pairs={{0,28},{4,24},{8,20},{12,16},{16,12},{20,8},{24,4},{28,0},{1,29},{... | collective-permute-start | bytes 55304 | tf_op jit(solution)/shard_map/ppermute | solution.py:322
  24.7 0.4 %collective-permute-start.9 = (bf16[8,1152]{1,0:T(8,128)(2,1)S(1)}, bf16[8,1152]{1,0:T(8,128)(2,1)S(1)}, u32[]{:S(2)}, u32[]{:S(2)}) collective-permute-start(bf16[8,1152]{1,0:T(8,128)(2,1)S(1)} %get-tuple-element.32), channel_id=1, source_target_pairs={{0,12},{4,8},{8,4},{12,0},{16,28},{20,24},{24,20},{28,16},{1,13},{... | collective-permute-start | bytes 55304 | tf_op jit(solution)/shard_map/ppermute | solution.py:322
  25.1 1.3 %collective-permute-start.10 = (bf16[8,1152]{1,0:T(8,128)(2,1)S(1)}, bf16[8,1152]{1,0:T(8,128)(2,1)S(1)}, u32[]{:S(2)}, u32[]{:S(2)}) collective-permute-start(bf16[8,1152]{1,0:T(8,128)(2,1)S(1)} %get-tuple-element.33), channel_id=1, source_target_pairs={{0,20},{4,16},{8,28},{12,24},{16,4},{20,0},{24,12},{28,8},{1,21},{... | collective-permute-start | bytes 55304 | tf_op jit(solution)/shard_map/ppermute | solution.py:322
  26.4 0.0 collective-permute-done.3.refs_1_
  26.4 0.0 collective-permute-done.7.refs_3_
  26.4 1.6 %shard_map.99 = (f32[1024,256]{1,0:T(8,128)}, f32[256,1024]{1,0:T(8,128)}, f32[8,128]{1,0:T(8,128)S(1)}) custom-call(bf16[64,1152]{1,0:T(8,128)(2,1)S(1)} %shard_map.95.refs_0_, bf16[64,1152]{1,0:T(8,128)(2,1)S(1)} %collective-permute-done.3.refs_1_, bf16[64,256]{1,0:T(8,128)(2,1)S(1)} %get-tuple-element.27.refs_2_, ...), custom_call_target="tpu_custom_call" | custom-call | flops 134217728 | bytes 2097152 | tf_op jit(solution)/shard_map/pallas_call | solution.py:38
  28.1 0.0 collective-permute-done.8.refs_2_
  28.1 0.0 collective-permute-done.9.refs_3_
  28.1 0.2 collective-permute-done.10.refs_4_
  28.3 1.1 %shard_map.100 = (bf16[256,1024]{1,0:T(8,128)(2,1)}, f32[2,256]{1,0:T(2,128)}) custom-call(f32[8,128]{1,0:T(8,128)S(1)} %get-tuple-element.29.refs_0_, f32[8,1152]{1,0:T(8,128)S(1)} %get-tuple-element.30.refs_1_, bf16[8,1152]{1,0:T(8,128)(2,1)S(1)} %collective-permute-done.8.refs_2_, bf16[8,1152]{1,0:T(8,128)(2,1)S(1)} %collective-permute-done.9.refs_3_, ...), custom_call_target="tpu_custom_call" | custom-call | flops 16777216 | bytes 524288 | tf_op jit(solution)/shard_map/pallas_call | solution.py:38
  (2 shorter events, 0.0 us)
Async XLA Ops:
  2.4 7.7 %collective-permute-start.4 = (bf16[512,1024]{1,0:T(8,128)(2,1)S(1)}, bf16[512,1024]{1,0:T(8,128)(2,1)S(1)}, u32[]{:S(2)}, u32[]{:S(2)}) collective-permute-start(bf16[512,1024]{1,0:T(8,128)(2,1)S(1)} %get-tuple-element.24.refs_1_.refs_3_), channel_id=1, source_target_pairs={{0,4},{4,0},{1,5},{5,1},{2,6},{6,2},{3,7},{7,3},{8,12},{12,8},{9,1... | collective-permute-start | bytes 3145736 | tf_op jit(solution)/shard_map/ppermute | solution.py:322
  2.9 5.4 %collective-permute-start = (bf16[16,1152]{1,0:T(8,128)(2,1)S(1)}, bf16[16,1152]{1,0:T(8,128)(2,1)S(1)}, u32[]{:S(2)}, u32[]{:S(2)}) collective-permute-start(bf16[16,1152]{1,0:T(8,128)(2,1)S(1)} %get-tuple-element.23), channel_id=1, source_target_pairs={{0,28},{4,24},{8,20},{12,16},{16,12},{20,8},{24,4},{28,0},{1,29},{... | collective-permute-start | bytes 110600 | tf_op jit(solution)/shard_map/ppermute | solution.py:322
  6.5 3.5 %collective-permute-start.1 = (bf16[16,1152]{1,0:T(8,128)(2,1)S(1)}, bf16[16,1152]{1,0:T(8,128)(2,1)S(1)}, u32[]{:S(2)}, u32[]{:S(2)}) collective-permute-start(bf16[16,1152]{1,0:T(8,128)(2,1)S(1)} %get-tuple-element.22.refs_0_), channel_id=1, source_target_pairs={{0,12},{4,8},{8,4},{12,0},{16,28},{20,24},{24,20},{28,16},{1,13},{... | collective-permute-start | bytes 110600 | tf_op jit(solution)/shard_map/ppermute | solution.py:322
  6.7 3.4 %collective-permute-start.2 = (bf16[16,1152]{1,0:T(8,128)(2,1)S(1)}, bf16[16,1152]{1,0:T(8,128)(2,1)S(1)}, u32[]{:S(2)}, u32[]{:S(2)}) collective-permute-start(bf16[16,1152]{1,0:T(8,128)(2,1)S(1)} %get-tuple-element.23), channel_id=1, source_target_pairs={{0,20},{4,16},{8,28},{12,24},{16,4},{20,0},{24,12},{28,8},{1,21},{... | collective-permute-start | bytes 110600 | tf_op jit(solution)/shard_map/ppermute | solution.py:322
  10.8 7.2 %collective-permute-start.5 = (s16[32,1152]{1,0:T(8,128)(2,1)S(1)}, s16[32,1152]{1,0:T(8,128)(2,1)S(1)}, u32[]{:S(2)}, u32[]{:S(2)}) collective-permute-start(s16[32,1152]{1,0:T(8,128)(2,1)S(1)} %get-tuple-element.25.refs_0_), channel_id=1, source_target_pairs={{0,2},{1,3},{2,0},{3,1},{4,6},{5,7},{6,4},{7,5},{8,10},{9,11},{10,... | collective-permute-start | bytes 221192 | tf_op jit(solution)/shard_map/ppermute | solution.py:322
  13.5 13.0 %collective-permute-start.3 = (bf16[64,1152]{1,0:T(8,128)(2,1)S(1)}, bf16[64,1152]{1,0:T(8,128)(2,1)S(1)}, u32[]{:S(2)}, u32[]{:S(2)}) collective-permute-start(bf16[64,1152]{1,0:T(8,128)(2,1)S(1)} %shard_map.95.refs_0_), channel_id=1, source_target_pairs={{0,4},{4,0},{1,5},{5,1},{2,6},{6,2},{3,7},{7,3},{8,12},{12,8},{9,1... | collective-permute-start | bytes 442376 | tf_op jit(solution)/shard_map/ppermute | solution.py:322
  18.2 4.4 %collective-permute-start.6 = (s16[32,1152]{1,0:T(8,128)(2,1)S(1)}, s16[32,1152]{1,0:T(8,128)(2,1)S(1)}, u32[]{:S(2)}, u32[]{:S(2)}) collective-permute-start(s16[32,1152]{1,0:T(8,128)(2,1)S(1)} %shard_map.97.refs_0_), channel_id=1, source_target_pairs={{0,1},{1,0},{2,3},{3,2},{4,5},{5,4},{6,7},{7,6},{8,9},{9,8},{10,11... | collective-permute-start | bytes 221192 | tf_op jit(solution)/shard_map/ppermute | solution.py:322
  23.1 3.4 %collective-permute-start.7 = (bf16[64,256]{1,0:T(8,128)(2,1)S(1)}, bf16[64,256]{1,0:T(8,128)(2,1)S(1)}, u32[]{:S(2)}, u32[]{:S(2)}) collective-permute-start(bf16[64,256]{1,0:T(8,128)(2,1)S(1)} %get-tuple-element.28), channel_id=1, source_target_pairs={{0,4},{4,0},{1,5},{5,1},{2,6},{6,2},{3,7},{7,3},{8,12},{12,8},{9,1... | collective-permute-start | bytes 98312 | tf_op jit(solution)/shard_map/ppermute | solution.py:322
  23.1 5.0 %collective-permute-start.8 = (bf16[8,1152]{1,0:T(8,128)(2,1)S(1)}, bf16[8,1152]{1,0:T(8,128)(2,1)S(1)}, u32[]{:S(2)}, u32[]{:S(2)}) collective-permute-start(bf16[8,1152]{1,0:T(8,128)(2,1)S(1)} %get-tuple-element.31), channel_id=1, source_target_pairs={{0,28},{4,24},{8,20},{12,16},{16,12},{20,8},{24,4},{28,0},{1,29},{... | collective-permute-start | bytes 55304 | tf_op jit(solution)/shard_map/ppermute | solution.py:322
  24.7 3.3 %collective-permute-start.9 = (bf16[8,1152]{1,0:T(8,128)(2,1)S(1)}, bf16[8,1152]{1,0:T(8,128)(2,1)S(1)}, u32[]{:S(2)}, u32[]{:S(2)}) collective-permute-start(bf16[8,1152]{1,0:T(8,128)(2,1)S(1)} %get-tuple-element.32), channel_id=1, source_target_pairs={{0,12},{4,8},{8,4},{12,0},{16,28},{20,24},{24,20},{28,16},{1,13},{... | collective-permute-start | bytes 55304 | tf_op jit(solution)/shard_map/ppermute | solution.py:322
  25.1 3.2 %collective-permute-start.10 = (bf16[8,1152]{1,0:T(8,128)(2,1)S(1)}, bf16[8,1152]{1,0:T(8,128)(2,1)S(1)}, u32[]{:S(2)}, u32[]{:S(2)}) collective-permute-start(bf16[8,1152]{1,0:T(8,128)(2,1)S(1)} %get-tuple-element.33), channel_id=1, source_target_pairs={{0,20},{4,16},{8,28},{12,24},{16,4},{20,0},{24,12},{28,8},{1,21},{... | collective-permute-start | bytes 55304 | tf_op jit(solution)/shard_map/ppermute | solution.py:322

commit v6 on v2

--- a/solution.py
+++ b/solution.py
@@ -91,8 +91,7 @@
 
 
 def gather_kernel(routes_hbm, gates_hbm, tokens_hbm, grads_hbm, w_in_hbm, w_out_hbm, own_ref,
-                  other_ref, place_ref, spread_ref, w_ref, routes_ref, gates_ref, tokens_ref,
-                  grads_ref, sems):
+                  other_ref, place_ref, routes_ref, w_ref, gates_ref, tokens_ref, grads_ref, sems):
     tok_rows, feats = tokens_ref.shape
     capacity = own_ref.shape[0] // 2
     slots = WINDOW * capacity
@@ -136,14 +135,7 @@
     before = jnp.dot(names, earlier, preferred_element_type=F32)
     parts = [jnp.where(before[e : e + 1] == slot_of, named[e], 0.0) for e in range(WINDOW)]
     place = jnp.concatenate(parts, axis=0).astype(BF16)
-    place_ref[:slots] = place
-    spread_ref[...] = jnp.concatenate(parts + parts, axis=0).T.astype(BF16)
-    masks = jnp.zeros((16, tok_rows), F32)
-    row_of = lax.broadcasted_iota(jnp.int32, masks.shape, 0)
-    for index, hit in enumerate(hits):
-        for k in range(2):
-            masks = jnp.where(row_of == 2 * index + k, hit[k : k + 1], masks)
-    place_ref[slots:] = masks.astype(BF16)
+    place_ref[...] = place
     for copy in copies[2 : 2 + PIECES]:
         copy.wait()
     rows_x = jnp.dot(place, tokens_ref[...], preferred_element_type=F32)
@@ -158,6 +150,15 @@
         out_ref[:, feats:] = jnp.broadcast_to(gate, (2 * capacity, LANES)).astype(BF16)
     for copy in copies[2 + 2 * PIECES :]:
         copy.wait()
+
+
+def plan_kernel(place_ref, routes_ref, spread_ref, masks_ref):
+    place = place_ref[...].astype(F32)
+    spread_ref[...] = jnp.concatenate([place, place], axis=0).T.astype(BF16)
+    routes = routes_ref[...]
+    own = own_expert()
+    for index, expert in enumerate((own, 1 - own)):
+        masks_ref[2 * index : 2 * index + 2] = (routes == expert).astype(F32)
 
 
 def join_kernel(*refs):
@@ -292,7 +293,7 @@
 
 def combine_kernel(steps, *refs):
     kept_ref, came_refs = refs[0], refs[1:steps]
-    place_ref, spread_ref, tokens_ref, gate_out_ref = refs[steps:]
+    place_ref, spread_ref, masks_ref, tokens_ref, gate_out_ref = refs[steps:]
     feats = tokens_ref.shape[1]
     capacity = kept_ref.shape[0]
     came = [ref[...].astype(F32) for ref in came_refs]
@@ -306,8 +307,8 @@
     both = jnp.concatenate([high, low], axis=0)
     tokens_ref[...] = jnp.dot(spread_ref[...], both, preferred_element_type=F32).astype(BF16)
     slot_gate = jnp.sum(slots[:, feats:], axis=1, keepdims=True)
-    picked = place_ref[: WINDOW * capacity].astype(F32) * slot_gate
-    masks = place_ref[WINDOW * capacity :].astype(F32)
+    picked = place_ref[...].astype(F32) * slot_gate
+    masks = masks_ref[...]
     result = jnp.zeros(gate_out_ref.shape, F32)
     for index in range(WINDOW):
         span = slice(index * capacity, (index + 1) * capacity)
@@ -350,20 +351,19 @@
         pltpu.with_memory_space_constraint(value, pltpu.HBM)
         for value in (routes.T, gates.T, tokens, grad_out, w_in, w_out)
     ]
-    own_rows, other_rows, place, spread, weights = call(
+    own_rows, other_rows, place, routes, weights = call(
         gather_kernel,
         (
             pltpu.VMEM((2 * capacity, wide), BF16),
             pltpu.VMEM((2 * capacity, wide), BF16),
-            pltpu.VMEM((slots + 16, tok_rows), BF16),
-            pltpu.VMEM((tok_rows, 2 * slots), BF16),
+            pltpu.VMEM((slots, tok_rows), BF16),
+            pltpu.VMEM((2, tok_rows), jnp.int32),
             pltpu.VMEM((2 * hidden, feats), BF16),
         ),
         4 * slots * tok_rows * feats,
         4 * tok_rows * feats + 4 * hidden * feats,
         in_specs=[hbm] * 6,
         scratch_shapes=[
-            pltpu.VMEM((2, tok_rows), jnp.int32),
             pltpu.VMEM((2, tok_rows), BF16),
             pltpu.VMEM((tok_rows, feats), BF16),
             pltpu.VMEM((tok_rows, feats), BF16),
@@ -428,6 +428,15 @@
             after=last,
         )(part, other, gate_rows, weights, other_weights, *theirs)
         last = (own,)
+        if index == 0:
+            spread, masks = call(
+                plan_kernel,
+                (shape((tok_rows, 2 * slots), BF16), shape((2 * WINDOW, tok_rows), F32)),
+                0,
+                8 * slots * tok_rows,
+                after=last,
+            )(place, routes)
+            last = (spread,)
         mine.append(own)
         theirs = (packed,)
         if locals_ > 2:
@@ -470,7 +479,7 @@
         4 * slots * tok_rows * feats,
         2 * tok_rows * feats,
         after=(written,),
-    )(*slots_back[:half_nodes], *reversed(slots_back[half_nodes:]), place, spread)
+    )(*slots_back[:half_nodes], *reversed(slots_back[half_nodes:]), place, spread, masks)
     return (grad_tokens, grad_gates.T, grad_w_in, grad_w_out)
 
 

time: 28 us -> 28 us (level)
    pallas_call x11 -> x12, Pallas kernels: 7.01 us -> 7.13 us  [run(): pl.pallas_call(lambda *refs: kernel(*refs[len(after):]), out_shape=out_sh...]
where the time goes in v6:
time: 28 us; the launch traced here: 27.8 us
  starting transfers between devices  15.4 us (55%)
  Pallas kernels  7.13 us (25%)
  waiting for transfers between devices  4.56 us (16%)
  between operations  0.71 us (3%)
    ppermute x14, starting transfers between devices, swap(): lax.ppermute(array, axes, [(index, index ^ bit) for index in range(size)])  15.4 us
    pallas_call x12, Pallas kernels, run(): pl.pallas_call(lambda *refs: kernel(*refs[len(after):]), out_shape=out_sh...  7.13 us
    ppermute x14, waiting for transfers between devices, swap(): lax.ppermute(array, axes, [(index, index ^ bit) for index in range(size)])  4.56 us
  transfers between devices with their start and end apart: 14, of which 6 were waited for; matrix products, arithmetic and copies ran while one was open for 0% of the time, Pallas kernels for 15%

profile of v6, /device:TPU:0, one launch (start us, length us, event | category | flops | bytes accessed | tf_op | source)
XLA Modules:
  0.0 27.8 jit_solution(6673602620276625265)
XLA Ops:
  0.6 1.8 %shard_map.93 = (bf16[16,1152]{1,0:T(8,128)(2,1)S(1)}, bf16[16,1152]{1,0:T(8,128)(2,1)S(1)}, bf16[16,256]{1,0:T(8,128)(2,1)S(1)}, s32[2,256]{1,0:T(2,128)S(1)}, bf16[512,1024]{1,0:T(8,128)(2,1)S(1)}) custom-call(s32[2,256]{1,0:T(2,128)} %bitcast.3, bf16[2,256]{1,0:T(2,128)(2,1)} %bitcast.4, bf16[256,1024]{1,0:T(8,128)(2,1)} %refs_2_.1, ...), custom_call_target="tpu_custom_call" | custom-call | flops 16777216 | bytes 2097152 | tf_op jit(solution)/shard_map/pallas_call | solution.py:38
  2.4 0.5 %collective-permute-start.1 = (bf16[512,1024]{1,0:T(8,128)(2,1)S(1)}, bf16[512,1024]{1,0:T(8,128)(2,1)S(1)}, u32[]{:S(2)}, u32[]{:S(2)}) collective-permute-start(bf16[512,1024]{1,0:T(8,128)(2,1)S(1)} %get-tuple-element.29.refs_1_.refs_2_.refs_4_), channel_id=1, source_target_pairs={{0,4},{4,0},{1,5},{5,1},{2,6},{6,2},{3,7},{7,3},{8,12},{12,8},{9,1... | collective-permute-start | bytes 3145736 | tf_op jit(solution)/shard_map/ppermute | solution.py:322
  2.9 2.6 %collective-permute-start = (bf16[16,1152]{1,0:T(8,128)(2,1)S(1)}, bf16[16,1152]{1,0:T(8,128)(2,1)S(1)}, u32[]{:S(2)}, u32[]{:S(2)}) collective-permute-start(bf16[16,1152]{1,0:T(8,128)(2,1)S(1)} %get-tuple-element.28.refs_0_), channel_id=1, source_target_pairs={{0,12},{4,8},{8,4},{12,0},{16,28},{20,24},{24,20},{28,16},{1,13},{... | collective-permute-start | bytes 110600 | tf_op jit(solution)/shard_map/ppermute | solution.py:322
  5.5 1.2 %collective-permute-start.3 = (bf16[16,1152]{1,0:T(8,128)(2,1)S(1)}, bf16[16,1152]{1,0:T(8,128)(2,1)S(1)}, u32[]{:S(2)}, u32[]{:S(2)}) collective-permute-start(bf16[16,1152]{1,0:T(8,128)(2,1)S(1)} %get-tuple-element.31), channel_id=1, source_target_pairs={{0,28},{4,24},{8,20},{12,16},{16,12},{20,8},{24,4},{28,0},{1,29},{... | collective-permute-start | bytes 110600 | tf_op jit(solution)/shard_map/ppermute | solution.py:322
  6.7 0.1 collective-permute-start.2
  6.7 0.5 %collective-permute-done.refs_1_ = bf16[16,1152]{1,0:T(8,128)(2,1)S(1)} collective-permute-done((bf16[16,1152]{1,0:T(8,128)(2,1)S(1)}, bf16[16,1152]{1,0:T(8,128)(2,1)S(1)}, u32[]{:S(2)}, u32[]{:S(2)}) %collective-permute-start) | collective-permute-done | bytes 36896 | tf_op jit(solution)/shard_map/ppermute | solution.py:322
  7.3 0.0 collective-permute-done.1.refs_2_.refs_3_.refs_5_
  7.3 0.7 %shard_map.95 = (s16[16,1152]{1,0:T(8,128)(2,1)S(1)}, f32[16,128]{1,0:T(8,128)S(1)}) custom-call(bf16[32,1152]{1,0:T(8,128)(2,1)S(1)} %shard_map.94.refs_0_.refs_1_, bf16[512,1024]{1,0:T(8,128)(2,1)S(1)} %get-tuple-element.29.refs_1_.refs_2_.refs_4_, bf16[512,1024]{1,0:T(8,128)(2,1)S(1)} %collective-permute-done.1.refs_2_.refs_3_.refs_5_), custom_call_target="tpu_custom_call" | custom-call | flops 67108864 | bytes 2162688 | tf_op jit(solution)/shard_map/pallas_call | solution.py:38
  8.0 2.7 %collective-permute-start.4 = (s16[16,1152]{1,0:T(8,128)(2,1)S(1)}, s16[16,1152]{1,0:T(8,128)(2,1)S(1)}, u32[]{:S(2)}, u32[]{:S(2)}) collective-permute-start(s16[16,1152]{1,0:T(8,128)(2,1)S(1)} %get-tuple-element.30.refs_0_.refs_1_), channel_id=1, source_target_pairs={{0,2},{1,3},{2,0},{3,1},{4,6},{5,7},{6,4},{7,5},{8,10},{9,11},{10,... | collective-permute-start | bytes 110600 | tf_op jit(solution)/shard_map/ppermute | solution.py:322
  10.7 0.0 collective-permute-done.3.refs_2_
  10.7 0.2 collective-permute-done.2.refs_1_
  10.9 0.7 %shard_map.97 = (s16[16,1152]{1,0:T(8,128)(2,1)S(1)}, f32[16,128]{1,0:T(8,128)S(1)}) custom-call(s16[16,1152]{1,0:T(8,128)(2,1)S(1)} %get-tuple-element.30.refs_0_.refs_1_, bf16[32,1152]{1,0:T(8,128)(2,1)S(1)} %shard_map.96.refs_1_.refs_2_, bf16[512,1024]{1,0:T(8,128)(2,1)S(1)} %get-tuple-element.29.refs_1_.refs_2_.refs_4_, ...), custom_call_target="tpu_custom_call" | custom-call | flops 67108864 | bytes 2162688 | tf_op jit(solution)/shard_map/pallas_call | solution.py:38
  11.6 2.7 %collective-permute-start.5 = (s16[16,1152]{1,0:T(8,128)(2,1)S(1)}, s16[16,1152]{1,0:T(8,128)(2,1)S(1)}, u32[]{:S(2)}, u32[]{:S(2)}) collective-permute-start(s16[16,1152]{1,0:T(8,128)(2,1)S(1)} %get-tuple-element.32.refs_0_.refs_1_), channel_id=1, source_target_pairs={{0,2},{1,3},{2,0},{3,1},{4,6},{5,7},{6,4},{7,5},{8,10},{9,11},{10,... | collective-permute-start | bytes 110600 | tf_op jit(solution)/shard_map/ppermute | solution.py:322
  14.2 0.0 collective-permute-start.8
  14.2 0.0 collective-permute-done.4.refs_2_
  14.2 0.2 shard_map.98.refs_0_.refs_1_
  14.4 1.6 %collective-permute-start.6 = (s16[16,1152]{1,0:T(8,128)(2,1)S(1)}, s16[16,1152]{1,0:T(8,128)(2,1)S(1)}, u32[]{:S(2)}, u32[]{:S(2)}) collective-permute-start(s16[16,1152]{1,0:T(8,128)(2,1)S(1)} %shard_map.98.refs_0_.refs_1_), channel_id=1, source_target_pairs={{0,1},{1,0},{2,3},{3,2},{4,5},{5,4},{6,7},{7,6},{8,9},{9,8},{10,11... | collective-permute-start | bytes 110600 | tf_op jit(solution)/shard_map/ppermute | solution.py:322
  16.1 0.2 collective-permute-start.9
  16.3 0.6 %collective-permute-done.5.refs_2_ = s16[16,1152]{1,0:T(8,128)(2,1)S(1)} collective-permute-done((s16[16,1152]{1,0:T(8,128)(2,1)S(1)}, s16[16,1152]{1,0:T(8,128)(2,1)S(1)}, u32[]{:S(2)}, u32[]{:S(2)}) %collective-permute-start.5) | collective-permute-done | bytes 36896 | tf_op jit(solution)/shard_map/ppermute | solution.py:322
  16.9 0.2 shard_map.99.refs_0_.refs_1_
  17.1 1.2 %collective-permute-start.10 = (s16[16,1152]{1,0:T(8,128)(2,1)S(1)}, s16[16,1152]{1,0:T(8,128)(2,1)S(1)}, u32[]{:S(2)}, u32[]{:S(2)}) collective-permute-start(s16[16,1152]{1,0:T(8,128)(2,1)S(1)} %shard_map.99.refs_0_.refs_1_), channel_id=1, source_target_pairs={{0,1},{1,0},{2,3},{3,2},{4,5},{5,4},{6,7},{7,6},{8,9},{9,8},{10,11... | collective-permute-start | bytes 110600 | tf_op jit(solution)/shard_map/ppermute | solution.py:322
  18.3 0.1 collective-permute-done.6.refs_2_
  18.5 0.4 %shard_map.100 = (bf16[32,256]{1,0:T(8,128)(2,1)S(1)}, bf16[32,256]{1,0:T(8,128)(2,1)S(1)}, f32[8,1152]{1,0:T(8,128)S(1)}, f32[8,1152]{1,0:T(8,128)S(1)}) custom-call(s16[16,1152]{1,0:T(8,128)(2,1)S(1)} %shard_map.99.refs_0_.refs_1_, s16[16,1152]{1,0:T(8,128)(2,1)S(1)} %shard_map.98.refs_0_.refs_1_, s16[16,1152]{1,0:T(8,128)(2,1)S(1)} %collective-permute-done.6.refs_2_, ...), custom_call_target="tpu_custom_call" | custom-call | flops 16777216 | bytes 1114112 | tf_op jit(solution)/shard_map/pallas_call | solution.py:38
  18.9 0.0 collective-permute-start.7
  18.9 0.1 shard_map.101
  19.0 2.1 %collective-permute-done.10.refs_2_ = s16[16,1152]{1,0:T(8,128)(2,1)S(1)} collective-permute-done((s16[16,1152]{1,0:T(8,128)(2,1)S(1)}, s16[16,1152]{1,0:T(8,128)(2,1)S(1)}, u32[]{:S(2)}, u32[]{:S(2)}) %collective-permute-start.10) | collective-permute-done | bytes 36896 | tf_op jit(solution)/shard_map/ppermute | solution.py:322
  21.1 0.4 %shard_map.102 = (bf16[32,256]{1,0:T(8,128)(2,1)S(1)}, bf16[64,256]{1,0:T(8,128)(2,1)S(1)}, bf16[8,1152]{1,0:T(8,128)(2,1)S(1)}, bf16[8,1152]{1,0:T(8,128)(2,1)S(1)}) custom-call(bf16[256,32]{1,0:T(8,128)(2,1)S(1)} %get-tuple-element.38.refs_0_.refs_6_, s16[16,1152]{1,0:T(8,128)(2,1)S(1)} %shard_map.99.refs_0_.refs_1_, ...), custom_call_target="tpu_custom_call" | custom-call | flops 16777216 | bytes 1114112 | tf_op jit(solution)/shard_map/pallas_call | solution.py:38
  21.5 0.0 collective-permute-start.11
  21.5 2.0 %collective-permute-start.12 = (bf16[8,1152]{1,0:T(8,128)(2,1)S(1)}, bf16[8,1152]{1,0:T(8,128)(2,1)S(1)}, u32[]{:S(2)}, u32[]{:S(2)}) collective-permute-start(bf16[8,1152]{1,0:T(8,128)(2,1)S(1)} %get-tuple-element.45), channel_id=1, source_target_pairs={{0,28},{4,24},{8,20},{12,16},{16,12},{20,8},{24,4},{28,0},{1,29},{... | collective-permute-start | bytes 55304 | tf_op jit(solution)/shard_map/ppermute | solution.py:322
  23.5 0.0 collective-permute-done.8.refs_3_
  23.5 0.5 %collective-permute-start.13 = (bf16[8,1152]{1,0:T(8,128)(2,1)S(1)}, bf16[8,1152]{1,0:T(8,128)(2,1)S(1)}, u32[]{:S(2)}, u32[]{:S(2)}) collective-permute-start(bf16[8,1152]{1,0:T(8,128)(2,1)S(1)} %get-tuple-element.46), channel_id=1, source_target_pairs={{0,20},{4,16},{8,28},{12,24},{16,4},{20,0},{24,12},{28,8},{1,21},{... | collective-permute-start | bytes 55304 | tf_op jit(solution)/shard_map/ppermute | solution.py:322
  24.1 0.0 collective-permute-done.9.refs_4_
  24.1 0.0 collective-permute-done.11.refs_7_
  24.1 0.0 collective-permute-done.7.refs_0_.refs_2_
  24.1 1.6 %shard_map.103 = (f32[1024,256]{1,0:T(8,128)}, f32[256,1024]{1,0:T(8,128)}, f32[8,128]{1,0:T(8,128)S(1)}) custom-call(f32[8,1152]{1,0:T(8,128)S(1)} %collective-permute-done.7.refs_0_.refs_2_, bf16[32,1152]{1,0:T(8,128)(2,1)S(1)} %shard_map.94.refs_0_.refs_1_, bf16[32,1152]{1,0:T(8,128)(2,1)S(1)} %shard_map.96.refs_1_.refs_2_, ...), custom_call_target="tpu_custom_call" | custom-call | flops 134217728 | bytes 2097152 | tf_op jit(solution)/shard_map/pallas_call | solution.py:38
  25.7 0.0 collective-permute-done.12.refs_3_
  25.7 1.0 %collective-permute-done.13.refs_4_ = bf16[8,1152]{1,0:T(8,128)(2,1)S(1)} collective-permute-done((bf16[8,1152]{1,0:T(8,128)(2,1)S(1)}, bf16[8,1152]{1,0:T(8,128)(2,1)S(1)}, u32[]{:S(2)}, u32[]{:S(2)}) %collective-permute-start.13) | collective-permute-done | bytes 18464 | tf_op jit(solution)/shard_map/ppermute | solution.py:322
  26.7 1.1 %shard_map.104 = (bf16[256,1024]{1,0:T(8,128)(2,1)}, f32[2,256]{1,0:T(2,128)}) custom-call(f32[8,128]{1,0:T(8,128)S(1)} %get-tuple-element.43.refs_0_, f32[8,1152]{1,0:T(8,128)S(1)} %get-tuple-element.44.refs_1_, f32[8,1152]{1,0:T(8,128)S(1)} %collective-permute-done.7.refs_0_.refs_2_, bf16[8,1152]{1,0:T(8,128)(2,1)S(1)} %collective-permute-done.12.refs_3_, ...), custom_call_target="tpu_custom_call" | custom-call | flops 16777216 | bytes 524288 | tf_op jit(solution)/shard_map/pallas_call | solution.py:38
  (2 shorter events, 0.0 us)
Async XLA Ops:
  2.4 4.9 %collective-permute-start.1 = (bf16[512,1024]{1,0:T(8,128)(2,1)S(1)}, bf16[512,1024]{1,0:T(8,128)(2,1)S(1)}, u32[]{:S(2)}, u32[]{:S(2)}) collective-permute-start(bf16[512,1024]{1,0:T(8,128)(2,1)S(1)} %get-tuple-element.29.refs_1_.refs_2_.refs_4_), channel_id=1, source_target_pairs={{0,4},{4,0},{1,5},{5,1},{2,6},{6,2},{3,7},{7,3},{8,12},{12,8},{9,1... | collective-permute-start | bytes 3145736 | tf_op jit(solution)/shard_map/ppermute | solution.py:322
  2.9 4.4 %collective-permute-start = (bf16[16,1152]{1,0:T(8,128)(2,1)S(1)}, bf16[16,1152]{1,0:T(8,128)(2,1)S(1)}, u32[]{:S(2)}, u32[]{:S(2)}) collective-permute-start(bf16[16,1152]{1,0:T(8,128)(2,1)S(1)} %get-tuple-element.28.refs_0_), channel_id=1, source_target_pairs={{0,12},{4,8},{8,4},{12,0},{16,28},{20,24},{24,20},{28,16},{1,13},{... | collective-permute-start | bytes 110600 | tf_op jit(solution)/shard_map/ppermute | solution.py:322
  5.5 5.2 %collective-permute-start.3 = (bf16[16,1152]{1,0:T(8,128)(2,1)S(1)}, bf16[16,1152]{1,0:T(8,128)(2,1)S(1)}, u32[]{:S(2)}, u32[]{:S(2)}) collective-permute-start(bf16[16,1152]{1,0:T(8,128)(2,1)S(1)} %get-tuple-element.31), channel_id=1, source_target_pairs={{0,28},{4,24},{8,20},{12,16},{16,12},{20,8},{24,4},{28,0},{1,29},{... | collective-permute-start | bytes 110600 | tf_op jit(solution)/shard_map/ppermute | solution.py:322
  6.7 4.2 %collective-permute-start.2 = (bf16[16,1152]{1,0:T(8,128)(2,1)S(1)}, bf16[16,1152]{1,0:T(8,128)(2,1)S(1)}, u32[]{:S(2)}, u32[]{:S(2)}) collective-permute-start(bf16[16,1152]{1,0:T(8,128)(2,1)S(1)} %get-tuple-element.31), channel_id=1, source_target_pairs={{0,20},{4,16},{8,28},{12,24},{16,4},{20,0},{24,12},{28,8},{1,21},{... | collective-permute-start | bytes 110600 | tf_op jit(solution)/shard_map/ppermute | solution.py:322
  8.0 6.3 %collective-permute-start.4 = (s16[16,1152]{1,0:T(8,128)(2,1)S(1)}, s16[16,1152]{1,0:T(8,128)(2,1)S(1)}, u32[]{:S(2)}, u32[]{:S(2)}) collective-permute-start(s16[16,1152]{1,0:T(8,128)(2,1)S(1)} %get-tuple-element.30.refs_0_.refs_1_), channel_id=1, source_target_pairs={{0,2},{1,3},{2,0},{3,1},{4,6},{5,7},{6,4},{7,5},{8,10},{9,11},{10,... | collective-permute-start | bytes 110600 | tf_op jit(solution)/shard_map/ppermute | solution.py:322
  11.6 5.3 %collective-permute-start.5 = (s16[16,1152]{1,0:T(8,128)(2,1)S(1)}, s16[16,1152]{1,0:T(8,128)(2,1)S(1)}, u32[]{:S(2)}, u32[]{:S(2)}) collective-permute-start(s16[16,1152]{1,0:T(8,128)(2,1)S(1)} %get-tuple-element.32.refs_0_.refs_1_), channel_id=1, source_target_pairs={{0,2},{1,3},{2,0},{3,1},{4,6},{5,7},{6,4},{7,5},{8,10},{9,11},{10,... | collective-permute-start | bytes 110600 | tf_op jit(solution)/shard_map/ppermute | solution.py:322
  14.2 9.3 %collective-permute-start.8 = (bf16[32,1152]{1,0:T(8,128)(2,1)S(1)}, bf16[32,1152]{1,0:T(8,128)(2,1)S(1)}, u32[]{:S(2)}, u32[]{:S(2)}) collective-permute-start(bf16[32,1152]{1,0:T(8,128)(2,1)S(1)} %shard_map.94.refs_0_.refs_1_), channel_id=1, source_target_pairs={{0,4},{4,0},{1,5},{5,1},{2,6},{6,2},{3,7},{7,3},{8,12},{12,8},{9,1... | collective-permute-start | bytes 221192 | tf_op jit(solution)/shard_map/ppermute | solution.py:322
  14.4 4.0 %collective-permute-start.6 = (s16[16,1152]{1,0:T(8,128)(2,1)S(1)}, s16[16,1152]{1,0:T(8,128)(2,1)S(1)}, u32[]{:S(2)}, u32[]{:S(2)}) collective-permute-start(s16[16,1152]{1,0:T(8,128)(2,1)S(1)} %shard_map.98.refs_0_.refs_1_), channel_id=1, source_target_pairs={{0,1},{1,0},{2,3},{3,2},{4,5},{5,4},{6,7},{7,6},{8,9},{9,8},{10,11... | collective-permute-start | bytes 110600 | tf_op jit(solution)/shard_map/ppermute | solution.py:322
  16.1 8.0 %collective-permute-start.9 = (bf16[32,1152]{1,0:T(8,128)(2,1)S(1)}, bf16[32,1152]{1,0:T(8,128)(2,1)S(1)}, u32[]{:S(2)}, u32[]{:S(2)}) collective-permute-start(bf16[32,1152]{1,0:T(8,128)(2,1)S(1)} %shard_map.96.refs_1_.refs_2_), channel_id=1, source_target_pairs={{0,4},{4,0},{1,5},{5,1},{2,6},{6,2},{3,7},{7,3},{8,12},{12,8},{9,1... | collective-permute-start | bytes 221192 | tf_op jit(solution)/shard_map/ppermute | solution.py:322
  17.1 4.0 %collective-permute-start.10 = (s16[16,1152]{1,0:T(8,128)(2,1)S(1)}, s16[16,1152]{1,0:T(8,128)(2,1)S(1)}, u32[]{:S(2)}, u32[]{:S(2)}) collective-permute-start(s16[16,1152]{1,0:T(8,128)(2,1)S(1)} %shard_map.99.refs_0_.refs_1_), channel_id=1, source_target_pairs={{0,1},{1,0},{2,3},{3,2},{4,5},{5,4},{6,7},{7,6},{8,9},{9,8},{10,11... | collective-permute-start | bytes 110600 | tf_op jit(solution)/shard_map/ppermute | solution.py:322
  18.9 5.2 %collective-permute-start.7 = (f32[8,1152]{1,0:T(8,128)S(1)}, f32[8,1152]{1,0:T(8,128)S(1)}, u32[]{:S(2)}, u32[]{:S(2)}) collective-permute-start(f32[8,1152]{1,0:T(8,128)S(1)} %get-tuple-element.34), channel_id=1, source_target_pairs={{0,12},{4,8},{8,4},{12,0},{16,28},{20,24},{24,20},{28,16},{1,13},{... | collective-permute-start | bytes 110600 | tf_op jit(solution)/shard_map/ppermute | solution.py:322
  21.5 2.6 %collective-permute-start.11 = (bf16[64,256]{1,0:T(8,128)(2,1)S(1)}, bf16[64,256]{1,0:T(8,128)(2,1)S(1)}, u32[]{:S(2)}, u32[]{:S(2)}) collective-permute-start(bf16[64,256]{1,0:T(8,128)(2,1)S(1)} %get-tuple-element.42), channel_id=1, source_target_pairs={{0,4},{4,0},{1,5},{5,1},{2,6},{6,2},{3,7},{7,3},{8,12},{12,8},{9,1... | collective-permute-start | bytes 98312 | tf_op jit(solution)/shard_map/ppermute | solution.py:322
  21.5 4.2 %collective-permute-start.12 = (bf16[8,1152]{1,0:T(8,128)(2,1)S(1)}, bf16[8,1152]{1,0:T(8,128)(2,1)S(1)}, u32[]{:S(2)}, u32[]{:S(2)}) collective-permute-start(bf16[8,1152]{1,0:T(8,128)(2,1)S(1)} %get-tuple-element.45), channel_id=1, source_target_pairs={{0,28},{4,24},{8,20},{12,16},{16,12},{20,8},{24,4},{28,0},{1,29},{... | collective-permute-start | bytes 55304 | tf_op jit(solution)/shard_map/ppermute | solution.py:322
  23.5 3.2 %collective-permute-start.13 = (bf16[8,1152]{1,0:T(8,128)(2,1)S(1)}, bf16[8,1152]{1,0:T(8,128)(2,1)S(1)}, u32[]{:S(2)}, u32[]{:S(2)}) collective-permute-start(bf16[8,1152]{1,0:T(8,128)(2,1)S(1)} %get-tuple-element.46), channel_id=1, source_target_pairs={{0,20},{4,16},{8,28},{12,24},{16,4},{20,0},{24,12},{28,8},{1,21},{... | collective-permute-start | bytes 55304 | tf_op jit(solution)/shard_map/ppermute | solution.py:322

commit v7 on v6

--- a/solution.py
+++ b/solution.py
@@ -11,6 +11,7 @@
 WINDOW = 2
 LANES = 128
 PIECES = 4
+LOADS = 8
 VMEM_LIMIT = 40 * 1024 * 1024
 
 BF16 = jnp.bfloat16
@@ -99,16 +100,19 @@
         pltpu.make_async_copy(routes_hbm, routes_ref, sems.at[0]),
         pltpu.make_async_copy(gates_hbm, gates_ref, sems.at[1]),
     ]
-    count = tok_rows // PIECES
+    count = tok_rows // LOADS
     for source, target in ((tokens_hbm, tokens_ref), (grads_hbm, grads_ref)):
-        for piece in range(PIECES):
+        for piece in range(LOADS):
             span = pl.ds(piece * count, count)
             copies.append(
                 pltpu.make_async_copy(source.at[span], target.at[span], sems.at[len(copies)])
             )
     hidden = w_out_hbm.shape[0]
-    upper, lower = pl.ds(0, hidden), pl.ds(hidden, hidden)
-    moves = [(w_out_hbm, w_ref.at[upper])]
+    lower = pl.ds(hidden, hidden)
+    moves = []
+    for block in range(0, hidden, hidden // PIECES):
+        span = pl.ds(block, hidden // PIECES)
+        moves.append((w_out_hbm.at[span], w_ref.at[span]))
     for block in range(0, feats, hidden):
         span = pl.ds(block, hidden)
         moves.append((w_in_hbm.at[span], w_ref.at[lower, span]))
@@ -136,10 +140,10 @@
     parts = [jnp.where(before[e : e + 1] == slot_of, named[e], 0.0) for e in range(WINDOW)]
     place = jnp.concatenate(parts, axis=0).astype(BF16)
     place_ref[...] = place
-    for copy in copies[2 : 2 + PIECES]:
+    for copy in copies[2 : 2 + LOADS]:
         copy.wait()
     rows_x = jnp.dot(place, tokens_ref[...], preferred_element_type=F32)
-    for copy in copies[2 + PIECES : 2 + 2 * PIECES]:
+    for copy in copies[2 + LOADS : 2 + 2 * LOADS]:
         copy.wait()
     rows_dy = jnp.dot(place, grads_ref[...], preferred_element_type=F32)
     for expert, out_ref in ((0, own_ref), (1, other_ref)):
@@ -148,7 +152,7 @@
         gate = jnp.sum(parts[expert] * weight[expert], axis=1, keepdims=True)
         gate = jnp.concatenate([gate, gate], axis=0)
         out_ref[:, feats:] = jnp.broadcast_to(gate, (2 * capacity, LANES)).astype(BF16)
-    for copy in copies[2 + 2 * PIECES :]:
+    for copy in copies[2 + 2 * LOADS :]:
         copy.wait()
 
 
@@ -367,7 +371,7 @@
             pltpu.VMEM((2, tok_rows), BF16),
             pltpu.VMEM((tok_rows, feats), BF16),
             pltpu.VMEM((tok_rows, feats), BF16),
-            pltpu.SemaphoreType.DMA((3 + 2 * PIECES + feats // hidden,)),
+            pltpu.SemaphoreType.DMA((2 + 2 * LOADS + PIECES + feats // hidden,)),
         ],
     )(*inputs)
 

time: 28 us -> 28.1 us (level)
  no operation moved by 1% of the time
where the time goes in v7:
time: 28.1 us; the launch traced here: 27.9 us
  starting transfers between devices  15.4 us (55%)
  Pallas kernels  7.24 us (26%)
  waiting for transfers between devices  4.56 us (16%)
  between operations  0.71 us (3%)
    ppermute x14, starting transfers between devices, swap(): lax.ppermute(array, axes, [(index, index ^ bit) for index in range(size)])  15.4 us
    pallas_call x12, Pallas kernels, run(): pl.pallas_call(lambda *refs: kernel(*refs[len(after):]), out_shape=out_sh...  7.24 us
    ppermute x14, waiting for transfers between devices, swap(): lax.ppermute(array, axes, [(index, index ^ bit) for index in range(size)])  4.56 us
  transfers between devices with their start and end apart: 14, of which 6 were waited for; matrix products, arithmetic and copies ran while one was open for 0% of the time, Pallas kernels for 15%

profile of v7, /device:TPU:0, one launch (start us, length us, event | category | flops | bytes accessed | tf_op | source)
XLA Modules:
  0.0 27.9 jit_solution(926148390946341020)
XLA Ops:
  0.6 1.9 %shard_map.93 = (bf16[16,1152]{1,0:T(8,128)(2,1)S(1)}, bf16[16,1152]{1,0:T(8,128)(2,1)S(1)}, bf16[16,256]{1,0:T(8,128)(2,1)S(1)}, s32[2,256]{1,0:T(2,128)S(1)}, bf16[512,1024]{1,0:T(8,128)(2,1)S(1)}) custom-call(s32[2,256]{1,0:T(2,128)} %bitcast.3, bf16[2,256]{1,0:T(2,128)(2,1)} %bitcast.4, bf16[256,1024]{1,0:T(8,128)(2,1)} %refs_2_.1, ...), custom_call_target="tpu_custom_call" | custom-call | flops 16777216 | bytes 2097152 | tf_op jit(solution)/shard_map/pallas_call | solution.py:39
  2.5 0.5 %collective-permute-start.1 = (bf16[512,1024]{1,0:T(8,128)(2,1)S(1)}, bf16[512,1024]{1,0:T(8,128)(2,1)S(1)}, u32[]{:S(2)}, u32[]{:S(2)}) collective-permute-start(bf16[512,1024]{1,0:T(8,128)(2,1)S(1)} %get-tuple-element.29.refs_1_.refs_2_.refs_4_), channel_id=1, source_target_pairs={{0,4},{4,0},{1,5},{5,1},{2,6},{6,2},{3,7},{7,3},{8,12},{12,8},{9,1... | collective-permute-start | bytes 3145736 | tf_op jit(solution)/shard_map/ppermute | solution.py:326
  3.0 2.6 %collective-permute-start = (bf16[16,1152]{1,0:T(8,128)(2,1)S(1)}, bf16[16,1152]{1,0:T(8,128)(2,1)S(1)}, u32[]{:S(2)}, u32[]{:S(2)}) collective-permute-start(bf16[16,1152]{1,0:T(8,128)(2,1)S(1)} %get-tuple-element.28.refs_0_), channel_id=1, source_target_pairs={{0,12},{4,8},{8,4},{12,0},{16,28},{20,24},{24,20},{28,16},{1,13},{... | collective-permute-start | bytes 110600 | tf_op jit(solution)/shard_map/ppermute | solution.py:326
  5.6 1.2 %collective-permute-start.3 = (bf16[16,1152]{1,0:T(8,128)(2,1)S(1)}, bf16[16,1152]{1,0:T(8,128)(2,1)S(1)}, u32[]{:S(2)}, u32[]{:S(2)}) collective-permute-start(bf16[16,1152]{1,0:T(8,128)(2,1)S(1)} %get-tuple-element.31), channel_id=1, source_target_pairs={{0,28},{4,24},{8,20},{12,16},{16,12},{20,8},{24,4},{28,0},{1,29},{... | collective-permute-start | bytes 110600 | tf_op jit(solution)/shard_map/ppermute | solution.py:326
  6.8 0.1 collective-permute-start.2
  6.8 0.5 %collective-permute-done.refs_1_ = bf16[16,1152]{1,0:T(8,128)(2,1)S(1)} collective-permute-done((bf16[16,1152]{1,0:T(8,128)(2,1)S(1)}, bf16[16,1152]{1,0:T(8,128)(2,1)S(1)}, u32[]{:S(2)}, u32[]{:S(2)}) %collective-permute-start) | collective-permute-done | bytes 36896 | tf_op jit(solution)/shard_map/ppermute | solution.py:326
  7.4 0.0 collective-permute-done.1.refs_2_.refs_3_.refs_5_
  7.4 0.7 %shard_map.95 = (s16[16,1152]{1,0:T(8,128)(2,1)S(1)}, f32[16,128]{1,0:T(8,128)S(1)}) custom-call(bf16[32,1152]{1,0:T(8,128)(2,1)S(1)} %shard_map.94.refs_0_.refs_1_, bf16[512,1024]{1,0:T(8,128)(2,1)S(1)} %get-tuple-element.29.refs_1_.refs_2_.refs_4_, bf16[512,1024]{1,0:T(8,128)(2,1)S(1)} %collective-permute-done.1.refs_2_.refs_3_.refs_5_), custom_call_target="tpu_custom_call" | custom-call | flops 67108864 | bytes 2162688 | tf_op jit(solution)/shard_map/pallas_call | solution.py:39
  8.1 2.7 %collective-permute-start.4 = (s16[16,1152]{1,0:T(8,128)(2,1)S(1)}, s16[16,1152]{1,0:T(8,128)(2,1)S(1)}, u32[]{:S(2)}, u32[]{:S(2)}) collective-permute-start(s16[16,1152]{1,0:T(8,128)(2,1)S(1)} %get-tuple-element.30.refs_0_.refs_1_), channel_id=1, source_target_pairs={{0,2},{1,3},{2,0},{3,1},{4,6},{5,7},{6,4},{7,5},{8,10},{9,11},{10,... | collective-permute-start | bytes 110600 | tf_op jit(solution)/shard_map/ppermute | solution.py:326
  10.8 0.0 collective-permute-done.3.refs_2_
  10.8 0.2 collective-permute-done.2.refs_1_
  11.0 0.7 %shard_map.97 = (s16[16,1152]{1,0:T(8,128)(2,1)S(1)}, f32[16,128]{1,0:T(8,128)S(1)}) custom-call(s16[16,1152]{1,0:T(8,128)(2,1)S(1)} %get-tuple-element.30.refs_0_.refs_1_, bf16[32,1152]{1,0:T(8,128)(2,1)S(1)} %shard_map.96.refs_1_.refs_2_, bf16[512,1024]{1,0:T(8,128)(2,1)S(1)} %get-tuple-element.29.refs_1_.refs_2_.refs_4_, ...), custom_call_target="tpu_custom_call" | custom-call | flops 67108864 | bytes 2162688 | tf_op jit(solution)/shard_map/pallas_call | solution.py:39
  11.7 2.7 %collective-permute-start.5 = (s16[16,1152]{1,0:T(8,128)(2,1)S(1)}, s16[16,1152]{1,0:T(8,128)(2,1)S(1)}, u32[]{:S(2)}, u32[]{:S(2)}) collective-permute-start(s16[16,1152]{1,0:T(8,128)(2,1)S(1)} %get-tuple-element.32.refs_0_.refs_1_), channel_id=1, source_target_pairs={{0,2},{1,3},{2,0},{3,1},{4,6},{5,7},{6,4},{7,5},{8,10},{9,11},{10,... | collective-permute-start | bytes 110600 | tf_op jit(solution)/shard_map/ppermute | solution.py:326
  14.3 0.0 collective-permute-start.8
  14.3 0.0 collective-permute-done.4.refs_2_
  14.3 0.2 shard_map.98.refs_0_.refs_1_
  14.5 1.6 %collective-permute-start.6 = (s16[16,1152]{1,0:T(8,128)(2,1)S(1)}, s16[16,1152]{1,0:T(8,128)(2,1)S(1)}, u32[]{:S(2)}, u32[]{:S(2)}) collective-permute-start(s16[16,1152]{1,0:T(8,128)(2,1)S(1)} %shard_map.98.refs_0_.refs_1_), channel_id=1, source_target_pairs={{0,1},{1,0},{2,3},{3,2},{4,5},{5,4},{6,7},{7,6},{8,9},{9,8},{10,11... | collective-permute-start | bytes 110600 | tf_op jit(solution)/shard_map/ppermute | solution.py:326
  16.2 0.2 collective-permute-start.9
  16.4 0.6 %collective-permute-done.5.refs_2_ = s16[16,1152]{1,0:T(8,128)(2,1)S(1)} collective-permute-done((s16[16,1152]{1,0:T(8,128)(2,1)S(1)}, s16[16,1152]{1,0:T(8,128)(2,1)S(1)}, u32[]{:S(2)}, u32[]{:S(2)}) %collective-permute-start.5) | collective-permute-done | bytes 36896 | tf_op jit(solution)/shard_map/ppermute | solution.py:326
  17.0 0.2 shard_map.99.refs_0_.refs_1_
  17.2 1.2 %collective-permute-start.10 = (s16[16,1152]{1,0:T(8,128)(2,1)S(1)}, s16[16,1152]{1,0:T(8,128)(2,1)S(1)}, u32[]{:S(2)}, u32[]{:S(2)}) collective-permute-start(s16[16,1152]{1,0:T(8,128)(2,1)S(1)} %shard_map.99.refs_0_.refs_1_), channel_id=1, source_target_pairs={{0,1},{1,0},{2,3},{3,2},{4,5},{5,4},{6,7},{7,6},{8,9},{9,8},{10,11... | collective-permute-start | bytes 110600 | tf_op jit(solution)/shard_map/ppermute | solution.py:326
  18.4 0.1 collective-permute-done.6.refs_2_
  18.6 0.4 %shard_map.100 = (bf16[32,256]{1,0:T(8,128)(2,1)S(1)}, bf16[32,256]{1,0:T(8,128)(2,1)S(1)}, f32[8,1152]{1,0:T(8,128)S(1)}, f32[8,1152]{1,0:T(8,128)S(1)}) custom-call(s16[16,1152]{1,0:T(8,128)(2,1)S(1)} %shard_map.99.refs_0_.refs_1_, s16[16,1152]{1,0:T(8,128)(2,1)S(1)} %shard_map.98.refs_0_.refs_1_, s16[16,1152]{1,0:T(8,128)(2,1)S(1)} %collective-permute-done.6.refs_2_, ...), custom_call_target="tpu_custom_call" | custom-call | flops 16777216 | bytes 1114112 | tf_op jit(solution)/shard_map/pallas_call | solution.py:39
  19.0 0.0 collective-permute-start.7
  19.0 0.1 shard_map.101
  19.1 2.1 %collective-permute-done.10.refs_2_ = s16[16,1152]{1,0:T(8,128)(2,1)S(1)} collective-permute-done((s16[16,1152]{1,0:T(8,128)(2,1)S(1)}, s16[16,1152]{1,0:T(8,128)(2,1)S(1)}, u32[]{:S(2)}, u32[]{:S(2)}) %collective-permute-start.10) | collective-permute-done | bytes 36896 | tf_op jit(solution)/shard_map/ppermute | solution.py:326
  21.2 0.4 %shard_map.102 = (bf16[32,256]{1,0:T(8,128)(2,1)S(1)}, bf16[64,256]{1,0:T(8,128)(2,1)S(1)}, bf16[8,1152]{1,0:T(8,128)(2,1)S(1)}, bf16[8,1152]{1,0:T(8,128)(2,1)S(1)}) custom-call(bf16[256,32]{1,0:T(8,128)(2,1)S(1)} %get-tuple-element.38.refs_0_.refs_6_, s16[16,1152]{1,0:T(8,128)(2,1)S(1)} %shard_map.99.refs_0_.refs_1_, ...), custom_call_target="tpu_custom_call" | custom-call | flops 16777216 | bytes 1114112 | tf_op jit(solution)/shard_map/pallas_call | solution.py:39
  21.6 0.0 collective-permute-start.11
  21.6 2.0 %collective-permute-start.12 = (bf16[8,1152]{1,0:T(8,128)(2,1)S(1)}, bf16[8,1152]{1,0:T(8,128)(2,1)S(1)}, u32[]{:S(2)}, u32[]{:S(2)}) collective-permute-start(bf16[8,1152]{1,0:T(8,128)(2,1)S(1)} %get-tuple-element.45), channel_id=1, source_target_pairs={{0,28},{4,24},{8,20},{12,16},{16,12},{20,8},{24,4},{28,0},{1,29},{... | collective-permute-start | bytes 55304 | tf_op jit(solution)/shard_map/ppermute | solution.py:326
  23.7 0.0 collective-permute-done.8.refs_3_
  23.7 0.5 %collective-permute-start.13 = (bf16[8,1152]{1,0:T(8,128)(2,1)S(1)}, bf16[8,1152]{1,0:T(8,128)(2,1)S(1)}, u32[]{:S(2)}, u32[]{:S(2)}) collective-permute-start(bf16[8,1152]{1,0:T(8,128)(2,1)S(1)} %get-tuple-element.46), channel_id=1, source_target_pairs={{0,20},{4,16},{8,28},{12,24},{16,4},{20,0},{24,12},{28,8},{1,21},{... | collective-permute-start | bytes 55304 | tf_op jit(solution)/shard_map/ppermute | solution.py:326
  24.2 0.0 collective-permute-done.9.refs_4_
  24.2 0.0 collective-permute-done.11.refs_7_
  24.2 0.0 collective-permute-done.7.refs_0_.refs_2_
  24.2 1.6 %shard_map.103 = (f32[1024,256]{1,0:T(8,128)}, f32[256,1024]{1,0:T(8,128)}, f32[8,128]{1,0:T(8,128)S(1)}) custom-call(f32[8,1152]{1,0:T(8,128)S(1)} %collective-permute-done.7.refs_0_.refs_2_, bf16[32,1152]{1,0:T(8,128)(2,1)S(1)} %shard_map.94.refs_0_.refs_1_, bf16[32,1152]{1,0:T(8,128)(2,1)S(1)} %shard_map.96.refs_1_.refs_2_, ...), custom_call_target="tpu_custom_call" | custom-call | flops 134217728 | bytes 2097152 | tf_op jit(solution)/shard_map/pallas_call | solution.py:39
  25.8 0.0 collective-permute-done.12.refs_3_
  25.9 1.0 %collective-permute-done.13.refs_4_ = bf16[8,1152]{1,0:T(8,128)(2,1)S(1)} collective-permute-done((bf16[8,1152]{1,0:T(8,128)(2,1)S(1)}, bf16[8,1152]{1,0:T(8,128)(2,1)S(1)}, u32[]{:S(2)}, u32[]{:S(2)}) %collective-permute-start.13) | collective-permute-done | bytes 18464 | tf_op jit(solution)/shard_map/ppermute | solution.py:326
  26.8 1.1 %shard_map.104 = (bf16[256,1024]{1,0:T(8,128)(2,1)}, f32[2,256]{1,0:T(2,128)}) custom-call(f32[8,128]{1,0:T(8,128)S(1)} %get-tuple-element.43.refs_0_, f32[8,1152]{1,0:T(8,128)S(1)} %get-tuple-element.44.refs_1_, f32[8,1152]{1,0:T(8,128)S(1)} %collective-permute-done.7.refs_0_.refs_2_, bf16[8,1152]{1,0:T(8,128)(2,1)S(1)} %collective-permute-done.12.refs_3_, ...), custom_call_target="tpu_custom_call" | custom-call | flops 16777216 | bytes 524288 | tf_op jit(solution)/shard_map/pallas_call | solution.py:39
  (2 shorter events, 0.0 us)
Async XLA Ops:
  2.5 4.9 %collective-permute-start.1 = (bf16[512,1024]{1,0:T(8,128)(2,1)S(1)}, bf16[512,1024]{1,0:T(8,128)(2,1)S(1)}, u32[]{:S(2)}, u32[]{:S(2)}) collective-permute-start(bf16[512,1024]{1,0:T(8,128)(2,1)S(1)} %get-tuple-element.29.refs_1_.refs_2_.refs_4_), channel_id=1, source_target_pairs={{0,4},{4,0},{1,5},{5,1},{2,6},{6,2},{3,7},{7,3},{8,12},{12,8},{9,1... | collective-permute-start | bytes 3145736 | tf_op jit(solution)/shard_map/ppermute | solution.py:326
  3.0 4.4 %collective-permute-start = (bf16[16,1152]{1,0:T(8,128)(2,1)S(1)}, bf16[16,1152]{1,0:T(8,128)(2,1)S(1)}, u32[]{:S(2)}, u32[]{:S(2)}) collective-permute-start(bf16[16,1152]{1,0:T(8,128)(2,1)S(1)} %get-tuple-element.28.refs_0_), channel_id=1, source_target_pairs={{0,12},{4,8},{8,4},{12,0},{16,28},{20,24},{24,20},{28,16},{1,13},{... | collective-permute-start | bytes 110600 | tf_op jit(solution)/shard_map/ppermute | solution.py:326
  5.6 5.2 %collective-permute-start.3 = (bf16[16,1152]{1,0:T(8,128)(2,1)S(1)}, bf16[16,1152]{1,0:T(8,128)(2,1)S(1)}, u32[]{:S(2)}, u32[]{:S(2)}) collective-permute-start(bf16[16,1152]{1,0:T(8,128)(2,1)S(1)} %get-tuple-element.31), channel_id=1, source_target_pairs={{0,28},{4,24},{8,20},{12,16},{16,12},{20,8},{24,4},{28,0},{1,29},{... | collective-permute-start | bytes 110600 | tf_op jit(solution)/shard_map/ppermute | solution.py:326
  6.8 4.2 %collective-permute-start.2 = (bf16[16,1152]{1,0:T(8,128)(2,1)S(1)}, bf16[16,1152]{1,0:T(8,128)(2,1)S(1)}, u32[]{:S(2)}, u32[]{:S(2)}) collective-permute-start(bf16[16,1152]{1,0:T(8,128)(2,1)S(1)} %get-tuple-element.31), channel_id=1, source_target_pairs={{0,20},{4,16},{8,28},{12,24},{16,4},{20,0},{24,12},{28,8},{1,21},{... | collective-permute-start | bytes 110600 | tf_op jit(solution)/shard_map/ppermute | solution.py:326
  8.1 6.3 %collective-permute-start.4 = (s16[16,1152]{1,0:T(8,128)(2,1)S(1)}, s16[16,1152]{1,0:T(8,128)(2,1)S(1)}, u32[]{:S(2)}, u32[]{:S(2)}) collective-permute-start(s16[16,1152]{1,0:T(8,128)(2,1)S(1)} %get-tuple-element.30.refs_0_.refs_1_), channel_id=1, source_target_pairs={{0,2},{1,3},{2,0},{3,1},{4,6},{5,7},{6,4},{7,5},{8,10},{9,11},{10,... | collective-permute-start | bytes 110600 | tf_op jit(solution)/shard_map/ppermute | solution.py:326
  11.7 5.3 %collective-permute-start.5 = (s16[16,1152]{1,0:T(8,128)(2,1)S(1)}, s16[16,1152]{1,0:T(8,128)(2,1)S(1)}, u32[]{:S(2)}, u32[]{:S(2)}) collective-permute-start(s16[16,1152]{1,0:T(8,128)(2,1)S(1)} %get-tuple-element.32.refs_0_.refs_1_), channel_id=1, source_target_pairs={{0,2},{1,3},{2,0},{3,1},{4,6},{5,7},{6,4},{7,5},{8,10},{9,11},{10,... | collective-permute-start | bytes 110600 | tf_op jit(solution)/shard_map/ppermute | solution.py:326
  14.3 9.3 %collective-permute-start.8 = (bf16[32,1152]{1,0:T(8,128)(2,1)S(1)}, bf16[32,1152]{1,0:T(8,128)(2,1)S(1)}, u32[]{:S(2)}, u32[]{:S(2)}) collective-permute-start(bf16[32,1152]{1,0:T(8,128)(2,1)S(1)} %shard_map.94.refs_0_.refs_1_), channel_id=1, source_target_pairs={{0,4},{4,0},{1,5},{5,1},{2,6},{6,2},{3,7},{7,3},{8,12},{12,8},{9,1... | collective-permute-start | bytes 221192 | tf_op jit(solution)/shard_map/ppermute | solution.py:326
  14.5 4.0 %collective-permute-start.6 = (s16[16,1152]{1,0:T(8,128)(2,1)S(1)}, s16[16,1152]{1,0:T(8,128)(2,1)S(1)}, u32[]{:S(2)}, u32[]{:S(2)}) collective-permute-start(s16[16,1152]{1,0:T(8,128)(2,1)S(1)} %shard_map.98.refs_0_.refs_1_), channel_id=1, source_target_pairs={{0,1},{1,0},{2,3},{3,2},{4,5},{5,4},{6,7},{7,6},{8,9},{9,8},{10,11... | collective-permute-start | bytes 110600 | tf_op jit(solution)/shard_map/ppermute | solution.py:326
  16.2 8.0 %collective-permute-start.9 = (bf16[32,1152]{1,0:T(8,128)(2,1)S(1)}, bf16[32,1152]{1,0:T(8,128)(2,1)S(1)}, u32[]{:S(2)}, u32[]{:S(2)}) collective-permute-start(bf16[32,1152]{1,0:T(8,128)(2,1)S(1)} %shard_map.96.refs_1_.refs_2_), channel_id=1, source_target_pairs={{0,4},{4,0},{1,5},{5,1},{2,6},{6,2},{3,7},{7,3},{8,12},{12,8},{9,1... | collective-permute-start | bytes 221192 | tf_op jit(solution)/shard_map/ppermute | solution.py:326
  17.2 4.0 %collective-permute-start.10 = (s16[16,1152]{1,0:T(8,128)(2,1)S(1)}, s16[16,1152]{1,0:T(8,128)(2,1)S(1)}, u32[]{:S(2)}, u32[]{:S(2)}) collective-permute-start(s16[16,1152]{1,0:T(8,128)(2,1)S(1)} %shard_map.99.refs_0_.refs_1_), channel_id=1, source_target_pairs={{0,1},{1,0},{2,3},{3,2},{4,5},{5,4},{6,7},{7,6},{8,9},{9,8},{10,11... | collective-permute-start | bytes 110600 | tf_op jit(solution)/shard_map/ppermute | solution.py:326
  19.0 5.2 %collective-permute-start.7 = (f32[8,1152]{1,0:T(8,128)S(1)}, f32[8,1152]{1,0:T(8,128)S(1)}, u32[]{:S(2)}, u32[]{:S(2)}) collective-permute-start(f32[8,1152]{1,0:T(8,128)S(1)} %get-tuple-element.34), channel_id=1, source_target_pairs={{0,12},{4,8},{8,4},{12,0},{16,28},{20,24},{24,20},{28,16},{1,13},{... | collective-permute-start | bytes 110600 | tf_op jit(solution)/shard_map/ppermute | solution.py:326
  21.6 2.6 %collective-permute-start.11 = (bf16[64,256]{1,0:T(8,128)(2,1)S(1)}, bf16[64,256]{1,0:T(8,128)(2,1)S(1)}, u32[]{:S(2)}, u32[]{:S(2)}) collective-permute-start(bf16[64,256]{1,0:T(8,128)(2,1)S(1)} %get-tuple-element.42), channel_id=1, source_target_pairs={{0,4},{4,0},{1,5},{5,1},{2,6},{6,2},{3,7},{7,3},{8,12},{12,8},{9,1... | collective-permute-start | bytes 98312 | tf_op jit(solution)/shard_map/ppermute | solution.py:326
  21.6 4.2 %collective-permute-start.12 = (bf16[8,1152]{1,0:T(8,128)(2,1)S(1)}, bf16[8,1152]{1,0:T(8,128)(2,1)S(1)}, u32[]{:S(2)}, u32[]{:S(2)}) collective-permute-start(bf16[8,1152]{1,0:T(8,128)(2,1)S(1)} %get-tuple-element.45), channel_id=1, source_target_pairs={{0,28},{4,24},{8,20},{12,16},{16,12},{20,8},{24,4},{28,0},{1,29},{... | collective-permute-start | bytes 55304 | tf_op jit(solution)/shard_map/ppermute | solution.py:326
  23.7 3.2 %collective-permute-start.13 = (bf16[8,1152]{1,0:T(8,128)(2,1)S(1)}, bf16[8,1152]{1,0:T(8,128)(2,1)S(1)}, u32[]{:S(2)}, u32[]{:S(2)}) collective-permute-start(bf16[8,1152]{1,0:T(8,128)(2,1)S(1)} %get-tuple-element.46), channel_id=1, source_target_pairs={{0,20},{4,16},{8,28},{12,24},{16,4},{20,0},{24,12},{28,8},{1,21},{... | collective-permute-start | bytes 55304 | tf_op jit(solution)/shard_map/ppermute | solution.py:326

commit v8 on v6

--- a/solution.py
+++ b/solution.py
@@ -373,6 +373,9 @@
 
     other_weights = swap(weights, "local", 1)
 
+    quarter = nodes // 4
+    near = list(range(quarter, nodes - quarter))
+    far = [*range(quarter), *range(nodes - quarter, nodes)]
     half_nodes = nodes // WINDOW
     pieces = [own_rows]
     for step in range(1, nodes):
@@ -381,8 +384,8 @@
     last = ()
     chains = []
     held = []
-    for chunk in (pieces[:half_nodes], pieces[half_nodes:]):
-        chunk = join(chunk, last)
+    for steps in (near, far):
+        chunk = join([pieces[step] for step in steps], last)
         bit = 2
         while bit < locals_:
             chunk = join([chunk, swap(chunk, "local", bit)])
@@ -413,9 +416,12 @@
 
     mine = []
     theirs = ()
-    slots_back = []
+    slots_back = {}
     for index, (part, other, gate_rows) in enumerate(chains):
-        dealt = [shape((capacity, wide), BF16 if index else F32)] * half_nodes
+        dealt = [
+            shape((capacity, wide), BF16 if index and step else F32)
+            for step in (far if index else near)
+        ]
         own, packed, *slot_parts = call(
             functools.partial(slot_kernel, capacity, len(theirs)),
             [
@@ -455,8 +461,8 @@
             slot_parts = call(deal_kernel, dealt, 4 * half * wide, 12 * half * wide)(
                 keep, swap(send, "local", bit)
             )
-        for step, send in enumerate(slot_parts, index * half_nodes):
-            slots_back.append(swap_nodes(send, step) if step else send)
+        for step, send in zip(far if index else near, slot_parts):
+            slots_back[step] = swap_nodes(send, step) if step else send
     came = [swap(chunk, "local", 1) for chunk in held]
     back = swap(theirs[0], "local", 1)
     grad_w_in, grad_w_out, written = call(
@@ -465,7 +471,7 @@
         32 * rows * feats * hidden,
         8 * feats * hidden,
         in_specs=[vmem] * 7,
-        after=slots_back[1:half_nodes],
+        after=[slots_back[step] for step in near],
         out_specs=[hbm, hbm, vmem],
         scratch_shapes=[
             pltpu.VMEM((feats, hidden), F32),
@@ -479,7 +485,7 @@
         4 * slots * tok_rows * feats,
         2 * tok_rows * feats,
         after=(written,),
-    )(*slots_back[:half_nodes], *reversed(slots_back[half_nodes:]), place, spread, masks)
+    )(*[slots_back[step] for step in range(nodes)], place, spread, masks)
     return (grad_tokens, grad_gates.T, grad_w_in, grad_w_out)
 
 

time: 28 us -> 28.4 us (1.014)
  waiting for transfers between devices: 4.56 us -> 6.1 us
  starting transfers between devices: 15.4 us -> 14.3 us
    ppermute x14, waiting for transfers between devices: 4.56 us -> 6.1 us  [swap(): lax.ppermute(array, axes, [(index, index ^ bit) for index in range(size)])]
    ppermute x14, starting transfers between devices: 15.4 us -> 14.3 us  [swap(): lax.ppermute(array, axes, [(index, index ^ bit) for index in range(size)])]
where the time goes in v8:
time: 28.4 us; the launch traced here: 28.3 us
  starting transfers between devices  14.3 us (50%)
  Pallas kernels  7.12 us (25%)
  waiting for transfers between devices  6.1 us (21%)
  between operations  0.72 us (3%)
    ppermute x14, starting transfers between devices, swap(): lax.ppermute(array, axes, [(index, index ^ bit) for index in range(size)])  14.3 us
    pallas_call x12, Pallas kernels, run(): pl.pallas_call(lambda *refs: kernel(*refs[len(after):]), out_shape=out_sh...  7.12 us
    ppermute x14, waiting for transfers between devices, swap(): lax.ppermute(array, axes, [(index, index ^ bit) for index in range(size)])  6.1 us
  transfers between devices with their start and end apart: 14, of which 6 were waited for; matrix products, arithmetic and copies ran while one was open for 0% of the time, Pallas kernels for 15%

profile of v8, /device:TPU:0, one launch (start us, length us, event | category | flops | bytes accessed | tf_op | source)
XLA Modules:
  0.0 28.3 jit_solution(10164516142304567971)
XLA Ops:
  0.6 1.8 %shard_map.93 = (bf16[16,1152]{1,0:T(8,128)(2,1)S(1)}, bf16[16,1152]{1,0:T(8,128)(2,1)S(1)}, bf16[16,256]{1,0:T(8,128)(2,1)S(1)}, s32[2,256]{1,0:T(2,128)S(1)}, bf16[512,1024]{1,0:T(8,128)(2,1)S(1)}) custom-call(s32[2,256]{1,0:T(2,128)} %bitcast.3, bf16[2,256]{1,0:T(2,128)(2,1)} %bitcast.4, bf16[256,1024]{1,0:T(8,128)(2,1)} %refs_2_.1, ...), custom_call_target="tpu_custom_call" | custom-call | flops 16777216 | bytes 2097152 | tf_op jit(solution)/shard_map/pallas_call | solution.py:38
  2.4 0.5 %collective-permute-start.2 = (bf16[512,1024]{1,0:T(8,128)(2,1)S(1)}, bf16[512,1024]{1,0:T(8,128)(2,1)S(1)}, u32[]{:S(2)}, u32[]{:S(2)}) collective-permute-start(bf16[512,1024]{1,0:T(8,128)(2,1)S(1)} %get-tuple-element.30.refs_1_.refs_2_.refs_4_), channel_id=1, source_target_pairs={{0,4},{4,0},{1,5},{5,1},{2,6},{6,2},{3,7},{7,3},{8,12},{12,8},{9,1... | collective-permute-start | bytes 3145736 | tf_op jit(solution)/shard_map/ppermute | solution.py:322
  2.9 2.6 %collective-permute-start = (bf16[16,1152]{1,0:T(8,128)(2,1)S(1)}, bf16[16,1152]{1,0:T(8,128)(2,1)S(1)}, u32[]{:S(2)}, u32[]{:S(2)}) collective-permute-start(bf16[16,1152]{1,0:T(8,128)(2,1)S(1)} %get-tuple-element.28.refs_1_), channel_id=1, source_target_pairs={{0,12},{4,8},{8,4},{12,0},{16,28},{20,24},{24,20},{28,16},{1,13},{... | collective-permute-start | bytes 110600 | tf_op jit(solution)/shard_map/ppermute | solution.py:322
  5.5 1.2 %collective-permute-start.1 = (bf16[16,1152]{1,0:T(8,128)(2,1)S(1)}, bf16[16,1152]{1,0:T(8,128)(2,1)S(1)}, u32[]{:S(2)}, u32[]{:S(2)}) collective-permute-start(bf16[16,1152]{1,0:T(8,128)(2,1)S(1)} %get-tuple-element.29), channel_id=1, source_target_pairs={{0,20},{4,16},{8,28},{12,24},{16,4},{20,0},{24,12},{28,8},{1,21},{... | collective-permute-start | bytes 110600 | tf_op jit(solution)/shard_map/ppermute | solution.py:322
  6.7 0.0 collective-permute-start.3
  6.7 0.5 %collective-permute-done.refs_0_ = bf16[16,1152]{1,0:T(8,128)(2,1)S(1)} collective-permute-done((bf16[16,1152]{1,0:T(8,128)(2,1)S(1)}, bf16[16,1152]{1,0:T(8,128)(2,1)S(1)}, u32[]{:S(2)}, u32[]{:S(2)}) %collective-permute-start) | collective-permute-done | bytes 36896 | tf_op jit(solution)/shard_map/ppermute | solution.py:322
  7.3 1.8 %collective-permute-done.1.refs_1_ = bf16[16,1152]{1,0:T(8,128)(2,1)S(1)} collective-permute-done((bf16[16,1152]{1,0:T(8,128)(2,1)S(1)}, bf16[16,1152]{1,0:T(8,128)(2,1)S(1)}, u32[]{:S(2)}, u32[]{:S(2)}) %collective-permute-start.1) | collective-permute-done | bytes 36896 | tf_op jit(solution)/shard_map/ppermute | solution.py:322
  9.1 0.0 collective-permute-done.2.refs_2_.refs_3_.refs_5_
  9.1 0.7 %shard_map.95 = (s16[16,1152]{1,0:T(8,128)(2,1)S(1)}, f32[16,128]{1,0:T(8,128)S(1)}) custom-call(bf16[32,1152]{1,0:T(8,128)(2,1)S(1)} %shard_map.94.refs_0_.refs_2_, bf16[512,1024]{1,0:T(8,128)(2,1)S(1)} %get-tuple-element.30.refs_1_.refs_2_.refs_4_, bf16[512,1024]{1,0:T(8,128)(2,1)S(1)} %collective-permute-done.2.refs_2_.refs_3_.refs_5_), custom_call_target="tpu_custom_call" | custom-call | flops 67108864 | bytes 2162688 | tf_op jit(solution)/shard_map/pallas_call | solution.py:38
  9.8 2.7 %collective-permute-start.4 = (s16[16,1152]{1,0:T(8,128)(2,1)S(1)}, s16[16,1152]{1,0:T(8,128)(2,1)S(1)}, u32[]{:S(2)}, u32[]{:S(2)}) collective-permute-start(s16[16,1152]{1,0:T(8,128)(2,1)S(1)} %get-tuple-element.31.refs_0_.refs_1_), channel_id=1, source_target_pairs={{0,2},{1,3},{2,0},{3,1},{4,6},{5,7},{6,4},{7,5},{8,10},{9,11},{10,... | collective-permute-start | bytes 110600 | tf_op jit(solution)/shard_map/ppermute | solution.py:322
  12.4 0.0 collective-permute-done.3.refs_2_
  12.4 0.7 %shard_map.97 = (s16[16,1152]{1,0:T(8,128)(2,1)S(1)}, f32[16,128]{1,0:T(8,128)S(1)}) custom-call(s16[16,1152]{1,0:T(8,128)(2,1)S(1)} %get-tuple-element.31.refs_0_.refs_1_, bf16[32,1152]{1,0:T(8,128)(2,1)S(1)} %shard_map.96.refs_1_.refs_3_, bf16[512,1024]{1,0:T(8,128)(2,1)S(1)} %get-tuple-element.30.refs_1_.refs_2_.refs_4_, ...), custom_call_target="tpu_custom_call" | custom-call | flops 67108864 | bytes 2162688 | tf_op jit(solution)/shard_map/pallas_call | solution.py:38
  13.1 1.2 %collective-permute-start.5 = (s16[16,1152]{1,0:T(8,128)(2,1)S(1)}, s16[16,1152]{1,0:T(8,128)(2,1)S(1)}, u32[]{:S(2)}, u32[]{:S(2)}) collective-permute-start(s16[16,1152]{1,0:T(8,128)(2,1)S(1)} %get-tuple-element.32.refs_0_.refs_1_), channel_id=1, source_target_pairs={{0,2},{1,3},{2,0},{3,1},{4,6},{5,7},{6,4},{7,5},{8,10},{9,11},{10,... | collective-permute-start | bytes 110600 | tf_op jit(solution)/shard_map/ppermute | solution.py:322
  14.3 0.2 collective-permute-start.9
  14.5 0.6 %collective-permute-done.4.refs_2_ = s16[16,1152]{1,0:T(8,128)(2,1)S(1)} collective-permute-done((s16[16,1152]{1,0:T(8,128)(2,1)S(1)}, s16[16,1152]{1,0:T(8,128)(2,1)S(1)}, u32[]{:S(2)}, u32[]{:S(2)}) %collective-permute-start.4) | collective-permute-done | bytes 36896 | tf_op jit(solution)/shard_map/ppermute | solution.py:322
  15.1 0.2 shard_map.98.refs_0_.refs_1_
  15.3 1.2 %collective-permute-start.6 = (s16[16,1152]{1,0:T(8,128)(2,1)S(1)}, s16[16,1152]{1,0:T(8,128)(2,1)S(1)}, u32[]{:S(2)}, u32[]{:S(2)}) collective-permute-start(s16[16,1152]{1,0:T(8,128)(2,1)S(1)} %shard_map.98.refs_0_.refs_1_), channel_id=1, source_target_pairs={{0,1},{1,0},{2,3},{3,2},{4,5},{5,4},{6,7},{7,6},{8,9},{9,8},{10,11... | collective-permute-start | bytes 110600 | tf_op jit(solution)/shard_map/ppermute | solution.py:322
  16.5 0.0 collective-permute-start.10
  16.5 1.9 %collective-permute-done.5.refs_2_ = s16[16,1152]{1,0:T(8,128)(2,1)S(1)} collective-permute-done((s16[16,1152]{1,0:T(8,128)(2,1)S(1)}, s16[16,1152]{1,0:T(8,128)(2,1)S(1)}, u32[]{:S(2)}, u32[]{:S(2)}) %collective-permute-start.5) | collective-permute-done | bytes 36896 | tf_op jit(solution)/shard_map/ppermute | solution.py:322
  18.4 0.2 shard_map.99.refs_0_.refs_1_
  18.6 1.4 %collective-permute-start.11 = (s16[16,1152]{1,0:T(8,128)(2,1)S(1)}, s16[16,1152]{1,0:T(8,128)(2,1)S(1)}, u32[]{:S(2)}, u32[]{:S(2)}) collective-permute-start(s16[16,1152]{1,0:T(8,128)(2,1)S(1)} %shard_map.99.refs_0_.refs_1_), channel_id=1, source_target_pairs={{0,1},{1,0},{2,3},{3,2},{4,5},{5,4},{6,7},{7,6},{8,9},{9,8},{10,11... | collective-permute-start | bytes 110600 | tf_op jit(solution)/shard_map/ppermute | solution.py:322
  20.0 0.0 collective-permute-done.6.refs_2_
  20.0 0.4 %shard_map.100 = (bf16[32,256]{1,0:T(8,128)(2,1)S(1)}, bf16[32,256]{1,0:T(8,128)(2,1)S(1)}, f32[8,1152]{1,0:T(8,128)S(1)}, f32[8,1152]{1,0:T(8,128)S(1)}) custom-call(s16[16,1152]{1,0:T(8,128)(2,1)S(1)} %shard_map.99.refs_0_.refs_1_, s16[16,1152]{1,0:T(8,128)(2,1)S(1)} %shard_map.98.refs_0_.refs_1_, s16[16,1152]{1,0:T(8,128)(2,1)S(1)} %collective-permute-done.6.refs_2_, ...), custom_call_target="tpu_custom_call" | custom-call | flops 16777216 | bytes 1114112 | tf_op jit(solution)/shard_map/pallas_call | solution.py:38
  20.4 0.0 collective-permute-start.7
  20.4 1.8 %collective-permute-start.8 = (f32[8,1152]{1,0:T(8,128)S(1)}, f32[8,1152]{1,0:T(8,128)S(1)}, u32[]{:S(2)}, u32[]{:S(2)}) collective-permute-start(f32[8,1152]{1,0:T(8,128)S(1)} %get-tuple-element.35), channel_id=1, source_target_pairs={{0,20},{4,16},{8,28},{12,24},{16,4},{20,0},{24,12},{28,8},{1,21},{... | collective-permute-start | bytes 110600 | tf_op jit(solution)/shard_map/ppermute | solution.py:322
  22.2 0.1 shard_map.101
  22.3 0.3 %collective-permute-done.11.refs_2_ = s16[16,1152]{1,0:T(8,128)(2,1)S(1)} collective-permute-done((s16[16,1152]{1,0:T(8,128)(2,1)S(1)}, s16[16,1152]{1,0:T(8,128)(2,1)S(1)}, u32[]{:S(2)}, u32[]{:S(2)}) %collective-permute-start.11) | collective-permute-done | bytes 36896 | tf_op jit(solution)/shard_map/ppermute | solution.py:322
  22.6 0.4 %shard_map.102 = (bf16[32,256]{1,0:T(8,128)(2,1)S(1)}, bf16[64,256]{1,0:T(8,128)(2,1)S(1)}, f32[8,1152]{1,0:T(8,128)S(1)}, bf16[8,1152]{1,0:T(8,128)(2,1)S(1)}) custom-call(bf16[256,32]{1,0:T(8,128)(2,1)S(1)} %get-tuple-element.39.refs_0_.refs_6_, s16[16,1152]{1,0:T(8,128)(2,1)S(1)} %shard_map.99.refs_0_.refs_1_, ...), custom_call_target="tpu_custom_call" | custom-call | flops 16777216 | bytes 1114112 | tf_op jit(solution)/shard_map/pallas_call | solution.py:38
  23.0 0.0 collective-permute-start.12
  23.0 0.0 collective-permute-done.9.refs_4_
  23.1 1.5 %collective-permute-start.13 = (bf16[8,1152]{1,0:T(8,128)(2,1)S(1)}, bf16[8,1152]{1,0:T(8,128)(2,1)S(1)}, u32[]{:S(2)}, u32[]{:S(2)}) collective-permute-start(bf16[8,1152]{1,0:T(8,128)(2,1)S(1)} %get-tuple-element.46), channel_id=1, source_target_pairs={{0,28},{4,24},{8,20},{12,16},{16,12},{20,8},{24,4},{28,0},{1,29},{... | collective-permute-start | bytes 55304 | tf_op jit(solution)/shard_map/ppermute | solution.py:322
  24.5 0.0 collective-permute-done.10.refs_5_
  24.6 0.0 collective-permute-done.12.refs_8_
  24.6 0.0 collective-permute-done.7.refs_0_.refs_2_
  24.6 0.0 collective-permute-done.8.refs_1_.refs_3_
  24.6 1.6 %shard_map.103 = (f32[1024,256]{1,0:T(8,128)}, f32[256,1024]{1,0:T(8,128)}, f32[8,128]{1,0:T(8,128)S(1)}) custom-call(f32[8,1152]{1,0:T(8,128)S(1)} %collective-permute-done.7.refs_0_.refs_2_, f32[8,1152]{1,0:T(8,128)S(1)} %collective-permute-done.8.refs_1_.refs_3_, bf16[32,1152]{1,0:T(8,128)(2,1)S(1)} %shard_map.94.refs_0_.refs_2_, ...), custom_call_target="tpu_custom_call" | custom-call | flops 134217728 | bytes 2097152 | tf_op jit(solution)/shard_map/pallas_call | solution.py:38
  26.2 1.0 %collective-permute-done.13.refs_4_ = bf16[8,1152]{1,0:T(8,128)(2,1)S(1)} collective-permute-done((bf16[8,1152]{1,0:T(8,128)(2,1)S(1)}, bf16[8,1152]{1,0:T(8,128)(2,1)S(1)}, u32[]{:S(2)}, u32[]{:S(2)}) %collective-permute-start.13) | collective-permute-done | bytes 18464 | tf_op jit(solution)/shard_map/ppermute | solution.py:322
  27.2 1.1 %shard_map.104 = (bf16[256,1024]{1,0:T(8,128)(2,1)}, f32[2,256]{1,0:T(2,128)}) custom-call(f32[8,128]{1,0:T(8,128)S(1)} %get-tuple-element.44.refs_0_, f32[8,1152]{1,0:T(8,128)S(1)} %get-tuple-element.45.refs_1_, f32[8,1152]{1,0:T(8,128)S(1)} %collective-permute-done.7.refs_0_.refs_2_, f32[8,1152]{1,0:T(8,128)S(1)} %collective-permute-done.8.refs_1_.refs_3_, ...), custom_call_target="tpu_custom_call" | custom-call | flops 16777216 | bytes 524288 | tf_op jit(solution)/shard_map/pallas_call | solution.py:38
  (2 shorter events, 0.0 us)
Async XLA Ops:
  2.4 6.7 %collective-permute-start.2 = (bf16[512,1024]{1,0:T(8,128)(2,1)S(1)}, bf16[512,1024]{1,0:T(8,128)(2,1)S(1)}, u32[]{:S(2)}, u32[]{:S(2)}) collective-permute-start(bf16[512,1024]{1,0:T(8,128)(2,1)S(1)} %get-tuple-element.30.refs_1_.refs_2_.refs_4_), channel_id=1, source_target_pairs={{0,4},{4,0},{1,5},{5,1},{2,6},{6,2},{3,7},{7,3},{8,12},{12,8},{9,1... | collective-permute-start | bytes 3145736 | tf_op jit(solution)/shard_map/ppermute | solution.py:322
  2.9 4.4 %collective-permute-start = (bf16[16,1152]{1,0:T(8,128)(2,1)S(1)}, bf16[16,1152]{1,0:T(8,128)(2,1)S(1)}, u32[]{:S(2)}, u32[]{:S(2)}) collective-permute-start(bf16[16,1152]{1,0:T(8,128)(2,1)S(1)} %get-tuple-element.28.refs_1_), channel_id=1, source_target_pairs={{0,12},{4,8},{8,4},{12,0},{16,28},{20,24},{24,20},{28,16},{1,13},{... | collective-permute-start | bytes 110600 | tf_op jit(solution)/shard_map/ppermute | solution.py:322
  5.5 3.5 %collective-permute-start.1 = (bf16[16,1152]{1,0:T(8,128)(2,1)S(1)}, bf16[16,1152]{1,0:T(8,128)(2,1)S(1)}, u32[]{:S(2)}, u32[]{:S(2)}) collective-permute-start(bf16[16,1152]{1,0:T(8,128)(2,1)S(1)} %get-tuple-element.29), channel_id=1, source_target_pairs={{0,20},{4,16},{8,28},{12,24},{16,4},{20,0},{24,12},{28,8},{1,21},{... | collective-permute-start | bytes 110600 | tf_op jit(solution)/shard_map/ppermute | solution.py:322
  6.7 5.7 %collective-permute-start.3 = (bf16[16,1152]{1,0:T(8,128)(2,1)S(1)}, bf16[16,1152]{1,0:T(8,128)(2,1)S(1)}, u32[]{:S(2)}, u32[]{:S(2)}) collective-permute-start(bf16[16,1152]{1,0:T(8,128)(2,1)S(1)} %get-tuple-element.29), channel_id=1, source_target_pairs={{0,28},{4,24},{8,20},{12,16},{16,12},{20,8},{24,4},{28,0},{1,29},{... | collective-permute-start | bytes 110600 | tf_op jit(solution)/shard_map/ppermute | solution.py:322
  9.8 5.3 %collective-permute-start.4 = (s16[16,1152]{1,0:T(8,128)(2,1)S(1)}, s16[16,1152]{1,0:T(8,128)(2,1)S(1)}, u32[]{:S(2)}, u32[]{:S(2)}) collective-permute-start(s16[16,1152]{1,0:T(8,128)(2,1)S(1)} %get-tuple-element.31.refs_0_.refs_1_), channel_id=1, source_target_pairs={{0,2},{1,3},{2,0},{3,1},{4,6},{5,7},{6,4},{7,5},{8,10},{9,11},{10,... | collective-permute-start | bytes 110600 | tf_op jit(solution)/shard_map/ppermute | solution.py:322
  13.1 5.3 %collective-permute-start.5 = (s16[16,1152]{1,0:T(8,128)(2,1)S(1)}, s16[16,1152]{1,0:T(8,128)(2,1)S(1)}, u32[]{:S(2)}, u32[]{:S(2)}) collective-permute-start(s16[16,1152]{1,0:T(8,128)(2,1)S(1)} %get-tuple-element.32.refs_0_.refs_1_), channel_id=1, source_target_pairs={{0,2},{1,3},{2,0},{3,1},{4,6},{5,7},{6,4},{7,5},{8,10},{9,11},{10,... | collective-permute-start | bytes 110600 | tf_op jit(solution)/shard_map/ppermute | solution.py:322
  14.3 8.7 %collective-permute-start.9 = (bf16[32,1152]{1,0:T(8,128)(2,1)S(1)}, bf16[32,1152]{1,0:T(8,128)(2,1)S(1)}, u32[]{:S(2)}, u32[]{:S(2)}) collective-permute-start(bf16[32,1152]{1,0:T(8,128)(2,1)S(1)} %shard_map.94.refs_0_.refs_2_), channel_id=1, source_target_pairs={{0,4},{4,0},{1,5},{5,1},{2,6},{6,2},{3,7},{7,3},{8,12},{12,8},{9,1... | collective-permute-start | bytes 221192 | tf_op jit(solution)/shard_map/ppermute | solution.py:322
  15.3 4.7 %collective-permute-start.6 = (s16[16,1152]{1,0:T(8,128)(2,1)S(1)}, s16[16,1152]{1,0:T(8,128)(2,1)S(1)}, u32[]{:S(2)}, u32[]{:S(2)}) collective-permute-start(s16[16,1152]{1,0:T(8,128)(2,1)S(1)} %shard_map.98.refs_0_.refs_1_), channel_id=1, source_target_pairs={{0,1},{1,0},{2,3},{3,2},{4,5},{5,4},{6,7},{7,6},{8,9},{9,8},{10,11... | collective-permute-start | bytes 110600 | tf_op jit(solution)/shard_map/ppermute | solution.py:322
  16.5 8.0 %collective-permute-start.10 = (bf16[32,1152]{1,0:T(8,128)(2,1)S(1)}, bf16[32,1152]{1,0:T(8,128)(2,1)S(1)}, u32[]{:S(2)}, u32[]{:S(2)}) collective-permute-start(bf16[32,1152]{1,0:T(8,128)(2,1)S(1)} %shard_map.96.refs_1_.refs_3_), channel_id=1, source_target_pairs={{0,4},{4,0},{1,5},{5,1},{2,6},{6,2},{3,7},{7,3},{8,12},{12,8},{9,1... | collective-permute-start | bytes 221192 | tf_op jit(solution)/shard_map/ppermute | solution.py:322
  18.6 4.0 %collective-permute-start.11 = (s16[16,1152]{1,0:T(8,128)(2,1)S(1)}, s16[16,1152]{1,0:T(8,128)(2,1)S(1)}, u32[]{:S(2)}, u32[]{:S(2)}) collective-permute-start(s16[16,1152]{1,0:T(8,128)(2,1)S(1)} %shard_map.99.refs_0_.refs_1_), channel_id=1, source_target_pairs={{0,1},{1,0},{2,3},{3,2},{4,5},{5,4},{6,7},{7,6},{8,9},{9,8},{10,11... | collective-permute-start | bytes 110600 | tf_op jit(solution)/shard_map/ppermute | solution.py:322
  20.4 4.1 %collective-permute-start.7 = (f32[8,1152]{1,0:T(8,128)S(1)}, f32[8,1152]{1,0:T(8,128)S(1)}, u32[]{:S(2)}, u32[]{:S(2)}) collective-permute-start(f32[8,1152]{1,0:T(8,128)S(1)} %get-tuple-element.34), channel_id=1, source_target_pairs={{0,12},{4,8},{8,4},{12,0},{16,28},{20,24},{24,20},{28,16},{1,13},{... | collective-permute-start | bytes 110600 | tf_op jit(solution)/shard_map/ppermute | solution.py:322
  20.4 4.2 %collective-permute-start.8 = (f32[8,1152]{1,0:T(8,128)S(1)}, f32[8,1152]{1,0:T(8,128)S(1)}, u32[]{:S(2)}, u32[]{:S(2)}) collective-permute-start(f32[8,1152]{1,0:T(8,128)S(1)} %get-tuple-element.35), channel_id=1, source_target_pairs={{0,20},{4,16},{8,28},{12,24},{16,4},{20,0},{24,12},{28,8},{1,21},{... | collective-permute-start | bytes 110600 | tf_op jit(solution)/shard_map/ppermute | solution.py:322
  23.0 1.5 %collective-permute-start.12 = (bf16[64,256]{1,0:T(8,128)(2,1)S(1)}, bf16[64,256]{1,0:T(8,128)(2,1)S(1)}, u32[]{:S(2)}, u32[]{:S(2)}) collective-permute-start(bf16[64,256]{1,0:T(8,128)(2,1)S(1)} %get-tuple-element.43), channel_id=1, source_target_pairs={{0,4},{4,0},{1,5},{5,1},{2,6},{6,2},{3,7},{7,3},{8,12},{12,8},{9,1... | collective-permute-start | bytes 98312 | tf_op jit(solution)/shard_map/ppermute | solution.py:322
  23.1 4.2 %collective-permute-start.13 = (bf16[8,1152]{1,0:T(8,128)(2,1)S(1)}, bf16[8,1152]{1,0:T(8,128)(2,1)S(1)}, u32[]{:S(2)}, u32[]{:S(2)}) collective-permute-start(bf16[8,1152]{1,0:T(8,128)(2,1)S(1)} %get-tuple-element.46), channel_id=1, source_target_pairs={{0,28},{4,24},{8,20},{12,16},{16,12},{20,8},{24,4},{28,0},{1,29},{... | collective-permute-start | bytes 55304 | tf_op jit(solution)/shard_map/ppermute | solution.py:322

commit v9 on v6

--- a/solution.py
+++ b/solution.py
@@ -378,10 +378,12 @@
     for step in range(1, nodes):
         pieces.append(swap_nodes(own_rows if step < half_nodes else other_rows, step))
     rows = half_nodes * (locals_ // 2) * capacity
+    bits = [1 << place for place in range(edatas.bit_length() - 1)]
+    orders = (bits[::-1], bits)
     last = ()
     chains = []
     held = []
-    for chunk in (pieces[:half_nodes], pieces[half_nodes:]):
+    for chunk, order in zip((pieces[:half_nodes], pieces[half_nodes:]), orders):
         chunk = join(chunk, last)
         bit = 2
         while bit < locals_:
@@ -396,9 +398,8 @@
             after=last,
         )(chunk, weights, other_weights)
         last = (part,)
-        chains.append((part, swap(part, "edata", edatas // 2), gate_rows))
-    bit = edatas // 4
-    while bit:
+        chains.append((part, swap(part, "edata", order[0]), gate_rows))
+    for stage in range(1, len(bits)):
         for index, (part, other, gate_rows) in enumerate(chains):
             part = call(
                 add_codes_kernel,
@@ -408,8 +409,7 @@
                 after=last,
             )(part, other)
             last = (part,)
-            chains[index] = (part, swap(part, "edata", bit), gate_rows)
-        bit //= 2
+            chains[index] = (part, swap(part, "edata", orders[index][stage]), gate_rows)
 
     mine = []
     theirs = ()

time: 28 us -> 28.3 us (1.011)
  starting transfers between devices: 15.4 us -> 16.6 us
  waiting for transfers between devices: 4.56 us -> 3.67 us
    ppermute x14, starting transfers between devices: 15.4 us -> 16.6 us  [swap(): lax.ppermute(array, axes, [(index, index ^ bit) for index in range(size)])]
    ppermute x14, waiting for transfers between devices: 4.56 us -> 3.67 us  [swap(): lax.ppermute(array, axes, [(index, index ^ bit) for index in range(size)])]
  transfers between devices with their start and end apart: 14 -> 14, of which waited for: 6 -> 5; matrix products, arithmetic and copies ran while one was open for 0% -> 0% of each run, Pallas kernels for 15% -> 15%
where the time goes in v9:
time: 28.3 us; the launch traced here: 28.1 us
  starting transfers between devices  16.6 us (59%)
  Pallas kernels  7.11 us (25%)
  waiting for transfers between devices  3.67 us (13%)
  between operations  0.72 us (3%)
    ppermute x14, starting transfers between devices, swap(): lax.ppermute(array, axes, [(index, index ^ bit) for index in range(size)])  16.6 us
    pallas_call x12, Pallas kernels, run(): pl.pallas_call(lambda *refs: kernel(*refs[len(after):]), out_shape=out_sh...  7.11 us
    ppermute x14, waiting for transfers between devices, swap(): lax.ppermute(array, axes, [(index, index ^ bit) for index in range(size)])  3.67 us
  transfers between devices with their start and end apart: 14, of which 5 were waited for; matrix products, arithmetic and copies ran while one was open for 0% of the time, Pallas kernels for 15%

profile of v9, /device:TPU:0, one launch (start us, length us, event | category | flops | bytes accessed | tf_op | source)
XLA Modules:
  0.0 28.1 jit_solution(18139165196901971651)
XLA Ops:
  0.6 1.8 %shard_map.93 = (bf16[16,1152]{1,0:T(8,128)(2,1)S(1)}, bf16[16,1152]{1,0:T(8,128)(2,1)S(1)}, bf16[16,256]{1,0:T(8,128)(2,1)S(1)}, s32[2,256]{1,0:T(2,128)S(1)}, bf16[512,1024]{1,0:T(8,128)(2,1)S(1)}) custom-call(s32[2,256]{1,0:T(2,128)} %bitcast.3, bf16[2,256]{1,0:T(2,128)(2,1)} %bitcast.4, bf16[256,1024]{1,0:T(8,128)(2,1)} %refs_2_.1, ...), custom_call_target="tpu_custom_call" | custom-call | flops 16777216 | bytes 2097152 | tf_op jit(solution)/shard_map/pallas_call | solution.py:38
  2.4 0.5 %collective-permute-start.1 = (bf16[512,1024]{1,0:T(8,128)(2,1)S(1)}, bf16[512,1024]{1,0:T(8,128)(2,1)S(1)}, u32[]{:S(2)}, u32[]{:S(2)}) collective-permute-start(bf16[512,1024]{1,0:T(8,128)(2,1)S(1)} %get-tuple-element.29.refs_1_.refs_2_.refs_4_), channel_id=1, source_target_pairs={{0,4},{4,0},{1,5},{5,1},{2,6},{6,2},{3,7},{7,3},{8,12},{12,8},{9,1... | collective-permute-start | bytes 3145736 | tf_op jit(solution)/shard_map/ppermute | solution.py:322
  2.9 2.6 %collective-permute-start = (bf16[16,1152]{1,0:T(8,128)(2,1)S(1)}, bf16[16,1152]{1,0:T(8,128)(2,1)S(1)}, u32[]{:S(2)}, u32[]{:S(2)}) collective-permute-start(bf16[16,1152]{1,0:T(8,128)(2,1)S(1)} %get-tuple-element.28.refs_0_), channel_id=1, source_target_pairs={{0,12},{4,8},{8,4},{12,0},{16,28},{20,24},{24,20},{28,16},{1,13},{... | collective-permute-start | bytes 110600 | tf_op jit(solution)/shard_map/ppermute | solution.py:322
  5.5 1.2 %collective-permute-start.3 = (bf16[16,1152]{1,0:T(8,128)(2,1)S(1)}, bf16[16,1152]{1,0:T(8,128)(2,1)S(1)}, u32[]{:S(2)}, u32[]{:S(2)}) collective-permute-start(bf16[16,1152]{1,0:T(8,128)(2,1)S(1)} %get-tuple-element.31), channel_id=1, source_target_pairs={{0,28},{4,24},{8,20},{12,16},{16,12},{20,8},{24,4},{28,0},{1,29},{... | collective-permute-start | bytes 110600 | tf_op jit(solution)/shard_map/ppermute | solution.py:322
  6.7 0.1 collective-permute-start.2
  6.7 0.5 %collective-permute-done.refs_1_ = bf16[16,1152]{1,0:T(8,128)(2,1)S(1)} collective-permute-done((bf16[16,1152]{1,0:T(8,128)(2,1)S(1)}, bf16[16,1152]{1,0:T(8,128)(2,1)S(1)}, u32[]{:S(2)}, u32[]{:S(2)}) %collective-permute-start) | collective-permute-done | bytes 36896 | tf_op jit(solution)/shard_map/ppermute | solution.py:322
  7.3 0.0 collective-permute-done.1.refs_2_.refs_3_.refs_5_
  7.3 0.7 %shard_map.95 = (s16[16,1152]{1,0:T(8,128)(2,1)S(1)}, f32[16,128]{1,0:T(8,128)S(1)}) custom-call(bf16[32,1152]{1,0:T(8,128)(2,1)S(1)} %shard_map.94.refs_0_.refs_1_, bf16[512,1024]{1,0:T(8,128)(2,1)S(1)} %get-tuple-element.29.refs_1_.refs_2_.refs_4_, bf16[512,1024]{1,0:T(8,128)(2,1)S(1)} %collective-permute-done.1.refs_2_.refs_3_.refs_5_), custom_call_target="tpu_custom_call" | custom-call | flops 67108864 | bytes 2162688 | tf_op jit(solution)/shard_map/pallas_call | solution.py:38
  8.0 2.7 %collective-permute-start.4 = (s16[16,1152]{1,0:T(8,128)(2,1)S(1)}, s16[16,1152]{1,0:T(8,128)(2,1)S(1)}, u32[]{:S(2)}, u32[]{:S(2)}) collective-permute-start(s16[16,1152]{1,0:T(8,128)(2,1)S(1)} %get-tuple-element.30.refs_0_.refs_1_), channel_id=1, source_target_pairs={{0,2},{1,3},{2,0},{3,1},{4,6},{5,7},{6,4},{7,5},{8,10},{9,11},{10,... | collective-permute-start | bytes 110600 | tf_op jit(solution)/shard_map/ppermute | solution.py:322
  10.7 0.0 collective-permute-done.3.refs_2_
  10.7 0.2 collective-permute-done.2.refs_1_
  10.9 0.7 %shard_map.97 = (s16[16,1152]{1,0:T(8,128)(2,1)S(1)}, f32[16,128]{1,0:T(8,128)S(1)}) custom-call(s16[16,1152]{1,0:T(8,128)(2,1)S(1)} %get-tuple-element.30.refs_0_.refs_1_, bf16[32,1152]{1,0:T(8,128)(2,1)S(1)} %shard_map.96.refs_1_.refs_2_, bf16[512,1024]{1,0:T(8,128)(2,1)S(1)} %get-tuple-element.29.refs_1_.refs_2_.refs_4_, ...), custom_call_target="tpu_custom_call" | custom-call | flops 67108864 | bytes 2162688 | tf_op jit(solution)/shard_map/pallas_call | solution.py:38
  11.6 1.6 %collective-permute-start.5 = (s16[16,1152]{1,0:T(8,128)(2,1)S(1)}, s16[16,1152]{1,0:T(8,128)(2,1)S(1)}, u32[]{:S(2)}, u32[]{:S(2)}) collective-permute-start(s16[16,1152]{1,0:T(8,128)(2,1)S(1)} %get-tuple-element.32.refs_0_.refs_1_), channel_id=1, source_target_pairs={{0,1},{1,0},{2,3},{3,2},{4,5},{5,4},{6,7},{7,6},{8,9},{9,8},{10,11... | collective-permute-start | bytes 110600 | tf_op jit(solution)/shard_map/ppermute | solution.py:322
  13.2 0.0 collective-permute-start.8
  13.2 0.0 collective-permute-done.4.refs_2_
  13.2 0.2 shard_map.98.refs_0_.refs_1_
  13.4 1.4 %collective-permute-start.6 = (s16[16,1152]{1,0:T(8,128)(2,1)S(1)}, s16[16,1152]{1,0:T(8,128)(2,1)S(1)}, u32[]{:S(2)}, u32[]{:S(2)}) collective-permute-start(s16[16,1152]{1,0:T(8,128)(2,1)S(1)} %shard_map.98.refs_0_.refs_1_), channel_id=1, source_target_pairs={{0,1},{1,0},{2,3},{3,2},{4,5},{5,4},{6,7},{7,6},{8,9},{9,8},{10,11... | collective-permute-start | bytes 110600 | tf_op jit(solution)/shard_map/ppermute | solution.py:322
  14.8 0.0 collective-permute-start.9
  14.8 0.8 %collective-permute-done.5.refs_2_ = s16[16,1152]{1,0:T(8,128)(2,1)S(1)} collective-permute-done((s16[16,1152]{1,0:T(8,128)(2,1)S(1)}, s16[16,1152]{1,0:T(8,128)(2,1)S(1)}, u32[]{:S(2)}, u32[]{:S(2)}) %collective-permute-start.5) | collective-permute-done | bytes 36896 | tf_op jit(solution)/shard_map/ppermute | solution.py:322
  15.6 0.2 shard_map.99.refs_0_.refs_1_
  15.8 2.7 %collective-permute-start.10 = (s16[16,1152]{1,0:T(8,128)(2,1)S(1)}, s16[16,1152]{1,0:T(8,128)(2,1)S(1)}, u32[]{:S(2)}, u32[]{:S(2)}) collective-permute-start(s16[16,1152]{1,0:T(8,128)(2,1)S(1)} %shard_map.99.refs_0_.refs_1_), channel_id=1, source_target_pairs={{0,2},{1,3},{2,0},{3,1},{4,6},{5,7},{6,4},{7,5},{8,10},{9,11},{10,... | collective-permute-start | bytes 110600 | tf_op jit(solution)/shard_map/ppermute | solution.py:322
  18.4 0.0 collective-permute-done.6.refs_2_
  18.5 0.4 %shard_map.100 = (bf16[32,256]{1,0:T(8,128)(2,1)S(1)}, bf16[32,256]{1,0:T(8,128)(2,1)S(1)}, f32[8,1152]{1,0:T(8,128)S(1)}, f32[8,1152]{1,0:T(8,128)S(1)}) custom-call(s16[16,1152]{1,0:T(8,128)(2,1)S(1)} %shard_map.99.refs_0_.refs_1_, s16[16,1152]{1,0:T(8,128)(2,1)S(1)} %shard_map.98.refs_0_.refs_1_, s16[16,1152]{1,0:T(8,128)(2,1)S(1)} %collective-permute-done.6.refs_2_, ...), custom_call_target="tpu_custom_call" | custom-call | flops 16777216 | bytes 1114112 | tf_op jit(solution)/shard_map/pallas_call | solution.py:38
  18.9 1.1 %collective-permute-start.7 = (f32[8,1152]{1,0:T(8,128)S(1)}, f32[8,1152]{1,0:T(8,128)S(1)}, u32[]{:S(2)}, u32[]{:S(2)}) collective-permute-start(f32[8,1152]{1,0:T(8,128)S(1)} %get-tuple-element.34), channel_id=1, source_target_pairs={{0,12},{4,8},{8,4},{12,0},{16,28},{20,24},{24,20},{28,16},{1,13},{... | collective-permute-start | bytes 110600 | tf_op jit(solution)/shard_map/ppermute | solution.py:322
  20.0 0.1 shard_map.101
  20.1 0.6 %collective-permute-done.10.refs_2_ = s16[16,1152]{1,0:T(8,128)(2,1)S(1)} collective-permute-done((s16[16,1152]{1,0:T(8,128)(2,1)S(1)}, s16[16,1152]{1,0:T(8,128)(2,1)S(1)}, u32[]{:S(2)}, u32[]{:S(2)}) %collective-permute-start.10) | collective-permute-done | bytes 36896 | tf_op jit(solution)/shard_map/ppermute | solution.py:322
  20.7 0.4 %shard_map.102 = (bf16[32,256]{1,0:T(8,128)(2,1)S(1)}, bf16[64,256]{1,0:T(8,128)(2,1)S(1)}, bf16[8,1152]{1,0:T(8,128)(2,1)S(1)}, bf16[8,1152]{1,0:T(8,128)(2,1)S(1)}) custom-call(bf16[256,32]{1,0:T(8,128)(2,1)S(1)} %get-tuple-element.38.refs_0_.refs_6_, s16[16,1152]{1,0:T(8,128)(2,1)S(1)} %shard_map.99.refs_0_.refs_1_, ...), custom_call_target="tpu_custom_call" | custom-call | flops 16777216 | bytes 1114112 | tf_op jit(solution)/shard_map/pallas_call | solution.py:38
  21.1 0.0 collective-permute-start.11
  21.1 2.7 %collective-permute-start.12 = (bf16[8,1152]{1,0:T(8,128)(2,1)S(1)}, bf16[8,1152]{1,0:T(8,128)(2,1)S(1)}, u32[]{:S(2)}, u32[]{:S(2)}) collective-permute-start(bf16[8,1152]{1,0:T(8,128)(2,1)S(1)} %get-tuple-element.45), channel_id=1, source_target_pairs={{0,28},{4,24},{8,20},{12,16},{16,12},{20,8},{24,4},{28,0},{1,29},{... | collective-permute-start | bytes 55304 | tf_op jit(solution)/shard_map/ppermute | solution.py:322
  23.8 0.0 collective-permute-done.8.refs_3_
  23.8 0.0 collective-permute-start.13
  23.9 0.0 collective-permute-done.9.refs_4_
  23.9 0.0 collective-permute-done.11.refs_7_
  23.9 0.0 collective-permute-done.7.refs_0_.refs_2_
  23.9 1.6 %shard_map.103 = (f32[1024,256]{1,0:T(8,128)}, f32[256,1024]{1,0:T(8,128)}, f32[8,128]{1,0:T(8,128)S(1)}) custom-call(f32[8,1152]{1,0:T(8,128)S(1)} %collective-permute-done.7.refs_0_.refs_2_, bf16[32,1152]{1,0:T(8,128)(2,1)S(1)} %shard_map.94.refs_0_.refs_1_, bf16[32,1152]{1,0:T(8,128)(2,1)S(1)} %shard_map.96.refs_1_.refs_2_, ...), custom_call_target="tpu_custom_call" | custom-call | flops 134217728 | bytes 2097152 | tf_op jit(solution)/shard_map/pallas_call | solution.py:38
  25.5 0.0 collective-permute-done.12.refs_3_
  25.5 1.5 %collective-permute-done.13.refs_4_ = bf16[8,1152]{1,0:T(8,128)(2,1)S(1)} collective-permute-done((bf16[8,1152]{1,0:T(8,128)(2,1)S(1)}, bf16[8,1152]{1,0:T(8,128)(2,1)S(1)}, u32[]{:S(2)}, u32[]{:S(2)}) %collective-permute-start.13) | collective-permute-done | bytes 18464 | tf_op jit(solution)/shard_map/ppermute | solution.py:322
  27.0 1.1 %shard_map.104 = (bf16[256,1024]{1,0:T(8,128)(2,1)}, f32[2,256]{1,0:T(2,128)}) custom-call(f32[8,128]{1,0:T(8,128)S(1)} %get-tuple-element.43.refs_0_, f32[8,1152]{1,0:T(8,128)S(1)} %get-tuple-element.44.refs_1_, f32[8,1152]{1,0:T(8,128)S(1)} %collective-permute-done.7.refs_0_.refs_2_, bf16[8,1152]{1,0:T(8,128)(2,1)S(1)} %collective-permute-done.12.refs_3_, ...), custom_call_target="tpu_custom_call" | custom-call | flops 16777216 | bytes 524288 | tf_op jit(solution)/shard_map/pallas_call | solution.py:38
  (2 shorter events, 0.0 us)
Async XLA Ops:
  2.4 4.9 %collective-permute-start.1 = (bf16[512,1024]{1,0:T(8,128)(2,1)S(1)}, bf16[512,1024]{1,0:T(8,128)(2,1)S(1)}, u32[]{:S(2)}, u32[]{:S(2)}) collective-permute-start(bf16[512,1024]{1,0:T(8,128)(2,1)S(1)} %get-tuple-element.29.refs_1_.refs_2_.refs_4_), channel_id=1, source_target_pairs={{0,4},{4,0},{1,5},{5,1},{2,6},{6,2},{3,7},{7,3},{8,12},{12,8},{9,1... | collective-permute-start | bytes 3145736 | tf_op jit(solution)/shard_map/ppermute | solution.py:322
  2.9 4.4 %collective-permute-start = (bf16[16,1152]{1,0:T(8,128)(2,1)S(1)}, bf16[16,1152]{1,0:T(8,128)(2,1)S(1)}, u32[]{:S(2)}, u32[]{:S(2)}) collective-permute-start(bf16[16,1152]{1,0:T(8,128)(2,1)S(1)} %get-tuple-element.28.refs_0_), channel_id=1, source_target_pairs={{0,12},{4,8},{8,4},{12,0},{16,28},{20,24},{24,20},{28,16},{1,13},{... | collective-permute-start | bytes 110600 | tf_op jit(solution)/shard_map/ppermute | solution.py:322
  5.5 5.2 %collective-permute-start.3 = (bf16[16,1152]{1,0:T(8,128)(2,1)S(1)}, bf16[16,1152]{1,0:T(8,128)(2,1)S(1)}, u32[]{:S(2)}, u32[]{:S(2)}) collective-permute-start(bf16[16,1152]{1,0:T(8,128)(2,1)S(1)} %get-tuple-element.31), channel_id=1, source_target_pairs={{0,28},{4,24},{8,20},{12,16},{16,12},{20,8},{24,4},{28,0},{1,29},{... | collective-permute-start | bytes 110600 | tf_op jit(solution)/shard_map/ppermute | solution.py:322
  6.7 4.2 %collective-permute-start.2 = (bf16[16,1152]{1,0:T(8,128)(2,1)S(1)}, bf16[16,1152]{1,0:T(8,128)(2,1)S(1)}, u32[]{:S(2)}, u32[]{:S(2)}) collective-permute-start(bf16[16,1152]{1,0:T(8,128)(2,1)S(1)} %get-tuple-element.31), channel_id=1, source_target_pairs={{0,20},{4,16},{8,28},{12,24},{16,4},{20,0},{24,12},{28,8},{1,21},{... | collective-permute-start | bytes 110600 | tf_op jit(solution)/shard_map/ppermute | solution.py:322
  8.0 5.3 %collective-permute-start.4 = (s16[16,1152]{1,0:T(8,128)(2,1)S(1)}, s16[16,1152]{1,0:T(8,128)(2,1)S(1)}, u32[]{:S(2)}, u32[]{:S(2)}) collective-permute-start(s16[16,1152]{1,0:T(8,128)(2,1)S(1)} %get-tuple-element.30.refs_0_.refs_1_), channel_id=1, source_target_pairs={{0,2},{1,3},{2,0},{3,1},{4,6},{5,7},{6,4},{7,5},{8,10},{9,11},{10,... | collective-permute-start | bytes 110600 | tf_op jit(solution)/shard_map/ppermute | solution.py:322
  11.6 4.0 %collective-permute-start.5 = (s16[16,1152]{1,0:T(8,128)(2,1)S(1)}, s16[16,1152]{1,0:T(8,128)(2,1)S(1)}, u32[]{:S(2)}, u32[]{:S(2)}) collective-permute-start(s16[16,1152]{1,0:T(8,128)(2,1)S(1)} %get-tuple-element.32.refs_0_.refs_1_), channel_id=1, source_target_pairs={{0,1},{1,0},{2,3},{3,2},{4,5},{5,4},{6,7},{7,6},{8,9},{9,8},{10,11... | collective-permute-start | bytes 110600 | tf_op jit(solution)/shard_map/ppermute | solution.py:322
  13.2 10.6 %collective-permute-start.8 = (bf16[32,1152]{1,0:T(8,128)(2,1)S(1)}, bf16[32,1152]{1,0:T(8,128)(2,1)S(1)}, u32[]{:S(2)}, u32[]{:S(2)}) collective-permute-start(bf16[32,1152]{1,0:T(8,128)(2,1)S(1)} %shard_map.94.refs_0_.refs_1_), channel_id=1, source_target_pairs={{0,4},{4,0},{1,5},{5,1},{2,6},{6,2},{3,7},{7,3},{8,12},{12,8},{9,1... | collective-permute-start | bytes 221192 | tf_op jit(solution)/shard_map/ppermute | solution.py:322
  13.4 5.0 %collective-permute-start.6 = (s16[16,1152]{1,0:T(8,128)(2,1)S(1)}, s16[16,1152]{1,0:T(8,128)(2,1)S(1)}, u32[]{:S(2)}, u32[]{:S(2)}) collective-permute-start(s16[16,1152]{1,0:T(8,128)(2,1)S(1)} %shard_map.98.refs_0_.refs_1_), channel_id=1, source_target_pairs={{0,1},{1,0},{2,3},{3,2},{4,5},{5,4},{6,7},{7,6},{8,9},{9,8},{10,11... | collective-permute-start | bytes 110600 | tf_op jit(solution)/shard_map/ppermute | solution.py:322
  14.8 9.0 %collective-permute-start.9 = (bf16[32,1152]{1,0:T(8,128)(2,1)S(1)}, bf16[32,1152]{1,0:T(8,128)(2,1)S(1)}, u32[]{:S(2)}, u32[]{:S(2)}) collective-permute-start(bf16[32,1152]{1,0:T(8,128)(2,1)S(1)} %shard_map.96.refs_1_.refs_2_), channel_id=1, source_target_pairs={{0,4},{4,0},{1,5},{5,1},{2,6},{6,2},{3,7},{7,3},{8,12},{12,8},{9,1... | collective-permute-start | bytes 221192 | tf_op jit(solution)/shard_map/ppermute | solution.py:322
  15.8 4.9 %collective-permute-start.10 = (s16[16,1152]{1,0:T(8,128)(2,1)S(1)}, s16[16,1152]{1,0:T(8,128)(2,1)S(1)}, u32[]{:S(2)}, u32[]{:S(2)}) collective-permute-start(s16[16,1152]{1,0:T(8,128)(2,1)S(1)} %shard_map.99.refs_0_.refs_1_), channel_id=1, source_target_pairs={{0,2},{1,3},{2,0},{3,1},{4,6},{5,7},{6,4},{7,5},{8,10},{9,11},{10,... | collective-permute-start | bytes 110600 | tf_op jit(solution)/shard_map/ppermute | solution.py:322
  18.9 5.0 %collective-permute-start.7 = (f32[8,1152]{1,0:T(8,128)S(1)}, f32[8,1152]{1,0:T(8,128)S(1)}, u32[]{:S(2)}, u32[]{:S(2)}) collective-permute-start(f32[8,1152]{1,0:T(8,128)S(1)} %get-tuple-element.34), channel_id=1, source_target_pairs={{0,12},{4,8},{8,4},{12,0},{16,28},{20,24},{24,20},{28,16},{1,13},{... | collective-permute-start | bytes 110600 | tf_op jit(solution)/shard_map/ppermute | solution.py:322
  21.1 2.7 %collective-permute-start.11 = (bf16[64,256]{1,0:T(8,128)(2,1)S(1)}, bf16[64,256]{1,0:T(8,128)(2,1)S(1)}, u32[]{:S(2)}, u32[]{:S(2)}) collective-permute-start(bf16[64,256]{1,0:T(8,128)(2,1)S(1)} %get-tuple-element.42), channel_id=1, source_target_pairs={{0,4},{4,0},{1,5},{5,1},{2,6},{6,2},{3,7},{7,3},{8,12},{12,8},{9,1... | collective-permute-start | bytes 98312 | tf_op jit(solution)/shard_map/ppermute | solution.py:322
  21.1 4.4 %collective-permute-start.12 = (bf16[8,1152]{1,0:T(8,128)(2,1)S(1)}, bf16[8,1152]{1,0:T(8,128)(2,1)S(1)}, u32[]{:S(2)}, u32[]{:S(2)}) collective-permute-start(bf16[8,1152]{1,0:T(8,128)(2,1)S(1)} %get-tuple-element.45), channel_id=1, source_target_pairs={{0,28},{4,24},{8,20},{12,16},{16,12},{20,8},{24,4},{28,0},{1,29},{... | collective-permute-start | bytes 55304 | tf_op jit(solution)/shard_map/ppermute | solution.py:322
  23.8 3.2 %collective-permute-start.13 = (bf16[8,1152]{1,0:T(8,128)(2,1)S(1)}, bf16[8,1152]{1,0:T(8,128)(2,1)S(1)}, u32[]{:S(2)}, u32[]{:S(2)}) collective-permute-start(bf16[8,1152]{1,0:T(8,128)(2,1)S(1)} %get-tuple-element.46), channel_id=1, source_target_pairs={{0,20},{4,16},{8,28},{12,24},{16,4},{20,0},{24,12},{28,8},{1,21},{... | collective-permute-start | bytes 55304 | tf_op jit(solution)/shard_map/ppermute | solution.py:322

commit v10 on v6

--- a/solution.py
+++ b/solution.py
@@ -263,8 +263,8 @@
 
 
 def weight_kernel(capacity, *refs):
-    rows_refs, both_refs = refs[:4], refs[4:7]
-    w_in_hbm, w_out_hbm, written_ref, w_in_ref, w_out_ref, sems = refs[7:]
+    rows_refs, both_refs = refs[:4], refs[4:8]
+    w_in_hbm, w_out_hbm, written_ref, w_in_ref, w_out_ref, sems = refs[8:]
     feats, hidden = w_in_ref.shape
     rows = jnp.concatenate([ref[:, :feats] for ref in rows_refs], axis=0)
     both = jnp.concatenate([ref[...] for ref in both_refs], axis=0).astype(F32)
@@ -417,16 +417,16 @@
     for index, (part, other, gate_rows) in enumerate(chains):
         dealt = [shape((capacity, wide), BF16 if index else F32)] * half_nodes
         own, packed, *slot_parts = call(
-            functools.partial(slot_kernel, capacity, len(theirs)),
+            functools.partial(slot_kernel, capacity, 0),
             [
                 shape((2 * rows, hidden), BF16),
-                shape(((1 + len(theirs)) * 2 * rows, hidden), BF16),
+                shape((2 * rows, hidden), BF16),
                 *(dealt if locals_ == 2 else [shape((rows, wide), F32)]),
             ],
             4 * rows * feats * hidden,
             4 * feats * hidden + 4 * rows * feats,
             after=last,
-        )(part, other, gate_rows, weights, other_weights, *theirs)
+        )(part, other, gate_rows, weights, other_weights)
         last = (own,)
         if index == 0:
             spread, masks = call(
@@ -438,7 +438,7 @@
             )(place, routes)
             last = (spread,)
         mine.append(own)
-        theirs = (packed,)
+        theirs += (packed,)
         if locals_ > 2:
             half = rows // 2
             keep, send = slot_parts[0][:half], slot_parts[0][half:]
@@ -458,13 +458,13 @@
         for step, send in enumerate(slot_parts, index * half_nodes):
             slots_back.append(swap_nodes(send, step) if step else send)
     came = [swap(chunk, "local", 1) for chunk in held]
-    back = swap(theirs[0], "local", 1)
+    back = [swap(packed, "local", 1) for packed in theirs]
     grad_w_in, grad_w_out, written = call(
         functools.partial(weight_kernel, capacity),
         (shape((feats, hidden), F32), shape((hidden, feats), F32), shape((8, LANES), F32)),
-        32 * rows * feats * hidden,
-        8 * feats * hidden,
-        in_specs=[vmem] * 7,
+        0,
+        0,
+        in_specs=[vmem] * 8,
         after=slots_back[1:half_nodes],
         out_specs=[hbm, hbm, vmem],
         scratch_shapes=[
@@ -472,7 +472,7 @@
             pltpu.VMEM((hidden, feats), F32),
             pltpu.SemaphoreType.DMA((2 * PIECES,)),
         ],
-    )(*held, *came, *mine, back)
+    )(*held, *came, *mine, *back)
     grad_tokens, grad_gates = call(
         functools.partial(combine_kernel, nodes),
         (shape((tok_rows, feats), BF16), shape((2, tok_rows), F32)),

time: 28 us -> 28.3 us (1.011)
  starting transfers between devices: 15.4 us -> 16.2 us
  waiting for transfers between devices: 4.56 us -> 4.13 us
    ppermute x14 -> x15, starting transfers between devices: 15.4 us -> 16.2 us  [swap(): lax.ppermute(array, axes, [(index, index ^ bit) for index in range(size)])]
    ppermute x14 -> x15, waiting for transfers between devices: 4.56 us -> 4.13 us  [swap(): lax.ppermute(array, axes, [(index, index ^ bit) for index in range(size)])]
  transfers between devices with their start and end apart: 14 -> 15, of which waited for: 6 -> 7; matrix products, arithmetic and copies ran while one was open for 0% -> 0% of each run, Pallas kernels for 15% -> 15%
where the time goes in v10:
time: 28.3 us; the launch traced here: 28.1 us
  starting transfers between devices  16.2 us (57%)
  Pallas kernels  7.13 us (25%)
  waiting for transfers between devices  4.13 us (15%)
  between operations  0.71 us (3%)
    ppermute x15, starting transfers between devices, swap(): lax.ppermute(array, axes, [(index, index ^ bit) for index in range(size)])  16.2 us
    pallas_call x12, Pallas kernels, run(): pl.pallas_call(lambda *refs: kernel(*refs[len(after):]), out_shape=out_sh...  7.13 us
    ppermute x15, waiting for transfers between devices, swap(): lax.ppermute(array, axes, [(index, index ^ bit) for index in range(size)])  4.13 us
  transfers between devices with their start and end apart: 15, of which 7 were waited for; matrix products, arithmetic and copies ran while one was open for 0% of the time, Pallas kernels for 15%

profile of v10, /device:TPU:0, one launch (start us, length us, event | category | flops | bytes accessed | tf_op | source)
XLA Modules:
  0.0 28.1 jit_solution(4981719879615907564)
XLA Ops:
  0.6 1.8 %shard_map.93 = (bf16[16,1152]{1,0:T(8,128)(2,1)S(1)}, bf16[16,1152]{1,0:T(8,128)(2,1)S(1)}, bf16[16,256]{1,0:T(8,128)(2,1)S(1)}, s32[2,256]{1,0:T(2,128)S(1)}, bf16[512,1024]{1,0:T(8,128)(2,1)S(1)}) custom-call(s32[2,256]{1,0:T(2,128)} %bitcast.3, bf16[2,256]{1,0:T(2,128)(2,1)} %bitcast.4, bf16[256,1024]{1,0:T(8,128)(2,1)} %refs_2_.1, ...), custom_call_target="tpu_custom_call" | custom-call | flops 16777216 | bytes 2097152 | tf_op jit(solution)/shard_map/pallas_call | solution.py:38
  2.4 0.5 %collective-permute-start.1 = (bf16[512,1024]{1,0:T(8,128)(2,1)S(1)}, bf16[512,1024]{1,0:T(8,128)(2,1)S(1)}, u32[]{:S(2)}, u32[]{:S(2)}) collective-permute-start(bf16[512,1024]{1,0:T(8,128)(2,1)S(1)} %get-tuple-element.29.refs_1_.refs_2_.refs_4_), channel_id=1, source_target_pairs={{0,4},{4,0},{1,5},{5,1},{2,6},{6,2},{3,7},{7,3},{8,12},{12,8},{9,1... | collective-permute-start | bytes 3145736 | tf_op jit(solution)/shard_map/ppermute | solution.py:322
  2.9 2.6 %collective-permute-start = (bf16[16,1152]{1,0:T(8,128)(2,1)S(1)}, bf16[16,1152]{1,0:T(8,128)(2,1)S(1)}, u32[]{:S(2)}, u32[]{:S(2)}) collective-permute-start(bf16[16,1152]{1,0:T(8,128)(2,1)S(1)} %get-tuple-element.28.refs_0_), channel_id=1, source_target_pairs={{0,12},{4,8},{8,4},{12,0},{16,28},{20,24},{24,20},{28,16},{1,13},{... | collective-permute-start | bytes 110600 | tf_op jit(solution)/shard_map/ppermute | solution.py:322
  5.5 1.2 %collective-permute-start.3 = (bf16[16,1152]{1,0:T(8,128)(2,1)S(1)}, bf16[16,1152]{1,0:T(8,128)(2,1)S(1)}, u32[]{:S(2)}, u32[]{:S(2)}) collective-permute-start(bf16[16,1152]{1,0:T(8,128)(2,1)S(1)} %get-tuple-element.31), channel_id=1, source_target_pairs={{0,28},{4,24},{8,20},{12,16},{16,12},{20,8},{24,4},{28,0},{1,29},{... | collective-permute-start | bytes 110600 | tf_op jit(solution)/shard_map/ppermute | solution.py:322
  6.7 0.1 collective-permute-start.2
  6.7 0.5 %collective-permute-done.refs_1_ = bf16[16,1152]{1,0:T(8,128)(2,1)S(1)} collective-permute-done((bf16[16,1152]{1,0:T(8,128)(2,1)S(1)}, bf16[16,1152]{1,0:T(8,128)(2,1)S(1)}, u32[]{:S(2)}, u32[]{:S(2)}) %collective-permute-start) | collective-permute-done | bytes 36896 | tf_op jit(solution)/shard_map/ppermute | solution.py:322
  7.3 0.0 collective-permute-done.1.refs_2_.refs_3_.refs_5_
  7.3 0.7 %shard_map.95 = (s16[16,1152]{1,0:T(8,128)(2,1)S(1)}, f32[16,128]{1,0:T(8,128)S(1)}) custom-call(bf16[32,1152]{1,0:T(8,128)(2,1)S(1)} %shard_map.94.refs_0_.refs_1_, bf16[512,1024]{1,0:T(8,128)(2,1)S(1)} %get-tuple-element.29.refs_1_.refs_2_.refs_4_, bf16[512,1024]{1,0:T(8,128)(2,1)S(1)} %collective-permute-done.1.refs_2_.refs_3_.refs_5_), custom_call_target="tpu_custom_call" | custom-call | flops 67108864 | bytes 2162688 | tf_op jit(solution)/shard_map/pallas_call | solution.py:38
  8.0 2.7 %collective-permute-start.4 = (s16[16,1152]{1,0:T(8,128)(2,1)S(1)}, s16[16,1152]{1,0:T(8,128)(2,1)S(1)}, u32[]{:S(2)}, u32[]{:S(2)}) collective-permute-start(s16[16,1152]{1,0:T(8,128)(2,1)S(1)} %get-tuple-element.30.refs_0_.refs_1_), channel_id=1, source_target_pairs={{0,2},{1,3},{2,0},{3,1},{4,6},{5,7},{6,4},{7,5},{8,10},{9,11},{10,... | collective-permute-start | bytes 110600 | tf_op jit(solution)/shard_map/ppermute | solution.py:322
  10.7 0.0 collective-permute-done.3.refs_2_
  10.7 0.2 collective-permute-done.2.refs_1_
  10.9 0.7 %shard_map.97 = (s16[16,1152]{1,0:T(8,128)(2,1)S(1)}, f32[16,128]{1,0:T(8,128)S(1)}) custom-call(s16[16,1152]{1,0:T(8,128)(2,1)S(1)} %get-tuple-element.30.refs_0_.refs_1_, bf16[32,1152]{1,0:T(8,128)(2,1)S(1)} %shard_map.96.refs_1_.refs_2_, bf16[512,1024]{1,0:T(8,128)(2,1)S(1)} %get-tuple-element.29.refs_1_.refs_2_.refs_4_, ...), custom_call_target="tpu_custom_call" | custom-call | flops 67108864 | bytes 2162688 | tf_op jit(solution)/shard_map/pallas_call | solution.py:38
  11.6 2.7 %collective-permute-start.5 = (s16[16,1152]{1,0:T(8,128)(2,1)S(1)}, s16[16,1152]{1,0:T(8,128)(2,1)S(1)}, u32[]{:S(2)}, u32[]{:S(2)}) collective-permute-start(s16[16,1152]{1,0:T(8,128)(2,1)S(1)} %get-tuple-element.32.refs_0_.refs_1_), channel_id=1, source_target_pairs={{0,2},{1,3},{2,0},{3,1},{4,6},{5,7},{6,4},{7,5},{8,10},{9,11},{10,... | collective-permute-start | bytes 110600 | tf_op jit(solution)/shard_map/ppermute | solution.py:322
  14.2 0.0 collective-permute-start.8
  14.2 0.5 %collective-permute-start.9 = (bf16[32,1152]{1,0:T(8,128)(2,1)S(1)}, bf16[32,1152]{1,0:T(8,128)(2,1)S(1)}, u32[]{:S(2)}, u32[]{:S(2)}) collective-permute-start(bf16[32,1152]{1,0:T(8,128)(2,1)S(1)} %shard_map.96.refs_1_.refs_2_), channel_id=1, source_target_pairs={{0,4},{4,0},{1,5},{5,1},{2,6},{6,2},{3,7},{7,3},{8,12},{12,8},{9,1... | collective-permute-start | bytes 221192 | tf_op jit(solution)/shard_map/ppermute | solution.py:322
  14.7 0.0 collective-permute-done.4.refs_2_
  14.7 0.2 shard_map.98.refs_0_.refs_1_
  14.9 1.6 %collective-permute-start.6 = (s16[16,1152]{1,0:T(8,128)(2,1)S(1)}, s16[16,1152]{1,0:T(8,128)(2,1)S(1)}, u32[]{:S(2)}, u32[]{:S(2)}) collective-permute-start(s16[16,1152]{1,0:T(8,128)(2,1)S(1)} %shard_map.98.refs_0_.refs_1_), channel_id=1, source_target_pairs={{0,1},{1,0},{2,3},{3,2},{4,5},{5,4},{6,7},{7,6},{8,9},{9,8},{10,11... | collective-permute-start | bytes 110600 | tf_op jit(solution)/shard_map/ppermute | solution.py:322
  16.6 0.3 %collective-permute-done.5.refs_2_ = s16[16,1152]{1,0:T(8,128)(2,1)S(1)} collective-permute-done((s16[16,1152]{1,0:T(8,128)(2,1)S(1)}, s16[16,1152]{1,0:T(8,128)(2,1)S(1)}, u32[]{:S(2)}, u32[]{:S(2)}) %collective-permute-start.5) | collective-permute-done | bytes 36896 | tf_op jit(solution)/shard_map/ppermute | solution.py:322
  16.9 0.2 shard_map.99.refs_0_.refs_1_
  17.1 1.2 %collective-permute-start.10 = (s16[16,1152]{1,0:T(8,128)(2,1)S(1)}, s16[16,1152]{1,0:T(8,128)(2,1)S(1)}, u32[]{:S(2)}, u32[]{:S(2)}) collective-permute-start(s16[16,1152]{1,0:T(8,128)(2,1)S(1)} %shard_map.99.refs_0_.refs_1_), channel_id=1, source_target_pairs={{0,1},{1,0},{2,3},{3,2},{4,5},{5,4},{6,7},{7,6},{8,9},{9,8},{10,11... | collective-permute-start | bytes 110600 | tf_op jit(solution)/shard_map/ppermute | solution.py:322
  18.3 0.6 %collective-permute-done.6.refs_2_ = s16[16,1152]{1,0:T(8,128)(2,1)S(1)} collective-permute-done((s16[16,1152]{1,0:T(8,128)(2,1)S(1)}, s16[16,1152]{1,0:T(8,128)(2,1)S(1)}, u32[]{:S(2)}, u32[]{:S(2)}) %collective-permute-start.6) | collective-permute-done | bytes 36896 | tf_op jit(solution)/shard_map/ppermute | solution.py:322
  19.0 0.4 %shard_map.100 = (bf16[32,256]{1,0:T(8,128)(2,1)S(1)}, bf16[32,256]{1,0:T(8,128)(2,1)S(1)}, f32[8,1152]{1,0:T(8,128)S(1)}, f32[8,1152]{1,0:T(8,128)S(1)}) custom-call(s16[16,1152]{1,0:T(8,128)(2,1)S(1)} %shard_map.99.refs_0_.refs_1_, s16[16,1152]{1,0:T(8,128)(2,1)S(1)} %shard_map.98.refs_0_.refs_1_, s16[16,1152]{1,0:T(8,128)(2,1)S(1)} %collective-permute-done.6.refs_2_, ...), custom_call_target="tpu_custom_call" | custom-call | flops 16777216 | bytes 1114112 | tf_op jit(solution)/shard_map/pallas_call | solution.py:38
  19.4 0.0 collective-permute-start.7
  19.4 0.1 shard_map.101
  19.5 1.6 %collective-permute-done.10.refs_2_ = s16[16,1152]{1,0:T(8,128)(2,1)S(1)} collective-permute-done((s16[16,1152]{1,0:T(8,128)(2,1)S(1)}, s16[16,1152]{1,0:T(8,128)(2,1)S(1)}, u32[]{:S(2)}, u32[]{:S(2)}) %collective-permute-start.10) | collective-permute-done | bytes 36896 | tf_op jit(solution)/shard_map/ppermute | solution.py:322
  21.1 0.4 %shard_map.102 = (bf16[32,256]{1,0:T(8,128)(2,1)S(1)}, bf16[32,256]{1,0:T(8,128)(2,1)S(1)}, bf16[8,1152]{1,0:T(8,128)(2,1)S(1)}, bf16[8,1152]{1,0:T(8,128)(2,1)S(1)}) custom-call(bf16[256,32]{1,0:T(8,128)(2,1)S(1)} %get-tuple-element.38.refs_0_.refs_6_, s16[16,1152]{1,0:T(8,128)(2,1)S(1)} %shard_map.99.refs_0_.refs_1_, ...), custom_call_target="tpu_custom_call" | custom-call | flops 16777216 | bytes 1114112 | tf_op jit(solution)/shard_map/pallas_call | solution.py:38
  21.5 0.3 %collective-permute-start.13 = (bf16[8,1152]{1,0:T(8,128)(2,1)S(1)}, bf16[8,1152]{1,0:T(8,128)(2,1)S(1)}, u32[]{:S(2)}, u32[]{:S(2)}) collective-permute-start(bf16[8,1152]{1,0:T(8,128)(2,1)S(1)} %get-tuple-element.45), channel_id=1, source_target_pairs={{0,28},{4,24},{8,20},{12,16},{16,12},{20,8},{24,4},{28,0},{1,29},{... | collective-permute-start | bytes 55304 | tf_op jit(solution)/shard_map/ppermute | solution.py:322
  21.9 2.2 %collective-permute-start.14 = (bf16[8,1152]{1,0:T(8,128)(2,1)S(1)}, bf16[8,1152]{1,0:T(8,128)(2,1)S(1)}, u32[]{:S(2)}, u32[]{:S(2)}) collective-permute-start(bf16[8,1152]{1,0:T(8,128)(2,1)S(1)} %get-tuple-element.46), channel_id=1, source_target_pairs={{0,20},{4,16},{8,28},{12,24},{16,4},{20,0},{24,12},{28,8},{1,21},{... | collective-permute-start | bytes 55304 | tf_op jit(solution)/shard_map/ppermute | solution.py:322
  24.0 0.0 collective-permute-done.8.refs_3_
  24.1 0.0 collective-permute-start.11
  24.1 0.0 collective-permute-done.9.refs_4_
  24.1 0.5 %collective-permute-start.12 = (bf16[32,256]{1,0:T(8,128)(2,1)S(1)}, bf16[32,256]{1,0:T(8,128)(2,1)S(1)}, u32[]{:S(2)}, u32[]{:S(2)}) collective-permute-start(bf16[32,256]{1,0:T(8,128)(2,1)S(1)} %get-tuple-element.42), channel_id=1, source_target_pairs={{0,4},{4,0},{1,5},{5,1},{2,6},{6,2},{3,7},{7,3},{8,12},{12,8},{9,1... | collective-permute-start | bytes 49160 | tf_op jit(solution)/shard_map/ppermute | solution.py:322
  24.6 0.7 %collective-permute-done.11.refs_7_ = bf16[32,256]{1,0:T(8,128)(2,1)S(1)} collective-permute-done((bf16[32,256]{1,0:T(8,128)(2,1)S(1)}, bf16[32,256]{1,0:T(8,128)(2,1)S(1)}, u32[]{:S(2)}, u32[]{:S(2)}) %collective-permute-start.11) | collective-permute-done | bytes 16416 | tf_op jit(solution)/shard_map/ppermute | solution.py:322
  25.2 0.2 collective-permute-done.12.refs_8_
  25.4 0.0 collective-permute-done.7.refs_0_.refs_2_
  25.4 1.6 %shard_map.103 = (f32[1024,256]{1,0:T(8,128)}, f32[256,1024]{1,0:T(8,128)}, f32[8,128]{1,0:T(8,128)S(1)}) custom-call(f32[8,1152]{1,0:T(8,128)S(1)} %collective-permute-done.7.refs_0_.refs_2_, bf16[32,1152]{1,0:T(8,128)(2,1)S(1)} %shard_map.94.refs_0_.refs_1_, bf16[32,1152]{1,0:T(8,128)(2,1)S(1)} %shard_map.96.refs_1_.refs_2_, ...), custom_call_target="tpu_custom_call" | custom-call | tf_op jit(solution)/shard_map/pallas_call | solution.py:38
  27.0 0.0 collective-permute-done.13.refs_3_
  27.1 0.0 collective-permute-done.14.refs_4_
  27.1 1.1 %shard_map.104 = (bf16[256,1024]{1,0:T(8,128)(2,1)}, f32[2,256]{1,0:T(2,128)}) custom-call(f32[8,128]{1,0:T(8,128)S(1)} %get-tuple-element.43.refs_0_, f32[8,1152]{1,0:T(8,128)S(1)} %get-tuple-element.44.refs_1_, f32[8,1152]{1,0:T(8,128)S(1)} %collective-permute-done.7.refs_0_.refs_2_, bf16[8,1152]{1,0:T(8,128)(2,1)S(1)} %collective-permute-done.13.refs_3_, ...), custom_call_target="tpu_custom_call" | custom-call | flops 16777216 | bytes 524288 | tf_op jit(solution)/shard_map/pallas_call | solution.py:38
  (2 shorter events, 0.0 us)
Async XLA Ops:
  2.4 4.9 %collective-permute-start.1 = (bf16[512,1024]{1,0:T(8,128)(2,1)S(1)}, bf16[512,1024]{1,0:T(8,128)(2,1)S(1)}, u32[]{:S(2)}, u32[]{:S(2)}) collective-permute-start(bf16[512,1024]{1,0:T(8,128)(2,1)S(1)} %get-tuple-element.29.refs_1_.refs_2_.refs_4_), channel_id=1, source_target_pairs={{0,4},{4,0},{1,5},{5,1},{2,6},{6,2},{3,7},{7,3},{8,12},{12,8},{9,1... | collective-permute-start | bytes 3145736 | tf_op jit(solution)/shard_map/ppermute | solution.py:322
  2.9 4.4 %collective-permute-start = (bf16[16,1152]{1,0:T(8,128)(2,1)S(1)}, bf16[16,1152]{1,0:T(8,128)(2,1)S(1)}, u32[]{:S(2)}, u32[]{:S(2)}) collective-permute-start(bf16[16,1152]{1,0:T(8,128)(2,1)S(1)} %get-tuple-element.28.refs_0_), channel_id=1, source_target_pairs={{0,12},{4,8},{8,4},{12,0},{16,28},{20,24},{24,20},{28,16},{1,13},{... | collective-permute-start | bytes 110600 | tf_op jit(solution)/shard_map/ppermute | solution.py:322
  5.5 5.2 %collective-permute-start.3 = (bf16[16,1152]{1,0:T(8,128)(2,1)S(1)}, bf16[16,1152]{1,0:T(8,128)(2,1)S(1)}, u32[]{:S(2)}, u32[]{:S(2)}) collective-permute-start(bf16[16,1152]{1,0:T(8,128)(2,1)S(1)} %get-tuple-element.31), channel_id=1, source_target_pairs={{0,28},{4,24},{8,20},{12,16},{16,12},{20,8},{24,4},{28,0},{1,29},{... | collective-permute-start | bytes 110600 | tf_op jit(solution)/shard_map/ppermute | solution.py:322
  6.7 4.2 %collective-permute-start.2 = (bf16[16,1152]{1,0:T(8,128)(2,1)S(1)}, bf16[16,1152]{1,0:T(8,128)(2,1)S(1)}, u32[]{:S(2)}, u32[]{:S(2)}) collective-permute-start(bf16[16,1152]{1,0:T(8,128)(2,1)S(1)} %get-tuple-element.31), channel_id=1, source_target_pairs={{0,20},{4,16},{8,28},{12,24},{16,4},{20,0},{24,12},{28,8},{1,21},{... | collective-permute-start | bytes 110600 | tf_op jit(solution)/shard_map/ppermute | solution.py:322
  8.0 6.8 %collective-permute-start.4 = (s16[16,1152]{1,0:T(8,128)(2,1)S(1)}, s16[16,1152]{1,0:T(8,128)(2,1)S(1)}, u32[]{:S(2)}, u32[]{:S(2)}) collective-permute-start(s16[16,1152]{1,0:T(8,128)(2,1)S(1)} %get-tuple-element.30.refs_0_.refs_1_), channel_id=1, source_target_pairs={{0,2},{1,3},{2,0},{3,1},{4,6},{5,7},{6,4},{7,5},{8,10},{9,11},{10,... | collective-permute-start | bytes 110600 | tf_op jit(solution)/shard_map/ppermute | solution.py:322
  11.6 5.3 %collective-permute-start.5 = (s16[16,1152]{1,0:T(8,128)(2,1)S(1)}, s16[16,1152]{1,0:T(8,128)(2,1)S(1)}, u32[]{:S(2)}, u32[]{:S(2)}) collective-permute-start(s16[16,1152]{1,0:T(8,128)(2,1)S(1)} %get-tuple-element.32.refs_0_.refs_1_), channel_id=1, source_target_pairs={{0,2},{1,3},{2,0},{3,1},{4,6},{5,7},{6,4},{7,5},{8,10},{9,11},{10,... | collective-permute-start | bytes 110600 | tf_op jit(solution)/shard_map/ppermute | solution.py:322
  14.2 9.8 %collective-permute-start.8 = (bf16[32,1152]{1,0:T(8,128)(2,1)S(1)}, bf16[32,1152]{1,0:T(8,128)(2,1)S(1)}, u32[]{:S(2)}, u32[]{:S(2)}) collective-permute-start(bf16[32,1152]{1,0:T(8,128)(2,1)S(1)} %shard_map.94.refs_0_.refs_1_), channel_id=1, source_target_pairs={{0,4},{4,0},{1,5},{5,1},{2,6},{6,2},{3,7},{7,3},{8,12},{12,8},{9,1... | collective-permute-start | bytes 221192 | tf_op jit(solution)/shard_map/ppermute | solution.py:322
  14.2 9.8 %collective-permute-start.9 = (bf16[32,1152]{1,0:T(8,128)(2,1)S(1)}, bf16[32,1152]{1,0:T(8,128)(2,1)S(1)}, u32[]{:S(2)}, u32[]{:S(2)}) collective-permute-start(bf16[32,1152]{1,0:T(8,128)(2,1)S(1)} %shard_map.96.refs_1_.refs_2_), channel_id=1, source_target_pairs={{0,4},{4,0},{1,5},{5,1},{2,6},{6,2},{3,7},{7,3},{8,12},{12,8},{9,1... | collective-permute-start | bytes 221192 | tf_op jit(solution)/shard_map/ppermute | solution.py:322
  14.9 4.0 %collective-permute-start.6 = (s16[16,1152]{1,0:T(8,128)(2,1)S(1)}, s16[16,1152]{1,0:T(8,128)(2,1)S(1)}, u32[]{:S(2)}, u32[]{:S(2)}) collective-permute-start(s16[16,1152]{1,0:T(8,128)(2,1)S(1)} %shard_map.98.refs_0_.refs_1_), channel_id=1, source_target_pairs={{0,1},{1,0},{2,3},{3,2},{4,5},{5,4},{6,7},{7,6},{8,9},{9,8},{10,11... | collective-permute-start | bytes 110600 | tf_op jit(solution)/shard_map/ppermute | solution.py:322
  17.1 4.0 %collective-permute-start.10 = (s16[16,1152]{1,0:T(8,128)(2,1)S(1)}, s16[16,1152]{1,0:T(8,128)(2,1)S(1)}, u32[]{:S(2)}, u32[]{:S(2)}) collective-permute-start(s16[16,1152]{1,0:T(8,128)(2,1)S(1)} %shard_map.99.refs_0_.refs_1_), channel_id=1, source_target_pairs={{0,1},{1,0},{2,3},{3,2},{4,5},{5,4},{6,7},{7,6},{8,9},{9,8},{10,11... | collective-permute-start | bytes 110600 | tf_op jit(solution)/shard_map/ppermute | solution.py:322
  19.4 6.0 %collective-permute-start.7 = (f32[8,1152]{1,0:T(8,128)S(1)}, f32[8,1152]{1,0:T(8,128)S(1)}, u32[]{:S(2)}, u32[]{:S(2)}) collective-permute-start(f32[8,1152]{1,0:T(8,128)S(1)} %get-tuple-element.34), channel_id=1, source_target_pairs={{0,12},{4,8},{8,4},{12,0},{16,28},{20,24},{24,20},{28,16},{1,13},{... | collective-permute-start | bytes 110600 | tf_op jit(solution)/shard_map/ppermute | solution.py:322
  21.5 5.5 %collective-permute-start.13 = (bf16[8,1152]{1,0:T(8,128)(2,1)S(1)}, bf16[8,1152]{1,0:T(8,128)(2,1)S(1)}, u32[]{:S(2)}, u32[]{:S(2)}) collective-permute-start(bf16[8,1152]{1,0:T(8,128)(2,1)S(1)} %get-tuple-element.45), channel_id=1, source_target_pairs={{0,28},{4,24},{8,20},{12,16},{16,12},{20,8},{24,4},{28,0},{1,29},{... | collective-permute-start | bytes 55304 | tf_op jit(solution)/shard_map/ppermute | solution.py:322
  21.9 5.2 %collective-permute-start.14 = (bf16[8,1152]{1,0:T(8,128)(2,1)S(1)}, bf16[8,1152]{1,0:T(8,128)(2,1)S(1)}, u32[]{:S(2)}, u32[]{:S(2)}) collective-permute-start(bf16[8,1152]{1,0:T(8,128)(2,1)S(1)} %get-tuple-element.46), channel_id=1, source_target_pairs={{0,20},{4,16},{8,28},{12,24},{16,4},{20,0},{24,12},{28,8},{1,21},{... | collective-permute-start | bytes 55304 | tf_op jit(solution)/shard_map/ppermute | solution.py:322
  24.1 1.2 %collective-permute-start.11 = (bf16[32,256]{1,0:T(8,128)(2,1)S(1)}, bf16[32,256]{1,0:T(8,128)(2,1)S(1)}, u32[]{:S(2)}, u32[]{:S(2)}) collective-permute-start(bf16[32,256]{1,0:T(8,128)(2,1)S(1)} %get-tuple-element.41), channel_id=1, source_target_pairs={{0,4},{4,0},{1,5},{5,1},{2,6},{6,2},{3,7},{7,3},{8,12},{12,8},{9,1... | collective-permute-start | bytes 49160 | tf_op jit(solution)/shard_map/ppermute | solution.py:322
  24.1 1.3 %collective-permute-start.12 = (bf16[32,256]{1,0:T(8,128)(2,1)S(1)}, bf16[32,256]{1,0:T(8,128)(2,1)S(1)}, u32[]{:S(2)}, u32[]{:S(2)}) collective-permute-start(bf16[32,256]{1,0:T(8,128)(2,1)S(1)} %get-tuple-element.42), channel_id=1, source_target_pairs={{0,4},{4,0},{1,5},{5,1},{2,6},{6,2},{3,7},{7,3},{8,12},{12,8},{9,1... | collective-permute-start | bytes 49160 | tf_op jit(solution)/shard_map/ppermute | solution.py:322

commit v11 on v2

--- a/solution.py
+++ b/solution.py
@@ -11,6 +11,7 @@
 WINDOW = 2
 LANES = 128
 PIECES = 4
+LOADS = 2
 VMEM_LIMIT = 40 * 1024 * 1024
 
 BF16 = jnp.bfloat16
@@ -100,9 +101,9 @@
         pltpu.make_async_copy(routes_hbm, routes_ref, sems.at[0]),
         pltpu.make_async_copy(gates_hbm, gates_ref, sems.at[1]),
     ]
-    count = tok_rows // PIECES
+    count = tok_rows // LOADS
     for source, target in ((tokens_hbm, tokens_ref), (grads_hbm, grads_ref)):
-        for piece in range(PIECES):
+        for piece in range(LOADS):
             span = pl.ds(piece * count, count)
             copies.append(
                 pltpu.make_async_copy(source.at[span], target.at[span], sems.at[len(copies)])
@@ -144,10 +145,10 @@
         for k in range(2):
             masks = jnp.where(row_of == 2 * index + k, hit[k : k + 1], masks)
     place_ref[slots:] = masks.astype(BF16)
-    for copy in copies[2 : 2 + PIECES]:
+    for copy in copies[2 : 2 + LOADS]:
         copy.wait()
     rows_x = jnp.dot(place, tokens_ref[...], preferred_element_type=F32)
-    for copy in copies[2 + PIECES : 2 + 2 * PIECES]:
+    for copy in copies[2 + LOADS : 2 + 2 * LOADS]:
         copy.wait()
     rows_dy = jnp.dot(place, grads_ref[...], preferred_element_type=F32)
     for expert, out_ref in ((0, own_ref), (1, other_ref)):
@@ -156,7 +157,7 @@
         gate = jnp.sum(parts[expert] * weight[expert], axis=1, keepdims=True)
         gate = jnp.concatenate([gate, gate], axis=0)
         out_ref[:, feats:] = jnp.broadcast_to(gate, (2 * capacity, LANES)).astype(BF16)
-    for copy in copies[2 + 2 * PIECES :]:
+    for copy in copies[2 + 2 * LOADS :]:
         copy.wait()
 
 
@@ -367,7 +368,7 @@
             pltpu.VMEM((2, tok_rows), BF16),
             pltpu.VMEM((tok_rows, feats), BF16),
             pltpu.VMEM((tok_rows, feats), BF16),
-            pltpu.SemaphoreType.DMA((3 + 2 * PIECES + feats // hidden,)),
+            pltpu.SemaphoreType.DMA((3 + 2 * LOADS + feats // hidden,)),
         ],
     )(*inputs)
 

time: 28 us -> 27.8 us (level)
  no operation moved by 1% of the time
where the time goes in v11:
time: 27.8 us; the launch traced here: 27.7 us
  starting transfers between devices  15.4 us (55%)
  Pallas kernels  6.88 us (25%)
  waiting for transfers between devices  4.69 us (17%)
  between operations  0.7 us (3%)
    ppermute x14, starting transfers between devices, swap(): lax.ppermute(array, axes, [(index, index ^ bit) for index in range(size)])  15.4 us
    pallas_call x11, Pallas kernels, run(): pl.pallas_call(lambda *refs: kernel(*refs[len(after):]), out_shape=out_sh...  6.88 us
    ppermute x14, waiting for transfers between devices, swap(): lax.ppermute(array, axes, [(index, index ^ bit) for index in range(size)])  4.69 us
  transfers between devices with their start and end apart: 14, of which 6 were waited for; matrix products, arithmetic and copies ran while one was open for 0% of the time, Pallas kernels for 15%

profile of v11, /device:TPU:0, one launch (start us, length us, event | category | flops | bytes accessed | tf_op | source)
XLA Modules:
  0.0 27.7 jit_solution(11345951623815849101)
XLA Ops:
  0.6 1.6 %shard_map.93 = (bf16[16,1152]{1,0:T(8,128)(2,1)S(1)}, bf16[16,1152]{1,0:T(8,128)(2,1)S(1)}, bf16[32,256]{1,0:T(8,128)(2,1)S(1)}, bf16[256,32]{1,0:T(8,128)(2,1)S(1)}, bf16[512,1024]{1,0:T(8,128)(2,1)S(1)}) custom-call(s32[2,256]{1,0:T(2,128)} %bitcast.3, bf16[2,256]{1,0:T(2,128)(2,1)} %bitcast.4, bf16[256,1024]{1,0:T(8,128)(2,1)} %refs_2_.1, ...), custom_call_target="tpu_custom_call" | custom-call | flops 16777216 | bytes 2097152 | tf_op jit(solution)/shard_map/pallas_call | solution.py:39
  2.3 0.5 %collective-permute-start.1 = (bf16[512,1024]{1,0:T(8,128)(2,1)S(1)}, bf16[512,1024]{1,0:T(8,128)(2,1)S(1)}, u32[]{:S(2)}, u32[]{:S(2)}) collective-permute-start(bf16[512,1024]{1,0:T(8,128)(2,1)S(1)} %get-tuple-element.27.refs_1_.refs_2_.refs_4_), channel_id=1, source_target_pairs={{0,4},{4,0},{1,5},{5,1},{2,6},{6,2},{3,7},{7,3},{8,12},{12,8},{9,1... | collective-permute-start | bytes 3145736 | tf_op jit(solution)/shard_map/ppermute | solution.py:322
  2.8 2.6 %collective-permute-start = (bf16[16,1152]{1,0:T(8,128)(2,1)S(1)}, bf16[16,1152]{1,0:T(8,128)(2,1)S(1)}, u32[]{:S(2)}, u32[]{:S(2)}) collective-permute-start(bf16[16,1152]{1,0:T(8,128)(2,1)S(1)} %get-tuple-element.26.refs_0_), channel_id=1, source_target_pairs={{0,12},{4,8},{8,4},{12,0},{16,28},{20,24},{24,20},{28,16},{1,13},{... | collective-permute-start | bytes 110600 | tf_op jit(solution)/shard_map/ppermute | solution.py:322
  5.4 1.2 %collective-permute-start.3 = (bf16[16,1152]{1,0:T(8,128)(2,1)S(1)}, bf16[16,1152]{1,0:T(8,128)(2,1)S(1)}, u32[]{:S(2)}, u32[]{:S(2)}) collective-permute-start(bf16[16,1152]{1,0:T(8,128)(2,1)S(1)} %get-tuple-element.29), channel_id=1, source_target_pairs={{0,28},{4,24},{8,20},{12,16},{16,12},{20,8},{24,4},{28,0},{1,29},{... | collective-permute-start | bytes 110600 | tf_op jit(solution)/shard_map/ppermute | solution.py:322
  6.6 0.1 collective-permute-start.2
  6.6 0.5 %collective-permute-done.refs_1_ = bf16[16,1152]{1,0:T(8,128)(2,1)S(1)} collective-permute-done((bf16[16,1152]{1,0:T(8,128)(2,1)S(1)}, bf16[16,1152]{1,0:T(8,128)(2,1)S(1)}, u32[]{:S(2)}, u32[]{:S(2)}) %collective-permute-start) | collective-permute-done | bytes 36896 | tf_op jit(solution)/shard_map/ppermute | solution.py:322
  7.2 0.0 collective-permute-done.1.refs_2_.refs_3_.refs_5_
  7.2 0.7 %shard_map.95 = (s16[16,1152]{1,0:T(8,128)(2,1)S(1)}, f32[16,128]{1,0:T(8,128)S(1)}) custom-call(bf16[32,1152]{1,0:T(8,128)(2,1)S(1)} %shard_map.94.refs_0_.refs_1_, bf16[512,1024]{1,0:T(8,128)(2,1)S(1)} %get-tuple-element.27.refs_1_.refs_2_.refs_4_, bf16[512,1024]{1,0:T(8,128)(2,1)S(1)} %collective-permute-done.1.refs_2_.refs_3_.refs_5_), custom_call_target="tpu_custom_call" | custom-call | flops 67108864 | bytes 2162688 | tf_op jit(solution)/shard_map/pallas_call | solution.py:39
  7.8 2.7 %collective-permute-start.4 = (s16[16,1152]{1,0:T(8,128)(2,1)S(1)}, s16[16,1152]{1,0:T(8,128)(2,1)S(1)}, u32[]{:S(2)}, u32[]{:S(2)}) collective-permute-start(s16[16,1152]{1,0:T(8,128)(2,1)S(1)} %get-tuple-element.28.refs_0_.refs_1_), channel_id=1, source_target_pairs={{0,2},{1,3},{2,0},{3,1},{4,6},{5,7},{6,4},{7,5},{8,10},{9,11},{10,... | collective-permute-start | bytes 110600 | tf_op jit(solution)/shard_map/ppermute | solution.py:322
  10.6 0.0 collective-permute-done.3.refs_2_
  10.6 0.2 collective-permute-done.2.refs_1_
  10.8 0.7 %shard_map.97 = (s16[16,1152]{1,0:T(8,128)(2,1)S(1)}, f32[16,128]{1,0:T(8,128)S(1)}) custom-call(s16[16,1152]{1,0:T(8,128)(2,1)S(1)} %get-tuple-element.28.refs_0_.refs_1_, bf16[32,1152]{1,0:T(8,128)(2,1)S(1)} %shard_map.96.refs_1_.refs_2_, bf16[512,1024]{1,0:T(8,128)(2,1)S(1)} %get-tuple-element.27.refs_1_.refs_2_.refs_4_, ...), custom_call_target="tpu_custom_call" | custom-call | flops 67108864 | bytes 2162688 | tf_op jit(solution)/shard_map/pallas_call | solution.py:39
  11.4 2.7 %collective-permute-start.5 = (s16[16,1152]{1,0:T(8,128)(2,1)S(1)}, s16[16,1152]{1,0:T(8,128)(2,1)S(1)}, u32[]{:S(2)}, u32[]{:S(2)}) collective-permute-start(s16[16,1152]{1,0:T(8,128)(2,1)S(1)} %get-tuple-element.30.refs_0_.refs_1_), channel_id=1, source_target_pairs={{0,2},{1,3},{2,0},{3,1},{4,6},{5,7},{6,4},{7,5},{8,10},{9,11},{10,... | collective-permute-start | bytes 110600 | tf_op jit(solution)/shard_map/ppermute | solution.py:322
  14.1 0.0 collective-permute-start.8
  14.1 0.0 collective-permute-done.4.refs_2_
  14.1 0.2 shard_map.98.refs_0_.refs_1_
  14.3 1.6 %collective-permute-start.6 = (s16[16,1152]{1,0:T(8,128)(2,1)S(1)}, s16[16,1152]{1,0:T(8,128)(2,1)S(1)}, u32[]{:S(2)}, u32[]{:S(2)}) collective-permute-start(s16[16,1152]{1,0:T(8,128)(2,1)S(1)} %shard_map.98.refs_0_.refs_1_), channel_id=1, source_target_pairs={{0,1},{1,0},{2,3},{3,2},{4,5},{5,4},{6,7},{7,6},{8,9},{9,8},{10,11... | collective-permute-start | bytes 110600 | tf_op jit(solution)/shard_map/ppermute | solution.py:322
  15.9 0.2 collective-permute-start.9
  16.2 0.6 %collective-permute-done.5.refs_2_ = s16[16,1152]{1,0:T(8,128)(2,1)S(1)} collective-permute-done((s16[16,1152]{1,0:T(8,128)(2,1)S(1)}, s16[16,1152]{1,0:T(8,128)(2,1)S(1)}, u32[]{:S(2)}, u32[]{:S(2)}) %collective-permute-start.5) | collective-permute-done | bytes 36896 | tf_op jit(solution)/shard_map/ppermute | solution.py:322
  16.8 0.2 shard_map.99.refs_0_.refs_1_
  17.0 1.2 %collective-permute-start.10 = (s16[16,1152]{1,0:T(8,128)(2,1)S(1)}, s16[16,1152]{1,0:T(8,128)(2,1)S(1)}, u32[]{:S(2)}, u32[]{:S(2)}) collective-permute-start(s16[16,1152]{1,0:T(8,128)(2,1)S(1)} %shard_map.99.refs_0_.refs_1_), channel_id=1, source_target_pairs={{0,1},{1,0},{2,3},{3,2},{4,5},{5,4},{6,7},{7,6},{8,9},{9,8},{10,11... | collective-permute-start | bytes 110600 | tf_op jit(solution)/shard_map/ppermute | solution.py:322
  18.2 0.1 collective-permute-done.6.refs_2_
  18.3 0.4 %shard_map.100 = (bf16[32,256]{1,0:T(8,128)(2,1)S(1)}, bf16[32,256]{1,0:T(8,128)(2,1)S(1)}, f32[8,1152]{1,0:T(8,128)S(1)}, f32[8,1152]{1,0:T(8,128)S(1)}) custom-call(s16[16,1152]{1,0:T(8,128)(2,1)S(1)} %shard_map.99.refs_0_.refs_1_, s16[16,1152]{1,0:T(8,128)(2,1)S(1)} %shard_map.98.refs_0_.refs_1_, s16[16,1152]{1,0:T(8,128)(2,1)S(1)} %collective-permute-done.6.refs_2_, ...), custom_call_target="tpu_custom_call" | custom-call | flops 16777216 | bytes 1114112 | tf_op jit(solution)/shard_map/pallas_call | solution.py:39
  18.7 0.0 collective-permute-start.7
  18.7 2.2 %collective-permute-done.10.refs_2_ = s16[16,1152]{1,0:T(8,128)(2,1)S(1)} collective-permute-done((s16[16,1152]{1,0:T(8,128)(2,1)S(1)}, s16[16,1152]{1,0:T(8,128)(2,1)S(1)}, u32[]{:S(2)}, u32[]{:S(2)}) %collective-permute-start.10) | collective-permute-done | bytes 36896 | tf_op jit(solution)/shard_map/ppermute | solution.py:322
  21.0 0.4 %shard_map.101 = (bf16[32,256]{1,0:T(8,128)(2,1)S(1)}, bf16[64,256]{1,0:T(8,128)(2,1)S(1)}, bf16[8,1152]{1,0:T(8,128)(2,1)S(1)}, bf16[8,1152]{1,0:T(8,128)(2,1)S(1)}) custom-call(bf16[32,256]{1,0:T(8,128)(2,1)S(1)} %get-tuple-element.33.refs_0_.refs_5_, s16[16,1152]{1,0:T(8,128)(2,1)S(1)} %shard_map.99.refs_0_.refs_1_, ...), custom_call_target="tpu_custom_call" | custom-call | flops 16777216 | bytes 1114112 | tf_op jit(solution)/shard_map/pallas_call | solution.py:39
  21.4 0.0 collective-permute-start.11
  21.4 2.0 %collective-permute-start.12 = (bf16[8,1152]{1,0:T(8,128)(2,1)S(1)}, bf16[8,1152]{1,0:T(8,128)(2,1)S(1)}, u32[]{:S(2)}, u32[]{:S(2)}) collective-permute-start(bf16[8,1152]{1,0:T(8,128)(2,1)S(1)} %get-tuple-element.40), channel_id=1, source_target_pairs={{0,28},{4,24},{8,20},{12,16},{16,12},{20,8},{24,4},{28,0},{1,29},{... | collective-permute-start | bytes 55304 | tf_op jit(solution)/shard_map/ppermute | solution.py:322
  23.4 0.0 collective-permute-done.8.refs_3_
  23.4 0.5 %collective-permute-start.13 = (bf16[8,1152]{1,0:T(8,128)(2,1)S(1)}, bf16[8,1152]{1,0:T(8,128)(2,1)S(1)}, u32[]{:S(2)}, u32[]{:S(2)}) collective-permute-start(bf16[8,1152]{1,0:T(8,128)(2,1)S(1)} %get-tuple-element.41), channel_id=1, source_target_pairs={{0,20},{4,16},{8,28},{12,24},{16,4},{20,0},{24,12},{28,8},{1,21},{... | collective-permute-start | bytes 55304 | tf_op jit(solution)/shard_map/ppermute | solution.py:322
  23.9 0.0 collective-permute-done.9.refs_4_
  24.0 0.0 collective-permute-done.11.refs_7_
  24.0 0.0 collective-permute-done.7.refs_0_.refs_2_
  24.0 1.6 %shard_map.102 = (f32[1024,256]{1,0:T(8,128)}, f32[256,1024]{1,0:T(8,128)}, f32[8,128]{1,0:T(8,128)S(1)}) custom-call(f32[8,1152]{1,0:T(8,128)S(1)} %collective-permute-done.7.refs_0_.refs_2_, bf16[32,1152]{1,0:T(8,128)(2,1)S(1)} %shard_map.94.refs_0_.refs_1_, bf16[32,1152]{1,0:T(8,128)(2,1)S(1)} %shard_map.96.refs_1_.refs_2_, ...), custom_call_target="tpu_custom_call" | custom-call | flops 134217728 | bytes 2097152 | tf_op jit(solution)/shard_map/pallas_call | solution.py:39
  25.6 0.0 collective-permute-done.12.refs_3_
  25.6 1.0 %collective-permute-done.13.refs_4_ = bf16[8,1152]{1,0:T(8,128)(2,1)S(1)} collective-permute-done((bf16[8,1152]{1,0:T(8,128)(2,1)S(1)}, bf16[8,1152]{1,0:T(8,128)(2,1)S(1)}, u32[]{:S(2)}, u32[]{:S(2)}) %collective-permute-start.13) | collective-permute-done | bytes 18464 | tf_op jit(solution)/shard_map/ppermute | solution.py:322
  26.6 1.1 %shard_map.103 = (bf16[256,1024]{1,0:T(8,128)(2,1)}, f32[2,256]{1,0:T(2,128)}) custom-call(f32[8,128]{1,0:T(8,128)S(1)} %get-tuple-element.38.refs_0_, f32[8,1152]{1,0:T(8,128)S(1)} %get-tuple-element.39.refs_1_, f32[8,1152]{1,0:T(8,128)S(1)} %collective-permute-done.7.refs_0_.refs_2_, bf16[8,1152]{1,0:T(8,128)(2,1)S(1)} %collective-permute-done.12.refs_3_, ...), custom_call_target="tpu_custom_call" | custom-call | flops 16777216 | bytes 524288 | tf_op jit(solution)/shard_map/pallas_call | solution.py:39
  (2 shorter events, 0.0 us)
Async XLA Ops:
  2.3 4.9 %collective-permute-start.1 = (bf16[512,1024]{1,0:T(8,128)(2,1)S(1)}, bf16[512,1024]{1,0:T(8,128)(2,1)S(1)}, u32[]{:S(2)}, u32[]{:S(2)}) collective-permute-start(bf16[512,1024]{1,0:T(8,128)(2,1)S(1)} %get-tuple-element.27.refs_1_.refs_2_.refs_4_), channel_id=1, source_target_pairs={{0,4},{4,0},{1,5},{5,1},{2,6},{6,2},{3,7},{7,3},{8,12},{12,8},{9,1... | collective-permute-start | bytes 3145736 | tf_op jit(solution)/shard_map/ppermute | solution.py:322
  2.8 4.4 %collective-permute-start = (bf16[16,1152]{1,0:T(8,128)(2,1)S(1)}, bf16[16,1152]{1,0:T(8,128)(2,1)S(1)}, u32[]{:S(2)}, u32[]{:S(2)}) collective-permute-start(bf16[16,1152]{1,0:T(8,128)(2,1)S(1)} %get-tuple-element.26.refs_0_), channel_id=1, source_target_pairs={{0,12},{4,8},{8,4},{12,0},{16,28},{20,24},{24,20},{28,16},{1,13},{... | collective-permute-start | bytes 110600 | tf_op jit(solution)/shard_map/ppermute | solution.py:322
  5.4 5.2 %collective-permute-start.3 = (bf16[16,1152]{1,0:T(8,128)(2,1)S(1)}, bf16[16,1152]{1,0:T(8,128)(2,1)S(1)}, u32[]{:S(2)}, u32[]{:S(2)}) collective-permute-start(bf16[16,1152]{1,0:T(8,128)(2,1)S(1)} %get-tuple-element.29), channel_id=1, source_target_pairs={{0,28},{4,24},{8,20},{12,16},{16,12},{20,8},{24,4},{28,0},{1,29},{... | collective-permute-start | bytes 110600 | tf_op jit(solution)/shard_map/ppermute | solution.py:322
  6.6 4.2 %collective-permute-start.2 = (bf16[16,1152]{1,0:T(8,128)(2,1)S(1)}, bf16[16,1152]{1,0:T(8,128)(2,1)S(1)}, u32[]{:S(2)}, u32[]{:S(2)}) collective-permute-start(bf16[16,1152]{1,0:T(8,128)(2,1)S(1)} %get-tuple-element.29), channel_id=1, source_target_pairs={{0,20},{4,16},{8,28},{12,24},{16,4},{20,0},{24,12},{28,8},{1,21},{... | collective-permute-start | bytes 110600 | tf_op jit(solution)/shard_map/ppermute | solution.py:322
  7.8 6.3 %collective-permute-start.4 = (s16[16,1152]{1,0:T(8,128)(2,1)S(1)}, s16[16,1152]{1,0:T(8,128)(2,1)S(1)}, u32[]{:S(2)}, u32[]{:S(2)}) collective-permute-start(s16[16,1152]{1,0:T(8,128)(2,1)S(1)} %get-tuple-element.28.refs_0_.refs_1_), channel_id=1, source_target_pairs={{0,2},{1,3},{2,0},{3,1},{4,6},{5,7},{6,4},{7,5},{8,10},{9,11},{10,... | collective-permute-start | bytes 110600 | tf_op jit(solution)/shard_map/ppermute | solution.py:322
  11.4 5.3 %collective-permute-start.5 = (s16[16,1152]{1,0:T(8,128)(2,1)S(1)}, s16[16,1152]{1,0:T(8,128)(2,1)S(1)}, u32[]{:S(2)}, u32[]{:S(2)}) collective-permute-start(s16[16,1152]{1,0:T(8,128)(2,1)S(1)} %get-tuple-element.30.refs_0_.refs_1_), channel_id=1, source_target_pairs={{0,2},{1,3},{2,0},{3,1},{4,6},{5,7},{6,4},{7,5},{8,10},{9,11},{10,... | collective-permute-start | bytes 110600 | tf_op jit(solution)/shard_map/ppermute | solution.py:322
  14.1 9.3 %collective-permute-start.8 = (bf16[32,1152]{1,0:T(8,128)(2,1)S(1)}, bf16[32,1152]{1,0:T(8,128)(2,1)S(1)}, u32[]{:S(2)}, u32[]{:S(2)}) collective-permute-start(bf16[32,1152]{1,0:T(8,128)(2,1)S(1)} %shard_map.94.refs_0_.refs_1_), channel_id=1, source_target_pairs={{0,4},{4,0},{1,5},{5,1},{2,6},{6,2},{3,7},{7,3},{8,12},{12,8},{9,1... | collective-permute-start | bytes 221192 | tf_op jit(solution)/shard_map/ppermute | solution.py:322
  14.3 4.0 %collective-permute-start.6 = (s16[16,1152]{1,0:T(8,128)(2,1)S(1)}, s16[16,1152]{1,0:T(8,128)(2,1)S(1)}, u32[]{:S(2)}, u32[]{:S(2)}) collective-permute-start(s16[16,1152]{1,0:T(8,128)(2,1)S(1)} %shard_map.98.refs_0_.refs_1_), channel_id=1, source_target_pairs={{0,1},{1,0},{2,3},{3,2},{4,5},{5,4},{6,7},{7,6},{8,9},{9,8},{10,11... | collective-permute-start | bytes 110600 | tf_op jit(solution)/shard_map/ppermute | solution.py:322
  15.9 8.0 %collective-permute-start.9 = (bf16[32,1152]{1,0:T(8,128)(2,1)S(1)}, bf16[32,1152]{1,0:T(8,128)(2,1)S(1)}, u32[]{:S(2)}, u32[]{:S(2)}) collective-permute-start(bf16[32,1152]{1,0:T(8,128)(2,1)S(1)} %shard_map.96.refs_1_.refs_2_), channel_id=1, source_target_pairs={{0,4},{4,0},{1,5},{5,1},{2,6},{6,2},{3,7},{7,3},{8,12},{12,8},{9,1... | collective-permute-start | bytes 221192 | tf_op jit(solution)/shard_map/ppermute | solution.py:322
  17.0 4.0 %collective-permute-start.10 = (s16[16,1152]{1,0:T(8,128)(2,1)S(1)}, s16[16,1152]{1,0:T(8,128)(2,1)S(1)}, u32[]{:S(2)}, u32[]{:S(2)}) collective-permute-start(s16[16,1152]{1,0:T(8,128)(2,1)S(1)} %shard_map.99.refs_0_.refs_1_), channel_id=1, source_target_pairs={{0,1},{1,0},{2,3},{3,2},{4,5},{5,4},{6,7},{7,6},{8,9},{9,8},{10,11... | collective-permute-start | bytes 110600 | tf_op jit(solution)/shard_map/ppermute | solution.py:322
  18.7 5.2 %collective-permute-start.7 = (f32[8,1152]{1,0:T(8,128)S(1)}, f32[8,1152]{1,0:T(8,128)S(1)}, u32[]{:S(2)}, u32[]{:S(2)}) collective-permute-start(f32[8,1152]{1,0:T(8,128)S(1)} %get-tuple-element.32), channel_id=1, source_target_pairs={{0,12},{4,8},{8,4},{12,0},{16,28},{20,24},{24,20},{28,16},{1,13},{... | collective-permute-start | bytes 110600 | tf_op jit(solution)/shard_map/ppermute | solution.py:322
  21.4 2.6 %collective-permute-start.11 = (bf16[64,256]{1,0:T(8,128)(2,1)S(1)}, bf16[64,256]{1,0:T(8,128)(2,1)S(1)}, u32[]{:S(2)}, u32[]{:S(2)}) collective-permute-start(bf16[64,256]{1,0:T(8,128)(2,1)S(1)} %get-tuple-element.37), channel_id=1, source_target_pairs={{0,4},{4,0},{1,5},{5,1},{2,6},{6,2},{3,7},{7,3},{8,12},{12,8},{9,1... | collective-permute-start | bytes 98312 | tf_op jit(solution)/shard_map/ppermute | solution.py:322
  21.4 4.2 %collective-permute-start.12 = (bf16[8,1152]{1,0:T(8,128)(2,1)S(1)}, bf16[8,1152]{1,0:T(8,128)(2,1)S(1)}, u32[]{:S(2)}, u32[]{:S(2)}) collective-permute-start(bf16[8,1152]{1,0:T(8,128)(2,1)S(1)} %get-tuple-element.40), channel_id=1, source_target_pairs={{0,28},{4,24},{8,20},{12,16},{16,12},{20,8},{24,4},{28,0},{1,29},{... | collective-permute-start | bytes 55304 | tf_op jit(solution)/shard_map/ppermute | solution.py:322
  23.4 3.2 %collective-permute-start.13 = (bf16[8,1152]{1,0:T(8,128)(2,1)S(1)}, bf16[8,1152]{1,0:T(8,128)(2,1)S(1)}, u32[]{:S(2)}, u32[]{:S(2)}) collective-permute-start(bf16[8,1152]{1,0:T(8,128)(2,1)S(1)} %get-tuple-element.41), channel_id=1, source_target_pairs={{0,20},{4,16},{8,28},{12,24},{16,4},{20,0},{24,12},{28,8},{1,21},{... | collective-permute-start | bytes 55304 | tf_op jit(solution)/shard_map/ppermute | solution.py:322

commit v12 on v11

--- a/solution.py
+++ b/solution.py
@@ -11,7 +11,7 @@
 WINDOW = 2
 LANES = 128
 PIECES = 4
-LOADS = 2
+LOADS = 1
 VMEM_LIMIT = 40 * 1024 * 1024
 
 BF16 = jnp.bfloat16

time: 27.8 us -> 27.8 us (level)
  no operation moved by 1% of the time
where the time goes in v12:
time: 27.8 us; the launch traced here: 27.7 us
  starting transfers between devices  15.4 us (55%)
  Pallas kernels  6.87 us (25%)
  waiting for transfers between devices  4.69 us (17%)
  between operations  0.7 us (3%)
    ppermute x14, starting transfers between devices, swap(): lax.ppermute(array, axes, [(index, index ^ bit) for index in range(size)])  15.4 us
    pallas_call x11, Pallas kernels, run(): pl.pallas_call(lambda *refs: kernel(*refs[len(after):]), out_shape=out_sh...  6.87 us
    ppermute x14, waiting for transfers between devices, swap(): lax.ppermute(array, axes, [(index, index ^ bit) for index in range(size)])  4.69 us
  transfers between devices with their start and end apart: 14, of which 6 were waited for; matrix products, arithmetic and copies ran while one was open for 0% of the time, Pallas kernels for 15%

profile of v12, /device:TPU:0, one launch (start us, length us, event | category | flops | bytes accessed | tf_op | source)
XLA Modules:
  0.0 27.7 jit_solution(1062155664049710617)
XLA Ops:
  0.6 1.6 %shard_map.93 = (bf16[16,1152]{1,0:T(8,128)(2,1)S(1)}, bf16[16,1152]{1,0:T(8,128)(2,1)S(1)}, bf16[32,256]{1,0:T(8,128)(2,1)S(1)}, bf16[256,32]{1,0:T(8,128)(2,1)S(1)}, bf16[512,1024]{1,0:T(8,128)(2,1)S(1)}) custom-call(s32[2,256]{1,0:T(2,128)} %bitcast.3, bf16[2,256]{1,0:T(2,128)(2,1)} %bitcast.4, bf16[256,1024]{1,0:T(8,128)(2,1)} %refs_2_.1, ...), custom_call_target="tpu_custom_call" | custom-call | flops 16777216 | bytes 2097152 | tf_op jit(solution)/shard_map/pallas_call | solution.py:39
  2.2 0.5 %collective-permute-start.1 = (bf16[512,1024]{1,0:T(8,128)(2,1)S(1)}, bf16[512,1024]{1,0:T(8,128)(2,1)S(1)}, u32[]{:S(2)}, u32[]{:S(2)}) collective-permute-start(bf16[512,1024]{1,0:T(8,128)(2,1)S(1)} %get-tuple-element.27.refs_1_.refs_2_.refs_4_), channel_id=1, source_target_pairs={{0,4},{4,0},{1,5},{5,1},{2,6},{6,2},{3,7},{7,3},{8,12},{12,8},{9,1... | collective-permute-start | bytes 3145736 | tf_op jit(solution)/shard_map/ppermute | solution.py:322
  2.8 2.6 %collective-permute-start = (bf16[16,1152]{1,0:T(8,128)(2,1)S(1)}, bf16[16,1152]{1,0:T(8,128)(2,1)S(1)}, u32[]{:S(2)}, u32[]{:S(2)}) collective-permute-start(bf16[16,1152]{1,0:T(8,128)(2,1)S(1)} %get-tuple-element.26.refs_0_), channel_id=1, source_target_pairs={{0,12},{4,8},{8,4},{12,0},{16,28},{20,24},{24,20},{28,16},{1,13},{... | collective-permute-start | bytes 110600 | tf_op jit(solution)/shard_map/ppermute | solution.py:322
  5.4 1.2 %collective-permute-start.3 = (bf16[16,1152]{1,0:T(8,128)(2,1)S(1)}, bf16[16,1152]{1,0:T(8,128)(2,1)S(1)}, u32[]{:S(2)}, u32[]{:S(2)}) collective-permute-start(bf16[16,1152]{1,0:T(8,128)(2,1)S(1)} %get-tuple-element.29), channel_id=1, source_target_pairs={{0,28},{4,24},{8,20},{12,16},{16,12},{20,8},{24,4},{28,0},{1,29},{... | collective-permute-start | bytes 110600 | tf_op jit(solution)/shard_map/ppermute | solution.py:322
  6.5 0.1 collective-permute-start.2
  6.6 0.5 %collective-permute-done.refs_1_ = bf16[16,1152]{1,0:T(8,128)(2,1)S(1)} collective-permute-done((bf16[16,1152]{1,0:T(8,128)(2,1)S(1)}, bf16[16,1152]{1,0:T(8,128)(2,1)S(1)}, u32[]{:S(2)}, u32[]{:S(2)}) %collective-permute-start) | collective-permute-done | bytes 36896 | tf_op jit(solution)/shard_map/ppermute | solution.py:322
  7.1 0.0 collective-permute-done.1.refs_2_.refs_3_.refs_5_
  7.2 0.7 %shard_map.95 = (s16[16,1152]{1,0:T(8,128)(2,1)S(1)}, f32[16,128]{1,0:T(8,128)S(1)}) custom-call(bf16[32,1152]{1,0:T(8,128)(2,1)S(1)} %shard_map.94.refs_0_.refs_1_, bf16[512,1024]{1,0:T(8,128)(2,1)S(1)} %get-tuple-element.27.refs_1_.refs_2_.refs_4_, bf16[512,1024]{1,0:T(8,128)(2,1)S(1)} %collective-permute-done.1.refs_2_.refs_3_.refs_5_), custom_call_target="tpu_custom_call" | custom-call | flops 67108864 | bytes 2162688 | tf_op jit(solution)/shard_map/pallas_call | solution.py:39
  7.8 2.7 %collective-permute-start.4 = (s16[16,1152]{1,0:T(8,128)(2,1)S(1)}, s16[16,1152]{1,0:T(8,128)(2,1)S(1)}, u32[]{:S(2)}, u32[]{:S(2)}) collective-permute-start(s16[16,1152]{1,0:T(8,128)(2,1)S(1)} %get-tuple-element.28.refs_0_.refs_1_), channel_id=1, source_target_pairs={{0,2},{1,3},{2,0},{3,1},{4,6},{5,7},{6,4},{7,5},{8,10},{9,11},{10,... | collective-permute-start | bytes 110600 | tf_op jit(solution)/shard_map/ppermute | solution.py:322
  10.6 0.0 collective-permute-done.3.refs_2_
  10.6 0.2 collective-permute-done.2.refs_1_
  10.8 0.7 %shard_map.97 = (s16[16,1152]{1,0:T(8,128)(2,1)S(1)}, f32[16,128]{1,0:T(8,128)S(1)}) custom-call(s16[16,1152]{1,0:T(8,128)(2,1)S(1)} %get-tuple-element.28.refs_0_.refs_1_, bf16[32,1152]{1,0:T(8,128)(2,1)S(1)} %shard_map.96.refs_1_.refs_2_, bf16[512,1024]{1,0:T(8,128)(2,1)S(1)} %get-tuple-element.27.refs_1_.refs_2_.refs_4_, ...), custom_call_target="tpu_custom_call" | custom-call | flops 67108864 | bytes 2162688 | tf_op jit(solution)/shard_map/pallas_call | solution.py:39
  11.4 2.7 %collective-permute-start.5 = (s16[16,1152]{1,0:T(8,128)(2,1)S(1)}, s16[16,1152]{1,0:T(8,128)(2,1)S(1)}, u32[]{:S(2)}, u32[]{:S(2)}) collective-permute-start(s16[16,1152]{1,0:T(8,128)(2,1)S(1)} %get-tuple-element.30.refs_0_.refs_1_), channel_id=1, source_target_pairs={{0,2},{1,3},{2,0},{3,1},{4,6},{5,7},{6,4},{7,5},{8,10},{9,11},{10,... | collective-permute-start | bytes 110600 | tf_op jit(solution)/shard_map/ppermute | solution.py:322
  14.1 0.0 collective-permute-start.8
  14.1 0.0 collective-permute-done.4.refs_2_
  14.1 0.2 shard_map.98.refs_0_.refs_1_
  14.3 1.6 %collective-permute-start.6 = (s16[16,1152]{1,0:T(8,128)(2,1)S(1)}, s16[16,1152]{1,0:T(8,128)(2,1)S(1)}, u32[]{:S(2)}, u32[]{:S(2)}) collective-permute-start(s16[16,1152]{1,0:T(8,128)(2,1)S(1)} %shard_map.98.refs_0_.refs_1_), channel_id=1, source_target_pairs={{0,1},{1,0},{2,3},{3,2},{4,5},{5,4},{6,7},{7,6},{8,9},{9,8},{10,11... | collective-permute-start | bytes 110600 | tf_op jit(solution)/shard_map/ppermute | solution.py:322
  15.9 0.2 collective-permute-start.9
  16.2 0.6 %collective-permute-done.5.refs_2_ = s16[16,1152]{1,0:T(8,128)(2,1)S(1)} collective-permute-done((s16[16,1152]{1,0:T(8,128)(2,1)S(1)}, s16[16,1152]{1,0:T(8,128)(2,1)S(1)}, u32[]{:S(2)}, u32[]{:S(2)}) %collective-permute-start.5) | collective-permute-done | bytes 36896 | tf_op jit(solution)/shard_map/ppermute | solution.py:322
  16.8 0.2 shard_map.99.refs_0_.refs_1_
  16.9 1.2 %collective-permute-start.10 = (s16[16,1152]{1,0:T(8,128)(2,1)S(1)}, s16[16,1152]{1,0:T(8,128)(2,1)S(1)}, u32[]{:S(2)}, u32[]{:S(2)}) collective-permute-start(s16[16,1152]{1,0:T(8,128)(2,1)S(1)} %shard_map.99.refs_0_.refs_1_), channel_id=1, source_target_pairs={{0,1},{1,0},{2,3},{3,2},{4,5},{5,4},{6,7},{7,6},{8,9},{9,8},{10,11... | collective-permute-start | bytes 110600 | tf_op jit(solution)/shard_map/ppermute | solution.py:322
  18.2 0.1 collective-permute-done.6.refs_2_
  18.3 0.4 %shard_map.100 = (bf16[32,256]{1,0:T(8,128)(2,1)S(1)}, bf16[32,256]{1,0:T(8,128)(2,1)S(1)}, f32[8,1152]{1,0:T(8,128)S(1)}, f32[8,1152]{1,0:T(8,128)S(1)}) custom-call(s16[16,1152]{1,0:T(8,128)(2,1)S(1)} %shard_map.99.refs_0_.refs_1_, s16[16,1152]{1,0:T(8,128)(2,1)S(1)} %shard_map.98.refs_0_.refs_1_, s16[16,1152]{1,0:T(8,128)(2,1)S(1)} %collective-permute-done.6.refs_2_, ...), custom_call_target="tpu_custom_call" | custom-call | flops 16777216 | bytes 1114112 | tf_op jit(solution)/shard_map/pallas_call | solution.py:39
  18.7 0.0 collective-permute-start.7
  18.7 2.2 %collective-permute-done.10.refs_2_ = s16[16,1152]{1,0:T(8,128)(2,1)S(1)} collective-permute-done((s16[16,1152]{1,0:T(8,128)(2,1)S(1)}, s16[16,1152]{1,0:T(8,128)(2,1)S(1)}, u32[]{:S(2)}, u32[]{:S(2)}) %collective-permute-start.10) | collective-permute-done | bytes 36896 | tf_op jit(solution)/shard_map/ppermute | solution.py:322
  21.0 0.4 %shard_map.101 = (bf16[32,256]{1,0:T(8,128)(2,1)S(1)}, bf16[64,256]{1,0:T(8,128)(2,1)S(1)}, bf16[8,1152]{1,0:T(8,128)(2,1)S(1)}, bf16[8,1152]{1,0:T(8,128)(2,1)S(1)}) custom-call(bf16[32,256]{1,0:T(8,128)(2,1)S(1)} %get-tuple-element.33.refs_0_.refs_5_, s16[16,1152]{1,0:T(8,128)(2,1)S(1)} %shard_map.99.refs_0_.refs_1_, ...), custom_call_target="tpu_custom_call" | custom-call | flops 16777216 | bytes 1114112 | tf_op jit(solution)/shard_map/pallas_call | solution.py:39
  21.4 0.0 collective-permute-start.11
  21.4 2.0 %collective-permute-start.12 = (bf16[8,1152]{1,0:T(8,128)(2,1)S(1)}, bf16[8,1152]{1,0:T(8,128)(2,1)S(1)}, u32[]{:S(2)}, u32[]{:S(2)}) collective-permute-start(bf16[8,1152]{1,0:T(8,128)(2,1)S(1)} %get-tuple-element.40), channel_id=1, source_target_pairs={{0,28},{4,24},{8,20},{12,16},{16,12},{20,8},{24,4},{28,0},{1,29},{... | collective-permute-start | bytes 55304 | tf_op jit(solution)/shard_map/ppermute | solution.py:322
  23.4 0.0 collective-permute-done.8.refs_3_
  23.4 0.5 %collective-permute-start.13 = (bf16[8,1152]{1,0:T(8,128)(2,1)S(1)}, bf16[8,1152]{1,0:T(8,128)(2,1)S(1)}, u32[]{:S(2)}, u32[]{:S(2)}) collective-permute-start(bf16[8,1152]{1,0:T(8,128)(2,1)S(1)} %get-tuple-element.41), channel_id=1, source_target_pairs={{0,20},{4,16},{8,28},{12,24},{16,4},{20,0},{24,12},{28,8},{1,21},{... | collective-permute-start | bytes 55304 | tf_op jit(solution)/shard_map/ppermute | solution.py:322
  23.9 0.0 collective-permute-done.9.refs_4_
  23.9 0.0 collective-permute-done.11.refs_7_
  23.9 0.0 collective-permute-done.7.refs_0_.refs_2_
  23.9 1.6 %shard_map.102 = (f32[1024,256]{1,0:T(8,128)}, f32[256,1024]{1,0:T(8,128)}, f32[8,128]{1,0:T(8,128)S(1)}) custom-call(f32[8,1152]{1,0:T(8,128)S(1)} %collective-permute-done.7.refs_0_.refs_2_, bf16[32,1152]{1,0:T(8,128)(2,1)S(1)} %shard_map.94.refs_0_.refs_1_, bf16[32,1152]{1,0:T(8,128)(2,1)S(1)} %shard_map.96.refs_1_.refs_2_, ...), custom_call_target="tpu_custom_call" | custom-call | flops 134217728 | bytes 2097152 | tf_op jit(solution)/shard_map/pallas_call | solution.py:39
  25.6 0.0 collective-permute-done.12.refs_3_
  25.6 1.0 %collective-permute-done.13.refs_4_ = bf16[8,1152]{1,0:T(8,128)(2,1)S(1)} collective-permute-done((bf16[8,1152]{1,0:T(8,128)(2,1)S(1)}, bf16[8,1152]{1,0:T(8,128)(2,1)S(1)}, u32[]{:S(2)}, u32[]{:S(2)}) %collective-permute-start.13) | collective-permute-done | bytes 18464 | tf_op jit(solution)/shard_map/ppermute | solution.py:322
  26.6 1.1 %shard_map.103 = (bf16[256,1024]{1,0:T(8,128)(2,1)}, f32[2,256]{1,0:T(2,128)}) custom-call(f32[8,128]{1,0:T(8,128)S(1)} %get-tuple-element.38.refs_0_, f32[8,1152]{1,0:T(8,128)S(1)} %get-tuple-element.39.refs_1_, f32[8,1152]{1,0:T(8,128)S(1)} %collective-permute-done.7.refs_0_.refs_2_, bf16[8,1152]{1,0:T(8,128)(2,1)S(1)} %collective-permute-done.12.refs_3_, ...), custom_call_target="tpu_custom_call" | custom-call | flops 16777216 | bytes 524288 | tf_op jit(solution)/shard_map/pallas_call | solution.py:39
  (2 shorter events, 0.0 us)
Async XLA Ops:
  2.2 4.9 %collective-permute-start.1 = (bf16[512,1024]{1,0:T(8,128)(2,1)S(1)}, bf16[512,1024]{1,0:T(8,128)(2,1)S(1)}, u32[]{:S(2)}, u32[]{:S(2)}) collective-permute-start(bf16[512,1024]{1,0:T(8,128)(2,1)S(1)} %get-tuple-element.27.refs_1_.refs_2_.refs_4_), channel_id=1, source_target_pairs={{0,4},{4,0},{1,5},{5,1},{2,6},{6,2},{3,7},{7,3},{8,12},{12,8},{9,1... | collective-permute-start | bytes 3145736 | tf_op jit(solution)/shard_map/ppermute | solution.py:322
  2.8 4.4 %collective-permute-start = (bf16[16,1152]{1,0:T(8,128)(2,1)S(1)}, bf16[16,1152]{1,0:T(8,128)(2,1)S(1)}, u32[]{:S(2)}, u32[]{:S(2)}) collective-permute-start(bf16[16,1152]{1,0:T(8,128)(2,1)S(1)} %get-tuple-element.26.refs_0_), channel_id=1, source_target_pairs={{0,12},{4,8},{8,4},{12,0},{16,28},{20,24},{24,20},{28,16},{1,13},{... | collective-permute-start | bytes 110600 | tf_op jit(solution)/shard_map/ppermute | solution.py:322
  5.4 5.2 %collective-permute-start.3 = (bf16[16,1152]{1,0:T(8,128)(2,1)S(1)}, bf16[16,1152]{1,0:T(8,128)(2,1)S(1)}, u32[]{:S(2)}, u32[]{:S(2)}) collective-permute-start(bf16[16,1152]{1,0:T(8,128)(2,1)S(1)} %get-tuple-element.29), channel_id=1, source_target_pairs={{0,28},{4,24},{8,20},{12,16},{16,12},{20,8},{24,4},{28,0},{1,29},{... | collective-permute-start | bytes 110600 | tf_op jit(solution)/shard_map/ppermute | solution.py:322
  6.5 4.2 %collective-permute-start.2 = (bf16[16,1152]{1,0:T(8,128)(2,1)S(1)}, bf16[16,1152]{1,0:T(8,128)(2,1)S(1)}, u32[]{:S(2)}, u32[]{:S(2)}) collective-permute-start(bf16[16,1152]{1,0:T(8,128)(2,1)S(1)} %get-tuple-element.29), channel_id=1, source_target_pairs={{0,20},{4,16},{8,28},{12,24},{16,4},{20,0},{24,12},{28,8},{1,21},{... | collective-permute-start | bytes 110600 | tf_op jit(solution)/shard_map/ppermute | solution.py:322
  7.8 6.3 %collective-permute-start.4 = (s16[16,1152]{1,0:T(8,128)(2,1)S(1)}, s16[16,1152]{1,0:T(8,128)(2,1)S(1)}, u32[]{:S(2)}, u32[]{:S(2)}) collective-permute-start(s16[16,1152]{1,0:T(8,128)(2,1)S(1)} %get-tuple-element.28.refs_0_.refs_1_), channel_id=1, source_target_pairs={{0,2},{1,3},{2,0},{3,1},{4,6},{5,7},{6,4},{7,5},{8,10},{9,11},{10,... | collective-permute-start | bytes 110600 | tf_op jit(solution)/shard_map/ppermute | solution.py:322
  11.4 5.3 %collective-permute-start.5 = (s16[16,1152]{1,0:T(8,128)(2,1)S(1)}, s16[16,1152]{1,0:T(8,128)(2,1)S(1)}, u32[]{:S(2)}, u32[]{:S(2)}) collective-permute-start(s16[16,1152]{1,0:T(8,128)(2,1)S(1)} %get-tuple-element.30.refs_0_.refs_1_), channel_id=1, source_target_pairs={{0,2},{1,3},{2,0},{3,1},{4,6},{5,7},{6,4},{7,5},{8,10},{9,11},{10,... | collective-permute-start | bytes 110600 | tf_op jit(solution)/shard_map/ppermute | solution.py:322
  14.1 9.3 %collective-permute-start.8 = (bf16[32,1152]{1,0:T(8,128)(2,1)S(1)}, bf16[32,1152]{1,0:T(8,128)(2,1)S(1)}, u32[]{:S(2)}, u32[]{:S(2)}) collective-permute-start(bf16[32,1152]{1,0:T(8,128)(2,1)S(1)} %shard_map.94.refs_0_.refs_1_), channel_id=1, source_target_pairs={{0,4},{4,0},{1,5},{5,1},{2,6},{6,2},{3,7},{7,3},{8,12},{12,8},{9,1... | collective-permute-start | bytes 221192 | tf_op jit(solution)/shard_map/ppermute | solution.py:322
  14.3 4.0 %collective-permute-start.6 = (s16[16,1152]{1,0:T(8,128)(2,1)S(1)}, s16[16,1152]{1,0:T(8,128)(2,1)S(1)}, u32[]{:S(2)}, u32[]{:S(2)}) collective-permute-start(s16[16,1152]{1,0:T(8,128)(2,1)S(1)} %shard_map.98.refs_0_.refs_1_), channel_id=1, source_target_pairs={{0,1},{1,0},{2,3},{3,2},{4,5},{5,4},{6,7},{7,6},{8,9},{9,8},{10,11... | collective-permute-start | bytes 110600 | tf_op jit(solution)/shard_map/ppermute | solution.py:322
  15.9 8.0 %collective-permute-start.9 = (bf16[32,1152]{1,0:T(8,128)(2,1)S(1)}, bf16[32,1152]{1,0:T(8,128)(2,1)S(1)}, u32[]{:S(2)}, u32[]{:S(2)}) collective-permute-start(bf16[32,1152]{1,0:T(8,128)(2,1)S(1)} %shard_map.96.refs_1_.refs_2_), channel_id=1, source_target_pairs={{0,4},{4,0},{1,5},{5,1},{2,6},{6,2},{3,7},{7,3},{8,12},{12,8},{9,1... | collective-permute-start | bytes 221192 | tf_op jit(solution)/shard_map/ppermute | solution.py:322
  16.9 4.0 %collective-permute-start.10 = (s16[16,1152]{1,0:T(8,128)(2,1)S(1)}, s16[16,1152]{1,0:T(8,128)(2,1)S(1)}, u32[]{:S(2)}, u32[]{:S(2)}) collective-permute-start(s16[16,1152]{1,0:T(8,128)(2,1)S(1)} %shard_map.99.refs_0_.refs_1_), channel_id=1, source_target_pairs={{0,1},{1,0},{2,3},{3,2},{4,5},{5,4},{6,7},{7,6},{8,9},{9,8},{10,11... | collective-permute-start | bytes 110600 | tf_op jit(solution)/shard_map/ppermute | solution.py:322
  18.7 5.2 %collective-permute-start.7 = (f32[8,1152]{1,0:T(8,128)S(1)}, f32[8,1152]{1,0:T(8,128)S(1)}, u32[]{:S(2)}, u32[]{:S(2)}) collective-permute-start(f32[8,1152]{1,0:T(8,128)S(1)} %get-tuple-element.32), channel_id=1, source_target_pairs={{0,12},{4,8},{8,4},{12,0},{16,28},{20,24},{24,20},{28,16},{1,13},{... | collective-permute-start | bytes 110600 | tf_op jit(solution)/shard_map/ppermute | solution.py:322
  21.4 2.6 %collective-permute-start.11 = (bf16[64,256]{1,0:T(8,128)(2,1)S(1)}, bf16[64,256]{1,0:T(8,128)(2,1)S(1)}, u32[]{:S(2)}, u32[]{:S(2)}) collective-permute-start(bf16[64,256]{1,0:T(8,128)(2,1)S(1)} %get-tuple-element.37), channel_id=1, source_target_pairs={{0,4},{4,0},{1,5},{5,1},{2,6},{6,2},{3,7},{7,3},{8,12},{12,8},{9,1... | collective-permute-start | bytes 98312 | tf_op jit(solution)/shard_map/ppermute | solution.py:322
  21.4 4.2 %collective-permute-start.12 = (bf16[8,1152]{1,0:T(8,128)(2,1)S(1)}, bf16[8,1152]{1,0:T(8,128)(2,1)S(1)}, u32[]{:S(2)}, u32[]{:S(2)}) collective-permute-start(bf16[8,1152]{1,0:T(8,128)(2,1)S(1)} %get-tuple-element.40), channel_id=1, source_target_pairs={{0,28},{4,24},{8,20},{12,16},{16,12},{20,8},{24,4},{28,0},{1,29},{... | collective-permute-start | bytes 55304 | tf_op jit(solution)/shard_map/ppermute | solution.py:322
  23.4 3.2 %collective-permute-start.13 = (bf16[8,1152]{1,0:T(8,128)(2,1)S(1)}, bf16[8,1152]{1,0:T(8,128)(2,1)S(1)}, u32[]{:S(2)}, u32[]{:S(2)}) collective-permute-start(bf16[8,1152]{1,0:T(8,128)(2,1)S(1)} %get-tuple-element.41), channel_id=1, source_target_pairs={{0,20},{4,16},{8,28},{12,24},{16,4},{20,0},{24,12},{28,8},{1,21},{... | collective-permute-start | bytes 55304 | tf_op jit(solution)/shard_map/ppermute | solution.py:322
